TPU v7x, 32 devices: a whole 2x2x4 slice. The times are simulated.
32 devices in a mesh: box: 4 (over y, x), samp: 8 (over z, core).
Axes of the slice: x: 2, y: 2, z: 4, core: 2. Of those that a mesh axis runs over, the one named last changes fastest.
Arguments:
- density: bfloat16 [512, 2, 128], P(('box', 'samp')), may hold values from -6 to 6
- radiate: bfloat16 [512, 128, 1024], P(('box', 'samp')), may hold values from -0.5 to 0.5
- receive: bfloat16 [512, 128, 1024], P(('box', 'samp')), may hold values from -0.1875 to 0.1875
- near_tiles: bfloat16 [7168, 2, 128, 128], P(('box', 'samp')), may hold values from -0.109375 to 0.109375
- near_src: int32 [512, 27], P(('box', 'samp')), may hold values from 0 to 512, as said below
- near_tile: int32 [512, 27], P(('box', 'samp')), may hold values from 0 to 7168, as said below
- send_box: int32 [32, 32, 4], P(('box', 'samp')), may hold values from 0 to 16, as said below
- distant_pattern_slot: int32 [512, 189], P(('box', 'samp')), may hold values from 0 to 128, as said below
- far_type: int32 [512, 189], P(('box', 'samp')), may hold values from 0 to 315
- trans_lo: bfloat16 [316, 2, 512], replicated, may hold values from -0.4375 to 0.4375
- interp_matrix: bfloat16 [512, 2048], replicated, may hold values from -0.25 to 0.25
- shifts: float32 [8, 2, 2048], replicated, may hold values from -2 to 2
- par_far: int32 [64, 189], P('box'), may hold values from 0 to 64, as said below
- par_type: int32 [64, 189], P('box'), may hold values from 0 to 315
- trans_hi: bfloat16 [316, 2, 2048], replicated, may hold values from -0.4375 to 0.4375
Outputs:
- field: float32 [512, 2, 128], P(('box', 'samp'))
Inputs may be any that keep to these rules, and one draw needn't show every extreme that they name: `send_box`: entries equal to 16 are empty and come last in a slot row. A sender fills slots for a receiver only if it lies within 8 device numbers of it, or is 16, 8 or 4 device numbers away cyclically; for every other pair all slots are empty. One device sends 4 patterns to another in every draw, and some device receives 4 from every device that fills slots for it. `distant_pattern_slot`: the value 32 * 4 marks an empty entry; empty entries come last in a row; every other entry names a non-empty slot that its sender fills for the box's device; at least 94 entries of a row are non-empty. `near_src`: the value 512 marks an empty entry; empty entries come last in a row; a source box lies on the box's own device or on the device of index one lower or one higher. `near_tile`: empty where near_src is; every other entry names a tile of the box's own device, and the non-empty entries of one device's boxes name each of its 224 tiles once. `par_far`: the value 64 marks an empty entry; empty entries come last in a row; at least 94 entries of a row are non-empty.
All inputs are finite; a program needn't handle non-finite values.
Results may differ from a plain program's by a relative error of at most 0.0065.
Values may be sent and summed in bfloat16 or wider, within the bound.
No kernel may reach another device: no remote copies, remote signals or barrier semaphores. Data moves between devices by JAX's collectives and lax.ppermute only.
A program may use at most 128 MiB of HBM per device.

v0:
```python
import jax
import jax.numpy as jnp
from jax import lax
from jax.sharding import PartitionSpec as P


def shifted(value, axis, steps):
    count = lax.axis_size(axis)
    first, last = (max(0, -steps), min(count, count - steps))
    return lax.ppermute(value, axis, [(source, source + steps) for source in range(first, last)])


def radiated(density, radiate):
    half_width = radiate.shape[-1] // 2
    matvec_result = jnp.einsum("lmq,lqj->lmj", density, radiate, preferred_element_type=jnp.float32)
    real_part = matvec_result[:, 0, :half_width] - matvec_result[:, 1, half_width:]
    imag_part = matvec_result[:, 0, half_width:] + matvec_result[:, 1, :half_width]
    return jnp.stack([real_part, imag_part], 1)


def pick_rows(table, index):
    selector = (index[..., None] == jnp.arange(table.shape[0], dtype=jnp.int32)).astype(table.dtype)
    return jnp.einsum("...r,rw->...w", selector, table, preferred_element_type=jnp.float32)


def translated_flat(pattern_rows, operator_rows, width):
    real_part = jnp.sum(
        operator_rows[..., :width] * pattern_rows[..., :width]
        - operator_rows[..., width:] * pattern_rows[..., width:],
        -2,
    )
    imag_part = jnp.sum(
        operator_rows[..., :width] * pattern_rows[..., width:]
        + operator_rows[..., width:] * pattern_rows[..., :width],
        -2,
    )
    return jnp.stack([real_part, imag_part], -2)


def shifted_sum(interpolated, shifts):
    width = interpolated.shape[-1]
    grouped = interpolated.reshape(-1, 8, 2, width)
    real_part = jnp.sum(grouped[:, :, 0] * shifts[:, 0] - grouped[:, :, 1] * shifts[:, 1], 1)
    imag_part = jnp.sum(grouped[:, :, 0] * shifts[:, 1] + grouped[:, :, 1] * shifts[:, 0], 1)
    return jnp.stack([real_part, imag_part], 1)


def spread_down(incoming_hi, shifts):
    parent = incoming_hi[:, None]
    real_part = shifts[None, :, 0] * parent[:, :, 0] + shifts[None, :, 1] * parent[:, :, 1]
    imag_part = shifts[None, :, 0] * parent[:, :, 1] - shifts[None, :, 1] * parent[:, :, 0]
    stacked = jnp.stack([real_part, imag_part], 2)
    return stacked.reshape(-1, 2, incoming_hi.shape[-1]).astype(jnp.bfloat16)


def received_field(receive, incoming):
    real_in = incoming[:, 0]
    imag_in = incoming[:, 1]
    blending_operator = jnp.stack(
        [jnp.concatenate([real_in, -imag_in], -1), jnp.concatenate([imag_in, real_in], -1)], 1
    )
    return jnp.einsum(
        "mws,mis->miw", receive, blending_operator, preferred_element_type=jnp.float32
    )


def on_device(
    density,
    radiate,
    receive,
    near_tiles,
    near_src,
    near_tile,
    send_box,
    distant_pattern_slot,
    far_type,
    trans_lo,
    interp_matrix,
    shifts,
    par_far,
    par_type,
    trans_hi,
):
    box_count = density.shape[0]
    panel_count = density.shape[2]
    box_groups = lax.axis_size("box")
    samp_count = lax.axis_size("samp")
    devices = box_groups * samp_count
    position = lax.axis_index("box") * samp_count + lax.axis_index("samp")
    slot_count = send_box.shape[2]
    type_count = trans_lo.shape[0]
    pattern_lo = radiated(density, radiate).astype(jnp.bfloat16)
    width_lo = pattern_lo.shape[-1]
    flat_lo = jnp.concatenate(
        [pattern_lo.reshape(box_count, 2 * width_lo), jnp.zeros((1, 2 * width_lo), jnp.bfloat16)], 0
    )
    outgoing = pick_rows(flat_lo, send_box[0]).astype(jnp.bfloat16)
    arrived = lax.all_to_all(outgoing, ("box", "samp"), split_axis=0, concat_axis=0, tiled=True)
    lower_density = shifted(density, ("box", "samp"), 1)
    upper_density = shifted(density, ("box", "samp"), -1)
    level_window = jnp.concatenate(
        [lower_density, density, upper_density, jnp.zeros((1, 2, panel_count), jnp.bfloat16)], 0
    )
    overall_box_count = box_count * devices
    near_live = near_src < overall_box_count
    local_source = jnp.where(near_live, near_src - (position - 1) * box_count, 3 * box_count)
    tile_total = near_tiles.shape[0]
    local_tile = jnp.where(near_live, near_tile - position * tile_total, tile_total)
    owners = jnp.broadcast_to(jnp.arange(box_count, dtype=jnp.int32)[:, None], near_src.shape)
    tile_owner = (
        jnp.full((tile_total,), box_count, jnp.int32)
        .at[local_tile.reshape(-1)]
        .set(owners.reshape(-1), mode="drop")
    )
    tile_source = (
        jnp.full((tile_total,), 3 * box_count, jnp.int32)
        .at[local_tile.reshape(-1)]
        .set(local_source.reshape(-1), mode="drop")
    )
    source_values = level_window[tile_source]
    matvec_result = jnp.einsum(
        "taij,tbj->tabi", near_tiles, source_values, preferred_element_type=jnp.float32
    )
    contrib = jnp.stack(
        [
            matvec_result[:, 0, 0] - matvec_result[:, 1, 1],
            matvec_result[:, 0, 1] + matvec_result[:, 1, 0],
        ],
        1,
    )
    onehot = (tile_owner[:, None] == jnp.arange(box_count, dtype=jnp.int32)[None, :]).astype(
        jnp.float32
    )
    close_range_field = jnp.einsum("tb,tcp->bcp", onehot, contrib, precision=lax.Precision.HIGHEST)
    received = jnp.concatenate(
        [
            arrived.reshape(devices * slot_count, 2 * width_lo),
            jnp.zeros((1, 2 * width_lo), jnp.bfloat16),
        ],
        0,
    )
    far_rows = pick_rows(received, distant_pattern_slot)
    operator_rows = pick_rows(trans_lo.reshape(type_count, 2 * width_lo), far_type)
    incoming_lo = translated_flat(far_rows, operator_rows, width_lo)
    interpolated = jnp.einsum(
        "gcq,qh->gch", pattern_lo, interp_matrix, preferred_element_type=jnp.float32
    )
    parents_own = shifted_sum(interpolated, shifts).astype(jnp.bfloat16)
    per_device = parents_own.shape[0]
    everyone = lax.all_gather(parents_own, ("box", "samp"), axis=0, tiled=True)
    width_hi = everyone.shape[-1]
    start_row = lax.axis_index("samp") * per_device
    own_far = lax.dynamic_slice_in_dim(par_far, start_row, per_device, 0)
    own_type = lax.dynamic_slice_in_dim(par_type, start_row, per_device, 0)
    padded_hi = jnp.concatenate([everyone, jnp.zeros((1, 2, width_hi), jnp.bfloat16)], 0)
    parent_rows = pick_rows(padded_hi.reshape(-1, 2 * width_hi), own_far)
    parent_ops = pick_rows(trans_hi.reshape(type_count, 2 * width_hi), own_type)
    incoming_hi = translated_flat(parent_rows, parent_ops, width_hi)
    down = spread_down(incoming_hi, shifts)
    from_parent = jnp.einsum("gch,qh->gcq", down, interp_matrix, preferred_element_type=jnp.float32)
    incoming = (incoming_lo + from_parent).astype(jnp.bfloat16)
    far_field = received_field(receive, incoming)
    return 0.5 * density.astype(jnp.float32) + close_range_field + far_field


def solution(mesh):
    return jax.shard_map(
        on_device,
        mesh=mesh,
        in_specs=(
            P(("box", "samp"), None, None),
            P(("box", "samp"), None, None),
            P(("box", "samp"), None, None),
            P(("box", "samp"), None, None, None),
            P(("box", "samp"), None),
            P(("box", "samp"), None),
            P(("box", "samp"), None, None),
            P(("box", "samp"), None),
            P(("box", "samp"), None),
            P(),
            P(),
            P(),
            P("box", None),
            P("box", None),
            P(),
        ),
        out_specs=P(("box", "samp"), None, None),
        check_vma=False,
    )
```

profile of v0, /device:TPU:0, one launch (start us, length us, event | category | flops | bytes accessed | tf_op | source)
XLA Modules:
  0.0 117.4 jit_solution(892937640941617647)
XLA Ops:
  0.0 1.4 %collective-permute-start.1 = (bf16[16,2,128]{2,1,0:T(2,128)(2,1)}, bf16[16,2,128]{2,1,0:T(2,128)(2,1)S(1)}, u32[]{:S(2)}, u32[]{:S(2)}) collective-permute-start(bf16[16,2,128]{2,1,0:T(2,128)(2,1)} %param.15), channel_id=1, source_target_pairs={{1,0},{2,1},{3,2},{4,3},{5,4},{6,5},{7,6},{8,7},{9,8},{10,9},{11,1... | collective-permute-start | bytes 24584 | tf_op jit(solution)/shard_map/ppermute | solution.py:10
  1.5 3.0 %collective-permute-start = (bf16[16,2,128]{2,1,0:T(2,128)(2,1)}, bf16[16,2,128]{2,1,0:T(2,128)(2,1)S(1)}, u32[]{:S(2)}, u32[]{:S(2)}) collective-permute-start(bf16[16,2,128]{2,1,0:T(2,128)(2,1)} %param.15), channel_id=1, source_target_pairs={{0,1},{1,2},{2,3},{3,4},{4,5},{5,6},{6,7},{7,8},{8,9},{9,10},{10,1... | collective-permute-start | bytes 24584 | tf_op jit(solution)/shard_map/ppermute | solution.py:10
  4.5 2.9 %fusion.49 = f32[16,2,1024]{2,1,0:T(2,128)S(1)} fusion(bf16[16,2,128]{2,1,0:T(2,128)(2,1)} %param.15, bf16[16,128,1024]{2,1,0:T(8,128)(2,1)} %param.16), kind=kOutput, calls=%fused_computation.94 | convolution fusion | flops 8388608 | bytes 4333568 | tf_op jit(solution)/shard_map/lmq,lqj->lmj/dot_general | solution.py:15
  7.8 0.9 copy.37
  8.8 10.8 %all-to-all-start = ((bf16[32,4,1024]{2,1,0:T(4,128)(2,1)}), bf16[32,4,1024]{2,1,0:T(4,128)(2,1)}, u32[]{:S(2)}, u32[]{:S(2)}) async-start(bf16[32,4,1024]{2,1,0:T(4,128)(2,1)} %copy.37), calls=%async_computation | async-start | bytes 524288 | tf_op jit(solution)/shard_map/all_to_all | solution.py:98
  19.8 2.9 %scatter_custom_fusion.1 = s32[224]{0:T(256)S(1)} fusion(s32[432]{0:T(512)S(1)} %bitcast.104, s32[432]{0:T(512)S(1)} %reshape.231, s32[]{:T(128)} %constant.5.clone.1), kind=kCustom, calls=%fused_computation.81 | custom fusion | bytes 900 | tf_op jit(solution)/shard_map/scatter | solution.py:118
  22.8 0.5 convolution_bitcast_fusion
  23.5 44.1 %all_gather.3 = bf16[64,2,2048]{2,1,0:T(2,128)(2,1)S(1)} all-gather(bf16[2,2,2048]{2,1,0:T(2,128)(2,1)S(1)} %copy.41), channel_id=1, replica_groups=mesh['box'=4,'samp'=8] {'box','samp'}, dimensions={0}, use_global_device_ids=true | all-gather | bytes 540672 | tf_op jit(solution)/shard_map/all_gather | solution.py:150
  68.3 2.3 %reshape.238 = bf16[316,1024,1]{1,0,2:T(8,128)(2,1)S(1)} reshape(bf16[316,2,512]{2,1,0:T(2,128)(2,1)} %param.24) | data formatting | bytes 1294336 | tf_op jit(solution)/shard_map/reshape | solution.py:143
  70.6 7.2 %reshape.241 = bf16[316,4096,1]{1,0,2:T(8,128)(2,1)} reshape(bf16[316,2,2048]{2,1,0:T(2,128)(2,1)} %param.29) | data formatting | bytes 5177344 | tf_op jit(solution)/shard_map/reshape | solution.py:157
  77.8 0.7 constant_dynamic-slice_fusion
  78.5 3.6 %fusion.14 = f32[2,189,4096]{2,1,0:T(8,128)S(1)} fusion(bf16[316,4096,1]{1,0,2:T(8,128)(2,1)} %reshape.241, s32[2,189]{1,0:T(2,128)S(1)} %get-tuple-element.31), kind=kOutput, calls=%fused_computation.24 | convolution fusion | flops 978637440 | bytes 8783336 | tf_op jit(solution)/shard_map/...r,rw->...w/dot_general | solution.py:23
  82.1 1.0 fusion.21
  83.1 1.6 %subtract_reduce_fusion.1 = (f32[2,2048]{1,0:T(2,128)S(1)}, f32[2,2048]{1,0:T(2,128)S(1)}) fusion(f32[2,189,4096]{2,1,0:T(8,128)S(1)} %fusion.21, f32[2,189,4096]{2,1,0:T(8,128)S(1)} %fusion.14), kind=kLoop, calls=%fused_computation.8 | loop fusion | flops 6184960 | bytes 12419072 | tf_op jit(solution)/shard_map/reduce_sum | solution.py:27
  84.8 6.5 %fusion = f32[16,189,1024]{2,1,0:T(8,128)} fusion(bf16[316,1024,1]{1,0,2:T(8,128)(2,1)S(1)} %reshape.238, s32[16,189]{1,0:T(8,128)S(1)} %copy-done.4), kind=kOutput, calls=%fused_computation.6 | convolution fusion | flops 1957991680 | bytes 13045568 | tf_op jit(solution)/shard_map/...r,rw->...w/dot_general | solution.py:23
  91.4 3.1 %scatter_custom_fusion = s32[224]{0:T(256)S(1)} fusion(s32[432]{0:T(512)S(1)} %bitcast.105, s32[432]{0:T(512)S(1)} %reshape.223, s32[]{:T(128)} %constant.15.clone.1), kind=kCustom, calls=%fused_computation.85 | custom fusion | bytes 900 | tf_op jit(solution)/shard_map/scatter | solution.py:113
  94.7 0.9 gather_fusion
  95.6 9.0 %convolution_bitcast_fusion.1 = f32[224,2,2,128]{3,2,1,0:T(2,128)S(1)} fusion(bf16[224,2,128,128]{3,2,1,0:T(8,128)(2,1)} %param.18, bf16[224,2,128]{2,1,0:T(2,128)(2,1)S(1)} %gather_fusion), kind=kOutput, calls=%fused_computation.16 | convolution fusion | flops 29360128 | bytes 15253504 | tf_op jit(solution)/shard_map/taij,tbj->tabi/dot_general | solution.py:121
  105.0 1.0 reshape.207
  106.1 2.1 %fusion.2 = f32[16,189,1024]{2,1,0:T(8,128)S(1)} fusion(s32[16,189]{1,0:T(8,128)S(1)} %copy-done.5, bf16[128,1024]{1,0:T(8,128)(2,1)S(1)} %reshape.207), kind=kOutput, calls=%fused_computation.12 | convolution fusion | flops 799306688 | bytes 12660544 | tf_op jit(solution)/shard_map/...r,rw->...w/dot_general | solution.py:23
  108.1 6.5 %subtract_reduce_fusion = (f32[16,512]{1,0:T(8,128)S(1)}, f32[16,512]{1,0:T(8,128)S(1)}) fusion(f32[16,189,1024]{2,1,0:T(8,128)S(1)} %fusion.2, f32[16,189,1024]{2,1,0:T(8,128)} %fusion), kind=kLoop, calls=%fused_computation.4 | loop fusion | flops 12369920 | bytes 24838144 | tf_op jit(solution)/shard_map/reduce_sum | solution.py:27
  114.6 0.7 fusion.9
  115.4 1.2 %fusion.29 = f32[16,2,128]{2,1,0:T(2,128)S(1)} fusion(bf16[16,128,1024]{2,1,0:T(8,128)(2,1)S(1)} %copy-done.1, bf16[16,2,1024]{2,0,1:T(8,128)(2,1)S(1)} %pad_maximum_fusion), kind=kOutput, calls=%fused_computation.52 | convolution fusion | flops 8388608 | bytes 4276224 | tf_op jit(solution)/shard_map/mws,mis->miw/dot_general | solution.py:62
  116.8 0.6 copy.44
  (52 shorter events, 2.6 us)
Async XLA Ops:
  0.0 22.8 %copy-start = (bf16[512,2048]{1,0:T(8,128)(2,1)S(1)}, bf16[512,2048]{1,0:T(8,128)(2,1)}, u32[]{:S(2)}) copy-start(bf16[512,2048]{1,0:T(8,128)(2,1)} %param.25) | copy-start | bytes 6291460
  0.0 7.5 %copy-start.8 = (s32[1,32,4]{1,2,0:T(4,128)S(1)}, s32[1,32,4]{1,2,0:T(4,128)}, u32[]{:S(2)}) copy-start(s32[1,32,4]{1,2,0:T(4,128)} %param.21) | copy-start | bytes 1540
  0.0 19.5 %copy-start.7 = (s32[16,27]{1,0:T(8,128)S(1)}, s32[16,27]{1,0:T(8,128)}, u32[]{:S(2)}) copy-start(s32[16,27]{1,0:T(8,128)} %param.20) | copy-start | bytes 5188
  0.0 19.5 %copy-start.6 = (s32[16,27]{1,0:T(8,128)S(1)}, s32[16,27]{1,0:T(8,128)}, u32[]{:S(2)}) copy-start(s32[16,27]{1,0:T(8,128)} %param.19) | copy-start | bytes 5188
  0.0 22.7 %copy-start.2 = (f32[8,2,2048]{2,1,0:T(2,128)S(1)}, f32[8,2,2048]{2,1,0:T(2,128)}, u32[]{:S(2)}) copy-start(f32[8,2,2048]{2,1,0:T(2,128)} %param.26) | copy-start | bytes 393220
  0.0 94.6 %collective-permute-start.1 = (bf16[16,2,128]{2,1,0:T(2,128)(2,1)}, bf16[16,2,128]{2,1,0:T(2,128)(2,1)S(1)}, u32[]{:S(2)}, u32[]{:S(2)}) collective-permute-start(bf16[16,2,128]{2,1,0:T(2,128)(2,1)} %param.15), channel_id=1, source_target_pairs={{1,0},{2,1},{3,2},{4,3},{5,4},{6,5},{7,6},{8,7},{9,8},{10,9},{11,1... | collective-permute-start | bytes 24584 | tf_op jit(solution)/shard_map/ppermute | solution.py:10
  1.5 93.2 %collective-permute-start = (bf16[16,2,128]{2,1,0:T(2,128)(2,1)}, bf16[16,2,128]{2,1,0:T(2,128)(2,1)S(1)}, u32[]{:S(2)}, u32[]{:S(2)}) collective-permute-start(bf16[16,2,128]{2,1,0:T(2,128)(2,1)} %param.15), channel_id=1, source_target_pairs={{0,1},{1,2},{2,3},{3,4},{4,5},{5,6},{6,7},{7,8},{8,9},{9,10},{10,1... | collective-permute-start | bytes 24584 | tf_op jit(solution)/shard_map/ppermute | solution.py:10
  8.8 96.3 %all-to-all-start = ((bf16[32,4,1024]{2,1,0:T(4,128)(2,1)}), bf16[32,4,1024]{2,1,0:T(4,128)(2,1)}, u32[]{:S(2)}, u32[]{:S(2)}) async-start(bf16[32,4,1024]{2,1,0:T(4,128)(2,1)} %copy.37), calls=%async_computation | async-start | bytes 524288 | tf_op jit(solution)/shard_map/all_to_all | solution.py:98
  83.1 1.7 %copy-start.4 = (s32[16,189]{1,0:T(8,128)S(1)}, s32[16,189]{1,0:T(8,128)}, u32[]{:S(2)}) copy-start(s32[16,189]{1,0:T(8,128)} %param.23) | copy-start | bytes 36292
  84.8 9.8 %copy-start.3 = (bf16[16,2,128]{2,1,0:T(2,128)(2,1)S(1)}, bf16[16,2,128]{2,1,0:T(2,128)(2,1)}, u32[]{:S(2)}) copy-start(bf16[16,2,128]{2,1,0:T(2,128)(2,1)} %param.15) | copy-start | bytes 24580
  95.6 10.4 %copy-start.5 = (s32[16,189]{1,0:T(8,128)S(1)}, s32[16,189]{1,0:T(8,128)}, u32[]{:S(2)}) copy-start(s32[16,189]{1,0:T(8,128)} %param.22) | copy-start | bytes 36292
  108.1 7.3 %copy-start.1 = (bf16[16,128,1024]{2,1,0:T(8,128)(2,1)S(1)}, bf16[16,128,1024]{2,1,0:T(8,128)(2,1)}, u32[]{:S(2)}) copy-start(bf16[16,128,1024]{2,1,0:T(8,128)(2,1)} %param.17) | copy-start | bytes 12582916
where the time goes:
time: 118 us; the launch traced here: 117 us
  blocking collectives  44.1 us (37%)
  matrix products  27.9 us (24%)
  local copies, waits for them, and re-layouts  20.9 us (18%)
  starting transfers between devices  15.2 us (13%)
  other arithmetic  8.92 us (8%)
    all_gather x1, blocking collectives, on_device(): everyone = lax.all_gather(parents_own, ('box', 'samp'), axis=0, tiled=True)  44.1 us
    dot_general x5, matrix products, pick_rows(): jnp.einsum('...r,rw->...w', selector, table, preferred_element_type=jnp.f...  13.4 us
    all_to_all x1, starting transfers between devices, on_device(): lax.all_to_all(outgoing, ('box', 'samp'), split_axis=0, concat_axis=0, ti...  10.8 us
    dot_general x1, matrix products, on_device(): jnp.einsum('taij,tbj->tabi', near_tiles, source_values, preferred_element...  9.05 us
    reduce_sum x2, other arithmetic, translated_flat(): jnp.sum(operator_rows[..., :width] * pattern_rows[..., :width] - operator...  8.09 us
    reshape x1, local copies, waits for them, and re-layouts, on_device(): parent_ops = pick_rows(trans_hi.reshape(type_count, 2 * width_hi), own_type)  7.16 us
    ppermute x2, starting transfers between devices, shifted(): lax.ppermute(value, axis, [(source, source + steps) for source in range(f...  4.46 us
    scatter x1, local copies, waits for them, and re-layouts, on_device(): tile_owner = jnp.full((tile_total,), box_count, jnp.int32).at[local_tile....  3.13 us
  transfers between devices with their start and end apart: 3, of which 0 were waited for; matrix products, arithmetic and copies ran while one was open for 39% of the time, Pallas kernels for 0%

commit v1 on v0

v1 whole, which is shorter than its diff:
```python
import functools

import jax
import jax.numpy as jnp
from jax import lax
from jax.experimental import pallas as pl
from jax.experimental.pallas import tpu as pltpu
from jax.sharding import PartitionSpec as P

F32 = jnp.float32
BF16 = jnp.bfloat16
LANE = 128
VMEM_SPEC = pl.BlockSpec(memory_space=pltpu.VMEM)
SMEM_SPEC = pl.BlockSpec(memory_space=pltpu.SMEM)
ANY_SPEC = pl.BlockSpec(memory_space=pl.ANY)
MIB = 1 << 20


def iota(shape, dim):
    return lax.broadcasted_iota(jnp.int32, shape, dim)


def dot_nn(lhs, rhs):
    return lax.dot_general(lhs, rhs, (((1,), (0,)), ((), ())), preferred_element_type=F32)


def dot_nt(lhs, rhs):
    return lax.dot_general(lhs, rhs, (((1,), (1,)), ((), ())), preferred_element_type=F32)


def shifted(value, axis, steps):
    count = lax.axis_size(axis)
    first, last = (max(0, -steps), min(count, count - steps))
    return lax.ppermute(value, axis, [(source, source + steps) for source in range(first, last)])


def radiate_kernel(
    dens_ref, radiate_ref, send_ref, interp_ref, shift_ref, out_ref, rad, summed, table, parent, sems
):
    boxes = rad.shape[0]
    width = rad.shape[2] // 2
    per_step = 4
    steps = boxes // per_step
    copies = []
    for step in range(steps):
        part = pl.ds(step * per_step, per_step)
        copies.append(pltpu.make_async_copy(radiate_ref.at[part], rad.at[part], sems.at[step]))
        copies[-1].start()
    dens = dens_ref[...].astype(F32)
    owner = (iota(dens.shape, 0) // 2) % per_step
    blocks = jnp.concatenate([jnp.where(owner == b, dens, 0.0) for b in range(per_step)], 1)
    for step in range(steps):
        copies[step].wait()
        rows = slice(step * 2 * per_step, (step + 1) * 2 * per_step)
        weights = rad[step * per_step : (step + 1) * per_step].reshape(per_step * LANE, 2 * width)
        summed[rows] = dot_nn(blocks[rows].astype(BF16), weights).reshape(
            2 * per_step, 2 * width // LANE, LANE
        )
    chunks = width // LANE
    re_chunks, im_chunks = [], []
    for r in range(chunks):
        first_lo = summed[pl.ds(0, boxes, stride=2), r, :]
        first_hi = summed[pl.ds(0, boxes, stride=2), chunks + r, :]
        second_lo = summed[pl.ds(1, boxes, stride=2), r, :]
        second_hi = summed[pl.ds(1, boxes, stride=2), chunks + r, :]
        re_chunks.append((first_lo - second_hi).astype(BF16))
        im_chunks.append((first_hi + second_lo).astype(BF16))
    re_part = jnp.concatenate(re_chunks, 1)
    im_part = jnp.concatenate(im_chunks, 1)
    for r in range(chunks):
        table[pl.ds(r, boxes, stride=8), :] = re_chunks[r].astype(F32)
        table[pl.ds(chunks + r, boxes, stride=8), :] = im_chunks[r].astype(F32)
    table[pl.ds(boxes * 8, 8), :] = jnp.zeros((8, LANE), F32)
    wide = dot_nn(jnp.concatenate([re_part, im_part], 0), interp_ref[...])
    hi_chunks = wide.shape[1] // LANE
    parents = boxes // 8
    for r in range(hi_chunks):
        cols = slice(r * LANE, (r + 1) * LANE)
        s_re = shift_ref[pl.ds(2 * r, 8, stride=2 * hi_chunks), :]
        s_im = shift_ref[pl.ds(2 * r + 1, 8, stride=2 * hi_chunks), :]
        for p in range(parents):
            w_re = wide[p * 8 : (p + 1) * 8, cols]
            w_im = wide[boxes + p * 8 : boxes + (p + 1) * 8, cols]
            row = p * 2 * hi_chunks + r
            parent[row : row + 1] = jnp.sum(w_re * s_re - w_im * s_im, 0, keepdims=True)
            row += hi_chunks
            parent[row : row + 1] = jnp.sum(w_re * s_im + w_im * s_re, 0, keepdims=True)
    slots, devices = send_ref.shape
    hi_rows = parents * 2 * hi_chunks
    parent_block = parent[...].astype(BF16)

    def fill(d, carry):
        for k in range(slots // 2):
            pair = [
                table[pl.ds(pl.multiple_of(send_ref[2 * k + h, d] * 8, 8), 8), :] for h in range(2)
            ]
            out_ref[d, 16 * k : 16 * (k + 1)] = jnp.concatenate(pair, 0).astype(BF16)
        out_ref[d, 8 * slots : 8 * slots + hi_rows] = parent_block
        return carry

    lax.fori_loop(0, devices, fill, 0)


def middle_kernel(
    types,
    box_total,
    lower_ref,
    dens_ref,
    upper_ref,
    near_src_ref,
    near_tile_ref,
    tiles_ref,
    slot_ref,
    type_ref,
    op_lo_ref,
    par_far_ref,
    par_type_ref,
    op_hi_ref,
    near_ref,
    d_lo_ref,
    d_hi_ref,
    tiles,
    dens3,
    acc,
    window,
    code,
    index,
    wide_op,
    wide_hi,
    op_lo,
    sems,
):
    boxes, near = near_src_ref.shape
    tile_count = tiles.shape[0]
    per_box = tile_count // boxes
    copies = []
    for step in range(boxes):
        part = pl.ds(step * per_box, per_box)
        copies.append(pltpu.make_async_copy(tiles_ref.at[part], tiles.at[part], sems.at[step]))
        copies[-1].start()
    position = lax.axis_index("box") * lax.axis_size("samp") + lax.axis_index("samp")

    def locate(g, carry):
        for n in range(near):
            source = near_src_ref[g, n]
            live = source < box_total
            tile = jnp.where(live, near_tile_ref[g, n] - position * tile_count, tile_count)
            code[tile] = g * 64 + source - (position - 1) * boxes
        return carry

    lax.fori_loop(0, boxes, locate, 0)

    for k, ref in enumerate((lower_ref, dens_ref, upper_ref)):
        dens3[pl.ds(2 * boxes * k, 2 * boxes), :] = ref[...].astype(F32)
    first = dens3[pl.ds(0, 3 * boxes, stride=2), :]
    second = dens3[pl.ds(1, 3 * boxes, stride=2), :]
    window[...] = jnp.concatenate(
        [
            jnp.concatenate([first, -second], 1),
            jnp.concatenate([second, first], 1),
            jnp.zeros((LANE - 6 * boxes, 2 * LANE), F32),
        ],
        0,
    ).astype(BF16)
    acc[...] = jnp.zeros(acc.shape, F32)

    faces = index.shape[1]
    index[...] = jnp.full(index.shape, -1, jnp.int32)
    far = slot_ref.shape[1]
    rows = slot_ref.shape[0]
    parents = boxes // 8
    index[0:rows, 0:far] = slot_ref[...]
    index[rows : 2 * rows, 0:far] = type_ref[...]
    prow = par_far_ref.shape[0]
    index[2 * rows : 2 * rows + prow, 0:far] = par_far_ref[...]
    index[2 * rows + prow : 2 * rows + 2 * prow, 0:far] = par_type_ref[...]

    type_pad = op_lo.shape[0]
    chunks = op_lo.shape[1] // (2 * LANE)
    wide_op[0 : types * 2 * chunks] = op_lo_ref[...].astype(F32)
    wide_op[types * 2 * chunks : type_pad * 2 * chunks] = jnp.zeros(
        ((type_pad - types) * 2 * chunks, LANE), F32
    )
    for c in range(2):
        for r in range(chunks):
            col = (c * chunks + r) * LANE
            op_lo[:, col : col + LANE] = wide_op[
                pl.ds(2 * r + c, type_pad, stride=2 * chunks), :
            ].astype(BF16)

    def counts(source_row, type_row, sources):
        source = index[pl.ds(source_row, 1), :]
        kind = index[pl.ds(type_row, 1), :]
        by_source = jnp.where(iota((sources, faces), 0) == source, 1.0, 0.0).astype(BF16)
        by_type = jnp.where(iota((type_pad, faces), 0) == kind, 1.0, 0.0).astype(BF16)
        return dot_nt(by_source, by_type).astype(BF16)

    lane = iota((8, LANE), 1)
    lane = jnp.where(lane < 3 * boxes, lane, jnp.where(lane < 6 * boxes, lane - 3 * boxes, -1))
    slot_total = d_lo_ref.shape[1]

    def step_box(g, carry):
        part = pl.ds(g * per_box, per_box)
        d_lo_ref[g] = dot_nn(counts(g, rows + g, slot_total), op_lo[...]).astype(d_lo_ref.dtype)
        pltpu.make_async_copy(tiles_ref.at[part], tiles.at[part], sems.at[g]).wait()
        both = tiles[part]
        lhs = jnp.concatenate(
            [both[:, 0].reshape(per_box * LANE, LANE), both[:, 1].reshape(per_box * LANE, LANE)], 1
        )
        product = dot_nt(lhs, window[...]).reshape(per_box, LANE // 8, 8, LANE)
        for j in range(per_box):
            entry = code[g * per_box + j]
            chosen = lane == (entry & 63)
            owner = entry >> 6
            acc[owner] = acc[owner] + jnp.where(chosen[None], product[j], 0.0)
        return carry

    lax.fori_loop(0, boxes, step_box, 0)

    start = 2 * rows + lax.axis_index("samp") * parents
    sources = d_hi_ref.shape[0] // parents
    count_hi = jnp.concatenate(
        [counts(start + p, start + prow + p, sources) for p in range(parents)], 0
    )
    hi_chunks = op_hi_ref.shape[0] // (2 * types)
    group = 4 * 2 * hi_chunks

    def widen(i, carry):
        part = pl.ds(pl.multiple_of(i * group, group), group)
        wide_hi[part] = op_hi_ref[part].astype(F32)
        return carry

    lax.fori_loop(0, types // 4, widen, 0, unroll=2)
    wide_hi[types * 2 * hi_chunks : type_pad * 2 * hi_chunks] = jnp.zeros(
        ((type_pad - types) * 2 * hi_chunks, LANE), F32
    )
    for c in range(2):
        for r in range(0, hi_chunks, 2):
            rhs = jnp.concatenate(
                [
                    wide_hi[pl.ds(2 * (r + q) + c, type_pad, stride=2 * hi_chunks), :].astype(BF16)
                    for q in range(2)
                ],
                1,
            )
            col = (c * hi_chunks + r) * LANE
            d_hi_ref[:, col : col + 2 * LANE] = dot_nn(count_hi, rhs).astype(d_hi_ref.dtype)

    for g in range(boxes):
        flipped = acc[g].reshape(LANE, LANE).T
        row = 2 * g
        near_ref[row : row + 1] = (
            jnp.sum(flipped[0 : 3 * boxes], 0, keepdims=True)
            + 0.5 * dens3[pl.ds(2 * boxes + row, 1), :]
        )
        near_ref[row + 1 : row + 2] = (
            jnp.sum(flipped[3 * boxes : 6 * boxes], 0, keepdims=True)
            + 0.5 * dens3[pl.ds(2 * boxes + row + 1, 1), :]
        )


def last_kernel(
    arrived_ref,
    d_lo_ref,
    d_hi_ref,
    shift_ref,
    interp_ref,
    receive_ref,
    near_ref,
    out_ref,
    receive,
    slots,
    parents,
    down,
    incoming,
    blend,
    sems,
):
    boxes = receive.shape[0]
    per_step = 4
    steps = boxes // per_step
    copies = []
    for step in range(steps):
        part = pl.ds(step * per_step, per_step)
        copies.append(pltpu.make_async_copy(receive_ref.at[part], receive.at[part], sems.at[step]))
        copies[-1].start()
    devices, lines, _ = arrived_ref.shape
    own_parents = boxes // 8
    sources = d_hi_ref.shape[0] // own_parents
    hi_chunks = d_hi_ref.shape[1] // (2 * LANE)
    slot_total = d_lo_ref.shape[1]
    chunks = d_lo_ref.shape[2] // (2 * LANE)
    lo_lines = slot_total // devices * 2 * chunks
    hi_lines = lines - lo_lines
    parents[...] = arrived_ref[:, lo_lines:, :].astype(F32).reshape(devices * hi_lines, LANE)
    slots[...] = arrived_ref[:, :lo_lines, :].astype(F32).reshape(devices * lo_lines, LANE)
    for r in range(hi_chunks):
        first = parents[pl.ds(r, sources, stride=2 * hi_chunks), :]
        second = parents[pl.ds(hi_chunks + r, sources, stride=2 * hi_chunks), :]
        s_re = shift_ref[pl.ds(2 * r, 8, stride=2 * hi_chunks), :]
        s_im = shift_ref[pl.ds(2 * r + 1, 8, stride=2 * hi_chunks), :]
        re_rows, im_rows = [], []
        for p in range(own_parents):
            rows = slice(p * sources, (p + 1) * sources)
            o_re = d_hi_ref[rows, r * LANE : (r + 1) * LANE].astype(F32)
            o_im = d_hi_ref[rows, (hi_chunks + r) * LANE : (hi_chunks + r + 1) * LANE].astype(F32)
            t_re = jnp.sum(o_re * first - o_im * second, 0, keepdims=True)
            t_im = jnp.sum(o_re * second + o_im * first, 0, keepdims=True)
            re_rows.append(s_re * t_re + s_im * t_im)
            im_rows.append(s_re * t_im - s_im * t_re)
        cols = slice(r * LANE, (r + 1) * LANE)
        down[:, cols] = jnp.concatenate(re_rows + im_rows, 0).astype(BF16)
    for r in range(chunks):
        first = slots[pl.ds(r, slot_total, stride=2 * chunks), :]
        second = slots[pl.ds(chunks + r, slot_total, stride=2 * chunks), :]
        for g in range(boxes):
            o_re = d_lo_ref[g, :, r * LANE : (r + 1) * LANE].astype(F32)
            o_im = d_lo_ref[g, :, (chunks + r) * LANE : (chunks + r + 1) * LANE].astype(F32)
            cols = slice(r * LANE, (r + 1) * LANE)
            incoming[g : g + 1, cols] = jnp.sum(o_re * first - o_im * second, 0, keepdims=True)
            incoming[boxes + g : boxes + g + 1, cols] = jnp.sum(
                o_re * second + o_im * first, 0, keepdims=True
            )
    total = incoming[...] + dot_nt(down[...], interp_ref[...])
    total = total.astype(BF16).astype(F32)
    for r in range(chunks):
        re_part = total[:boxes, r * LANE : (r + 1) * LANE]
        im_part = total[boxes:, r * LANE : (r + 1) * LANE]
        blend[pl.ds(0, boxes, stride=2), r, :] = re_part
        blend[pl.ds(1, boxes, stride=2), r, :] = im_part
        blend[pl.ds(0, boxes, stride=2), chunks + r, :] = -im_part
        blend[pl.ds(1, boxes, stride=2), chunks + r, :] = re_part
    owner = (iota((2 * per_step, LANE), 0) // 2) % per_step
    for step in range(steps):
        rows = slice(step * 2 * per_step, (step + 1) * 2 * per_step)
        lhs = jnp.concatenate([blend[rows, r, :] for r in range(2 * chunks)], 1).astype(BF16)
        copies[step].wait()
        weights = receive[step * per_step : (step + 1) * per_step]
        product = dot_nt(lhs, weights.reshape(per_step * LANE, 2 * chunks * LANE))
        total = near_ref[rows]
        for b in range(per_step):
            total = total + jnp.where(owner == b, product[:, b * LANE : (b + 1) * LANE], 0.0)
        out_ref[rows] = total


def tiled_rows(array):
    count, parts, width = array.shape
    cut = array.reshape(count, parts, width // LANE, LANE)
    return cut.transpose(0, 2, 1, 3).reshape(-1, LANE)


def on_device(
    density,
    radiate,
    receive,
    near_tiles,
    near_src,
    near_tile,
    send_box,
    distant_pattern_slot,
    far_type,
    trans_lo,
    interp_matrix,
    shifts,
    par_far,
    par_type,
    trans_hi,
):
    boxes, _, panels = density.shape
    devices = lax.axis_size("box") * lax.axis_size("samp")
    slots = send_box.shape[2]
    types, _, width_lo = trans_lo.shape
    width_hi = trans_hi.shape[2]
    parents = boxes // 8
    slot_total = devices * slots
    par_total = devices * parents
    type_pad = -(-types // 8) * 8
    lines = slots * 2 * width_lo // LANE + parents * 2 * width_hi // LANE
    held = F32 if slot_total <= 128 else BF16
    rows = density.reshape(boxes * 2, panels)
    lower = shifted(rows, ("box", "samp"), 1)
    upper = shifted(rows, ("box", "samp"), -1)
    shift_rows = tiled_rows(shifts)
    outgoing = pl.pallas_call(
        radiate_kernel,
        out_shape=jax.ShapeDtypeStruct((devices, lines, LANE), BF16),
        in_specs=[VMEM_SPEC, ANY_SPEC, SMEM_SPEC, VMEM_SPEC, VMEM_SPEC],
        out_specs=VMEM_SPEC,
        scratch_shapes=[
            pltpu.VMEM(radiate.shape, BF16),
            pltpu.VMEM((2 * boxes, 2 * width_lo // LANE, LANE), F32),
            pltpu.VMEM((boxes * 8 + 8, LANE), F32),
            pltpu.VMEM((parents * 2 * width_hi // LANE, LANE), F32),
            pltpu.SemaphoreType.DMA((boxes // 4,)),
        ],
        compiler_params=pltpu.CompilerParams(vmem_limit_bytes=12 * MIB),
        cost_estimate=pl.CostEstimate(flops=10**9, bytes_accessed=8 * MIB, transcendentals=0),
    )(rows, radiate, send_box[0].T, interp_matrix, shift_rows)
    arrived = lax.all_to_all(outgoing, ("box", "samp"), split_axis=0, concat_axis=0, tiled=True)
    tile_count = near_tiles.shape[0]
    near, d_lo, d_hi = pl.pallas_call(
        functools.partial(middle_kernel, types, boxes * devices),
        out_shape=(
            pltpu.VMEM((2 * boxes, panels), F32),
            pltpu.VMEM((boxes, slot_total, 2 * width_lo), held),
            pltpu.VMEM((parents * par_total, 2 * width_hi), held),
        ),
        in_specs=[VMEM_SPEC] * 3
        + [SMEM_SPEC] * 2
        + [ANY_SPEC]
        + [VMEM_SPEC] * 6,
        out_specs=(VMEM_SPEC,) * 3,
        scratch_shapes=[
            pltpu.VMEM(near_tiles.shape, BF16),
            pltpu.VMEM((6 * boxes, panels), F32),
            pltpu.VMEM((boxes, panels // 8, 8, LANE), F32),
            pltpu.VMEM((LANE, 2 * LANE), BF16),
            pltpu.SMEM((tile_count + 8,), jnp.int32),
            pltpu.VMEM((2 * boxes + 2 * par_far.shape[0], 2 * LANE), jnp.int32),
            pltpu.VMEM((type_pad * 2 * width_lo // LANE, LANE), F32),
            pltpu.VMEM((type_pad * 2 * width_hi // LANE, LANE), F32),
            pltpu.VMEM((type_pad, 2 * width_lo), BF16),
            pltpu.SemaphoreType.DMA((boxes,)),
        ],
        compiler_params=pltpu.CompilerParams(vmem_limit_bytes=30 * MIB),
        cost_estimate=pl.CostEstimate(flops=10**10, bytes_accessed=20 * MIB, transcendentals=0),
    )(
        lower,
        rows,
        upper,
        near_src,
        near_tile,
        near_tiles,
        distant_pattern_slot,
        far_type,
        tiled_rows(trans_lo),
        par_far,
        par_type,
        tiled_rows(trans_hi),
    )
    lo_lines = slots * 2 * width_lo // LANE
    field = pl.pallas_call(
        last_kernel,
        out_shape=jax.ShapeDtypeStruct((2 * boxes, panels), F32),
        in_specs=[VMEM_SPEC] * 5 + [ANY_SPEC] + [VMEM_SPEC],
        out_specs=VMEM_SPEC,
        scratch_shapes=[
            pltpu.VMEM(receive.shape, BF16),
            pltpu.VMEM((devices * lo_lines, LANE), F32),
            pltpu.VMEM((devices * (lines - lo_lines), LANE), F32),
            pltpu.VMEM((2 * boxes, width_hi), BF16),
            pltpu.VMEM((2 * boxes, width_lo), F32),
            pltpu.VMEM((2 * boxes, 2 * width_lo // LANE, LANE), F32),
            pltpu.SemaphoreType.DMA((boxes // 4,)),
        ],
        compiler_params=pltpu.CompilerParams(vmem_limit_bytes=20 * MIB),
        cost_estimate=pl.CostEstimate(flops=10**9, bytes_accessed=8 * MIB, transcendentals=0),
    )(arrived, d_lo, d_hi, shift_rows, interp_matrix, receive, near)
    return field.reshape(boxes, 2, panels)


def solution(mesh):
    both = ("box", "samp")
    return jax.shard_map(
        on_device,
        mesh=mesh,
        in_specs=(
            P(both, None, None),
            P(both, None, None),
            P(both, None, None),
            P(both, None, None, None),
            P(both, None),
            P(both, None),
            P(both, None, None),
            P(both, None),
            P(both, None),
            P(),
            P(),
            P(),
            P("box", None),
            P("box", None),
            P(),
        ),
        out_specs=P(both, None, None),
        check_vma=False,
    )
```

time: 118 us -> 78.2 us (0.66)
  the two profiles are of different devices: /device:TPU:0 before, /device:TPU:11 now
where the time goes in v1:
time: 78.2 us; the launch traced here: 77.7 us
  Pallas kernels  31.1 us (40%)
  local copies, waits for them, and re-layouts  20.7 us (26%)
  waiting for transfers between devices  13.8 us (18%)
  starting transfers between devices  11.9 us (15%)
    pallas_call x1, Pallas kernels, on_device(): pl.pallas_call(functools.partial(middle_kernel, types, boxes * devices),...  21.2 us
    unnamed x42, local copies, waits for them, and re-layouts  20.7 us
    ppermute x2, waiting for transfers between devices, shifted(): lax.ppermute(value, axis, [(source, source + steps) for source in range(f...  13.8 us
    all_to_all x1, starting transfers between devices, on_device(): lax.all_to_all(outgoing, ('box', 'samp'), split_axis=0, concat_axis=0, ti...  6.34 us
    pallas_call x1, Pallas kernels, on_device(): pl.pallas_call(last_kernel, out_shape=jax.ShapeDtypeStruct((2 * boxes, pa...  6.3 us
    ppermute x2, starting transfers between devices, shifted(): lax.ppermute(value, axis, [(source, source + steps) for source in range(f...  5.56 us
    pallas_call x1, Pallas kernels, on_device(): pl.pallas_call(radiate_kernel, out_shape=jax.ShapeDtypeStruct((devices, l...  3.68 us
  transfers between devices with their start and end apart: 3, of which 1 were waited for; matrix products, arithmetic and copies ran while one was open for 0% of the time, Pallas kernels for 27%

profile of v1, /device:TPU:11, one launch (start us, length us, event | category | flops | bytes accessed | tf_op | source)
XLA Modules:
  0.0 77.7 jit_solution(14586323206629368681)
XLA Ops:
  0.0 1.6 %copy-done = bf16[512,2048]{1,0:T(8,128)(2,1)S(1)} copy-done((bf16[512,2048]{1,0:T(8,128)(2,1)S(1)}, bf16[512,2048]{1,0:T(8,128)(2,1)}, u32[]{:S(2)}) %copy-start) | copy-done | bytes 2097176
  1.6 2.2 %copy-done.4 = bf16[16,128,1024]{2,1,0:T(8,128)(2,1)S(1)} copy-done((bf16[16,128,1024]{2,1,0:T(8,128)(2,1)S(1)}, bf16[16,128,1024]{2,1,0:T(8,128)(2,1)}, u32[]{:S(2)}) %copy-start.4) | copy-done | bytes 4194328
  3.8 0.9 %copy-done.8 = f32[8,2,2048]{2,1,0:T(2,128)S(1)} copy-done((f32[8,2,2048]{2,1,0:T(2,128)S(1)}, f32[8,2,2048]{2,1,0:T(2,128)}, u32[]{:S(2)}) %copy-start.8) | copy-done | bytes 131096
  4.7 0.7 copy-done.10
  5.4 0.7 copy-done.12
  6.1 3.7 %shard_map.145 = bf16[32,96,128]{2,1,0:T(8,128)(2,1)} custom-call(bf16[32,128]{1,0:T(8,128)(2,1)S(1)} %bitcast.22, bf16[16,128,1024]{2,1,0:T(8,128)(2,1)S(1)} %copy-done.4, s32[4,32]{1,0:T(4,128)S(1)} %bitcast.26, bf16[512,2048]{1,0:T(8,128)(2,1)S(1)} %copy-done, f32[256,128]{1,0:T(8,128)S(1)} %bitcast.20), custom_call_target="tpu_custom_call" | custom-call | flops 1000000000 | bytes 8388608 | tf_op jit(solution)/shard_map/pallas_call | solution.py:384
  9.8 6.3 %all-to-all-start = ((bf16[32,96,128]{2,1,0:T(8,128)(2,1)}), bf16[32,96,128]{2,1,0:T(8,128)(2,1)S(1)}, u32[]{:S(2)}, u32[]{:S(2)}) async-start(bf16[32,96,128]{2,1,0:T(8,128)(2,1)} %shard_map.145), calls=%async_computation | async-start | bytes 1572864 | tf_op jit(solution)/shard_map/all_to_all | solution.py:399
  16.1 0.0 copy-done.11
  16.1 2.3 %collective-permute-start.1 = (bf16[32,128]{1,0:T(8,128)(2,1)S(1)}, bf16[32,128]{1,0:T(8,128)(2,1)S(1)}, u32[]{:S(2)}, u32[]{:S(2)}) collective-permute-start(bf16[32,128]{1,0:T(8,128)(2,1)S(1)} %bitcast.23), channel_id=1, source_target_pairs={{1,0},{2,1},{3,2},{4,3},{5,4},{6,5},{7,6},{8,7},{9,8},{10,9},{11,1... | collective-permute-start | bytes 24584 | tf_op jit(solution)/shard_map/ppermute | solution.py:34
  18.4 3.3 %collective-permute-start = (bf16[32,128]{1,0:T(8,128)(2,1)S(1)}, bf16[32,128]{1,0:T(8,128)(2,1)S(1)}, u32[]{:S(2)}, u32[]{:S(2)}) collective-permute-start(bf16[32,128]{1,0:T(8,128)(2,1)S(1)} %bitcast.24), channel_id=1, source_target_pairs={{0,1},{1,2},{2,3},{3,4},{4,5},{5,6},{6,7},{7,8},{8,9},{9,10},{10,1... | collective-permute-start | bytes 24584 | tf_op jit(solution)/shard_map/ppermute | solution.py:34
  21.7 13.8 %collective-permute-done.1.upper_ref = bf16[32,128]{1,0:T(8,128)(2,1)S(1)} collective-permute-done((bf16[32,128]{1,0:T(8,128)(2,1)S(1)}, bf16[32,128]{1,0:T(8,128)(2,1)S(1)}, u32[]{:S(2)}, u32[]{:S(2)}) %collective-permute-start.1) | collective-permute-done | bytes 8224 | tf_op jit(solution)/shard_map/ppermute | solution.py:34
  35.5 0.0 collective-permute-done.lower_ref
  35.5 0.0 copy-done.16
  35.6 0.0 copy-start.13
  35.6 1.7 %copy-done.13 = bf16[316,2,2048]{2,1,0:T(2,128)(2,1)S(1)} copy-done((bf16[316,2,2048]{2,1,0:T(2,128)(2,1)S(1)}, bf16[316,2,2048]{2,1,0:T(2,128)(2,1)}, u32[]{:S(2)}) %copy-start.13) | copy-done | bytes 2588696
  37.3 1.1 %copy-done.14 = bf16[316,2,512]{2,1,0:T(2,128)(2,1)S(1)} copy-done((bf16[316,2,512]{2,1,0:T(2,128)(2,1)S(1)}, bf16[316,2,512]{2,1,0:T(2,128)(2,1)}, u32[]{:S(2)}) %copy-start.14) | copy-done | bytes 647192
  38.4 21.2 %shard_map.146 = (f32[32,128]{1,0:T(8,128)S(1)}, f32[16,128,1024]{2,1,0:T(8,128)S(1)}, f32[128,4096]{1,0:T(8,128)S(1)}) custom-call(bf16[32,128]{1,0:T(8,128)(2,1)S(1)} %collective-permute-done.lower_ref, bf16[32,128]{1,0:T(8,128)(2,1)S(1)} %bitcast.25, bf16[32,128]{1,0:T(8,128)(2,1)S(1)} %collective-permute-done.1.upper_ref, s32[16,27]{1,0:T(8,128)S(1)} %copy-done.19, ...), custom_call_target="tpu_custom_call" | custom-call | flops 10000000000 | bytes 20971520 | tf_op jit(solution)/shard_map/pallas_call | solution.py:401
  59.6 3.3 %copy-done.2 = f32[16,128,1024]{2,1,0:T(8,128)} copy-done((f32[16,128,1024]{2,1,0:T(8,128)}, f32[16,128,1024]{2,1,0:T(8,128)S(1)}, u32[]{:S(2)}) %copy-start.2) | copy-done | bytes 8388632
  62.8 1.4 %copy-done.6 = f32[128,4096]{1,0:T(8,128)} copy-done((f32[128,4096]{1,0:T(8,128)}, f32[128,4096]{1,0:T(8,128)S(1)}, u32[]{:S(2)}) %copy-start.6) | copy-done | bytes 2097176
  64.2 0.0 all-to-all-done.arrived_ref
  64.2 3.4 %copy-done.3 = f32[16,128,1024]{2,1,0:T(8,128)S(1)} copy-done((f32[16,128,1024]{2,1,0:T(8,128)S(1)}, f32[16,128,1024]{2,1,0:T(8,128)}, u32[]{:S(2)}) %copy-start.3) | copy-done | bytes 8388632
  67.6 2.2 %copy-done.5 = bf16[16,128,1024]{2,1,0:T(8,128)(2,1)S(1)} copy-done((bf16[16,128,1024]{2,1,0:T(8,128)(2,1)S(1)}, bf16[16,128,1024]{2,1,0:T(8,128)(2,1)}, u32[]{:S(2)}) %copy-start.5) | copy-done | bytes 4194328
  69.8 1.6 %copy-done.7 = f32[128,4096]{1,0:T(8,128)S(1)} copy-done((f32[128,4096]{1,0:T(8,128)S(1)}, f32[128,4096]{1,0:T(8,128)}, u32[]{:S(2)}) %copy-start.7) | copy-done | bytes 2097176
  71.4 6.3 %shard_map.147 = f32[32,128]{1,0:T(8,128)} custom-call(bf16[32,96,128]{2,1,0:T(8,128)(2,1)S(1)} %all-to-all-done.arrived_ref, f32[16,128,1024]{2,1,0:T(8,128)S(1)} %copy-done.3, f32[128,4096]{1,0:T(8,128)S(1)} %copy-done.7, f32[256,128]{1,0:T(8,128)S(1)} %bitcast.21, bf16[512,2048]{1,0:T(8,128)(2,1)S(1)} %copy-done.1, bf16[16,128,1024]{2,1,0:T(8,128)(2,1)S(1)} %copy-done.5, ...), custom_call_target="tpu_custom_call" | custom-call | flops 1000000000 | bytes 8388608 | tf_op jit(solution)/shard_map/pallas_call | solution.py:442
  (27 shorter events, 0.0 us)
Async XLA Ops:
  0.0 1.6 %copy-start = (bf16[512,2048]{1,0:T(8,128)(2,1)S(1)}, bf16[512,2048]{1,0:T(8,128)(2,1)}, u32[]{:S(2)}) copy-start(bf16[512,2048]{1,0:T(8,128)(2,1)} %interp_ref.3) | copy-start | bytes 6291460
  1.6 2.2 %copy-start.4 = (bf16[16,128,1024]{2,1,0:T(8,128)(2,1)S(1)}, bf16[16,128,1024]{2,1,0:T(8,128)(2,1)}, u32[]{:S(2)}) copy-start(bf16[16,128,1024]{2,1,0:T(8,128)(2,1)} %radiate_ref.1) | copy-start | bytes 12582916
  3.8 0.9 %copy-start.8 = (f32[8,2,2048]{2,1,0:T(2,128)S(1)}, f32[8,2,2048]{2,1,0:T(2,128)}, u32[]{:S(2)}) copy-start(f32[8,2,2048]{2,1,0:T(2,128)} %param.26) | copy-start | bytes 393220
  4.7 0.7 copy-start.10
  5.4 0.7 copy-start.12
  6.1 10.1 %copy-start.11 = (bf16[16,2,128]{2,1,0:T(2,128)(2,1)S(1)}, bf16[16,2,128]{2,1,0:T(2,128)(2,1)}, u32[]{:S(2)}) copy-start(bf16[16,2,128]{2,1,0:T(2,128)(2,1)} %param.15) | copy-start | bytes 24580
  6.1 29.4 %copy-start.15 = (s32[16,189]{1,0:T(8,128)S(1)}, s32[16,189]{1,0:T(8,128)}, u32[]{:S(2)}) copy-start(s32[16,189]{1,0:T(8,128)} %slot_ref.1) | copy-start | bytes 36292
  6.1 29.4 %copy-start.16 = (s32[16,189]{1,0:T(8,128)S(1)}, s32[16,189]{1,0:T(8,128)}, u32[]{:S(2)}) copy-start(s32[16,189]{1,0:T(8,128)} %type_ref.1) | copy-start | bytes 36292
  6.1 29.4 %copy-start.17 = (s32[16,189]{1,0:T(8,128)S(1)}, s32[16,189]{1,0:T(8,128)}, u32[]{:S(2)}) copy-start(s32[16,189]{1,0:T(8,128)} %par_far_ref.1) | copy-start | bytes 36292
  6.1 29.5 %copy-start.18 = (s32[16,189]{1,0:T(8,128)S(1)}, s32[16,189]{1,0:T(8,128)}, u32[]{:S(2)}) copy-start(s32[16,189]{1,0:T(8,128)} %par_type_ref.1) | copy-start | bytes 36292
  6.1 29.5 %copy-start.19 = (s32[16,27]{1,0:T(8,128)S(1)}, s32[16,27]{1,0:T(8,128)}, u32[]{:S(2)}) copy-start(s32[16,27]{1,0:T(8,128)} %near_src_ref.1) | copy-start | bytes 5188
  6.1 29.5 %copy-start.20 = (s32[16,27]{1,0:T(8,128)S(1)}, s32[16,27]{1,0:T(8,128)}, u32[]{:S(2)}) copy-start(s32[16,27]{1,0:T(8,128)} %near_tile_ref.1) | copy-start | bytes 5188
  9.8 54.4 %all-to-all-start = ((bf16[32,96,128]{2,1,0:T(8,128)(2,1)}), bf16[32,96,128]{2,1,0:T(8,128)(2,1)S(1)}, u32[]{:S(2)}, u32[]{:S(2)}) async-start(bf16[32,96,128]{2,1,0:T(8,128)(2,1)} %shard_map.145), calls=%async_computation | async-start | bytes 1572864 | tf_op jit(solution)/shard_map/all_to_all | solution.py:399
  16.1 19.4 %collective-permute-start.1 = (bf16[32,128]{1,0:T(8,128)(2,1)S(1)}, bf16[32,128]{1,0:T(8,128)(2,1)S(1)}, u32[]{:S(2)}, u32[]{:S(2)}) collective-permute-start(bf16[32,128]{1,0:T(8,128)(2,1)S(1)} %bitcast.23), channel_id=1, source_target_pairs={{1,0},{2,1},{3,2},{4,3},{5,4},{6,5},{7,6},{8,7},{9,8},{10,9},{11,1... | collective-permute-start | bytes 24584 | tf_op jit(solution)/shard_map/ppermute | solution.py:34
  18.4 17.1 %collective-permute-start = (bf16[32,128]{1,0:T(8,128)(2,1)S(1)}, bf16[32,128]{1,0:T(8,128)(2,1)S(1)}, u32[]{:S(2)}, u32[]{:S(2)}) collective-permute-start(bf16[32,128]{1,0:T(8,128)(2,1)S(1)} %bitcast.24), channel_id=1, source_target_pairs={{0,1},{1,2},{2,3},{3,4},{4,5},{5,6},{6,7},{7,8},{8,9},{9,10},{10,1... | collective-permute-start | bytes 24584 | tf_op jit(solution)/shard_map/ppermute | solution.py:34
  35.6 1.7 %copy-start.13 = (bf16[316,2,2048]{2,1,0:T(2,128)(2,1)S(1)}, bf16[316,2,2048]{2,1,0:T(2,128)(2,1)}, u32[]{:S(2)}) copy-start(bf16[316,2,2048]{2,1,0:T(2,128)(2,1)} %param.29) | copy-start | bytes 7766020
  37.3 1.1 %copy-start.14 = (bf16[316,2,512]{2,1,0:T(2,128)(2,1)S(1)}, bf16[316,2,512]{2,1,0:T(2,128)(2,1)}, u32[]{:S(2)}) copy-start(bf16[316,2,512]{2,1,0:T(2,128)(2,1)} %param.24) | copy-start | bytes 1941508
  38.4 25.8 %copy-start.1 = (bf16[512,2048]{1,0:T(8,128)(2,1)S(1)}, bf16[512,2048]{1,0:T(8,128)(2,1)}, u32[]{:S(2)}) copy-start(bf16[512,2048]{1,0:T(8,128)(2,1)} %interp_ref.3) | copy-start | bytes 6291460
  38.4 25.8 %copy-start.9 = (f32[8,2,2048]{2,1,0:T(2,128)S(1)}, f32[8,2,2048]{2,1,0:T(2,128)}, u32[]{:S(2)}) copy-start(f32[8,2,2048]{2,1,0:T(2,128)} %param.26) | copy-start | bytes 393220
  59.5 3.3 %copy-start.2 = (f32[16,128,1024]{2,1,0:T(8,128)}, f32[16,128,1024]{2,1,0:T(8,128)S(1)}, u32[]{:S(2)}) copy-start(f32[16,128,1024]{2,1,0:T(8,128)S(1)} %get-tuple-element.8.d_lo_ref) | copy-start | bytes 25165828
  62.8 1.4 %copy-start.6 = (f32[128,4096]{1,0:T(8,128)}, f32[128,4096]{1,0:T(8,128)S(1)}, u32[]{:S(2)}) copy-start(f32[128,4096]{1,0:T(8,128)S(1)} %get-tuple-element.9.d_hi_ref) | copy-start | bytes 6291460
  64.2 3.4 %copy-start.3 = (f32[16,128,1024]{2,1,0:T(8,128)S(1)}, f32[16,128,1024]{2,1,0:T(8,128)}, u32[]{:S(2)}) copy-start(f32[16,128,1024]{2,1,0:T(8,128)} %copy-done.2) | copy-start | bytes 25165828
  67.6 2.2 %copy-start.5 = (bf16[16,128,1024]{2,1,0:T(8,128)(2,1)S(1)}, bf16[16,128,1024]{2,1,0:T(8,128)(2,1)}, u32[]{:S(2)}) copy-start(bf16[16,128,1024]{2,1,0:T(8,128)(2,1)} %receive_ref.1) | copy-start | bytes 12582916
  69.8 1.6 %copy-start.7 = (f32[128,4096]{1,0:T(8,128)S(1)}, f32[128,4096]{1,0:T(8,128)}, u32[]{:S(2)}) copy-start(f32[128,4096]{1,0:T(8,128)} %copy-done.6) | copy-start | bytes 6291460

commit v2 on v1

v2 whole, which is shorter than its diff:
```python
import functools

import jax
import jax.numpy as jnp
from jax import lax
from jax.experimental import pallas as pl
from jax.experimental.pallas import tpu as pltpu
from jax.sharding import PartitionSpec as P

F32 = jnp.float32
BF16 = jnp.bfloat16
LANE = 128
VMEM_SPEC = pl.BlockSpec(memory_space=pltpu.VMEM)
SMEM_SPEC = pl.BlockSpec(memory_space=pltpu.SMEM)
ANY_SPEC = pl.BlockSpec(memory_space=pl.ANY)
HBM_SPEC = pl.BlockSpec(memory_space=pltpu.HBM)
MIB = 1 << 20


def iota(shape, dim):
    return lax.broadcasted_iota(jnp.int32, shape, dim)


def dot_nn(lhs, rhs):
    return lax.dot_general(lhs, rhs, (((1,), (0,)), ((), ())), preferred_element_type=F32)


def dot_nt(lhs, rhs):
    return lax.dot_general(lhs, rhs, (((1,), (1,)), ((), ())), preferred_element_type=F32)


def shifted(value, axis, steps):
    count = lax.axis_size(axis)
    first, last = (max(0, -steps), min(count, count - steps))
    return lax.ppermute(value, axis, [(source, source + steps) for source in range(first, last)])


def fetch(pairs, sems, first=0):
    copies = []
    for k, (source, target) in enumerate(pairs):
        copies.append(pltpu.make_async_copy(source, target, sems.at[first + k]))
        copies[-1].start()
    return copies


def radiate_kernel(
    dens_hbm,
    radiate_ref,
    send_hbm,
    interp_hbm,
    shift_hbm,
    out_ref,
    rad,
    dens_ref,
    send_ref,
    interp_ref,
    shift_ref,
    summed,
    table,
    parent,
    sems,
    extra,
):
    boxes = rad.shape[0]
    width = rad.shape[2] // 2
    per_step = 4
    steps = boxes // per_step
    others = fetch(
        [(dens_hbm, dens_ref), (send_hbm, send_ref), (shift_hbm, shift_ref)], extra
    )
    copies = []
    for step in range(steps):
        part = pl.ds(step * per_step, per_step)
        copies.append(pltpu.make_async_copy(radiate_ref.at[part], rad.at[part], sems.at[step]))
        copies[-1].start()
    others += fetch([(interp_hbm, interp_ref)], extra, 3)
    others[0].wait()
    dens = dens_ref[...].astype(F32)
    owner = (iota(dens.shape, 0) // 2) % per_step
    blocks = jnp.concatenate([jnp.where(owner == b, dens, 0.0) for b in range(per_step)], 1)
    for step in range(steps):
        copies[step].wait()
        rows = slice(step * 2 * per_step, (step + 1) * 2 * per_step)
        weights = rad[step * per_step : (step + 1) * per_step].reshape(per_step * LANE, 2 * width)
        summed[rows] = dot_nn(blocks[rows].astype(BF16), weights).reshape(
            2 * per_step, 2 * width // LANE, LANE
        )
    chunks = width // LANE
    re_chunks, im_chunks = [], []
    for r in range(chunks):
        first_lo = summed[pl.ds(0, boxes, stride=2), r, :]
        first_hi = summed[pl.ds(0, boxes, stride=2), chunks + r, :]
        second_lo = summed[pl.ds(1, boxes, stride=2), r, :]
        second_hi = summed[pl.ds(1, boxes, stride=2), chunks + r, :]
        re_chunks.append((first_lo - second_hi).astype(BF16))
        im_chunks.append((first_hi + second_lo).astype(BF16))
    re_part = jnp.concatenate(re_chunks, 1)
    im_part = jnp.concatenate(im_chunks, 1)
    for r in range(chunks):
        table[pl.ds(r, boxes, stride=8), :] = re_chunks[r].astype(F32)
        table[pl.ds(chunks + r, boxes, stride=8), :] = im_chunks[r].astype(F32)
    table[pl.ds(boxes * 8, 8), :] = jnp.zeros((8, LANE), F32)
    for copy in others[1:]:
        copy.wait()
    wide = dot_nn(jnp.concatenate([re_part, im_part], 0), interp_ref[...])
    hi_chunks = wide.shape[1] // LANE
    parents = boxes // 8
    for r in range(hi_chunks):
        cols = slice(r * LANE, (r + 1) * LANE)
        s_re = shift_ref[pl.ds(2 * r, 8, stride=2 * hi_chunks), :]
        s_im = shift_ref[pl.ds(2 * r + 1, 8, stride=2 * hi_chunks), :]
        for p in range(parents):
            w_re = wide[p * 8 : (p + 1) * 8, cols]
            w_im = wide[boxes + p * 8 : boxes + (p + 1) * 8, cols]
            row = p * 2 * hi_chunks + r
            parent[row : row + 1] = jnp.sum(w_re * s_re - w_im * s_im, 0, keepdims=True)
            row += hi_chunks
            parent[row : row + 1] = jnp.sum(w_re * s_im + w_im * s_re, 0, keepdims=True)
    slots, devices = send_ref.shape
    hi_rows = parents * 2 * hi_chunks
    parent_block = parent[...].astype(BF16)

    def fill(d, carry):
        for k in range(slots // 2):
            pair = [
                table[pl.ds(pl.multiple_of(send_ref[2 * k + h, d] * 8, 8), 8), :] for h in range(2)
            ]
            out_ref[d, 16 * k : 16 * (k + 1)] = jnp.concatenate(pair, 0).astype(BF16)
        out_ref[d, 8 * slots : 8 * slots + hi_rows] = parent_block
        return carry

    lax.fori_loop(0, devices, fill, 0)


def middle_kernel(
    types,
    box_total,
    lower_hbm,
    dens_hbm,
    upper_hbm,
    near_src_hbm,
    near_tile_hbm,
    tiles_hbm,
    slot_hbm,
    type_hbm,
    op_lo_hbm,
    par_far_hbm,
    par_type_hbm,
    op_hi_hbm,
    near_ref,
    d_lo_ref,
    d_hi_ref,
    tiles,
    halo,
    near_src_ref,
    near_tile_ref,
    slot_ref,
    type_ref,
    op_lo_ref,
    par_far_ref,
    par_type_ref,
    op_hi,
    dens3,
    left,
    right,
    acc,
    code,
    index,
    wide_op,
    op_lo,
    sems,
    extra,
):
    boxes, near = near_src_ref.shape
    tile_count = tiles.shape[0]
    steps = sems.shape[0]
    per_step = tile_count // steps
    others = fetch(
        [
            (near_src_hbm, near_src_ref),
            (near_tile_hbm, near_tile_ref),
            (op_lo_hbm, op_lo_ref),
            (slot_hbm, slot_ref),
            (type_hbm, type_ref),
            (lower_hbm, halo.at[0]),
            (dens_hbm, halo.at[1]),
            (upper_hbm, halo.at[2]),
            (par_far_hbm, par_far_ref),
            (par_type_hbm, par_type_ref),
            (op_hi_hbm, op_hi),
        ],
        extra,
    )

    def tile_copy(step):
        part = pl.ds(step * per_step, per_step)
        return pltpu.make_async_copy(tiles_hbm.at[part], tiles.at[part], sems.at[step])

    for step in range(steps):
        tile_copy(step).start()
    position = lax.axis_index("box") * lax.axis_size("samp") + lax.axis_index("samp")
    d_hi_ref[...] = jnp.zeros(d_hi_ref.shape, F32)
    acc[...] = jnp.zeros(acc.shape, F32)
    index[...] = jnp.full(index.shape, -1, jnp.int32)
    left[...] = jnp.zeros(left.shape, F32)
    right[...] = jnp.zeros(right.shape, F32)
    type_pad = op_lo.shape[0]
    chunks = op_lo.shape[1] // (2 * LANE)
    wide_op[types * 2 * chunks : type_pad * 2 * chunks] = jnp.zeros(
        ((type_pad - types) * 2 * chunks, LANE), F32
    )
    others[0].wait()
    others[1].wait()

    def locate(g, carry):
        for n in range(near):
            source = near_src_ref[g, n]
            live = source < box_total
            tile = jnp.where(live, near_tile_ref[g, n] - position * tile_count, tile_count)
            code[tile] = g * 64 + source - (position - 1) * boxes
        return carry

    lax.fori_loop(0, boxes, locate, 0)

    for copy in others[2:]:
        copy.wait()
    wide_op[0 : types * 2 * chunks] = op_lo_ref[...].astype(F32)
    for c in range(2):
        for r in range(chunks):
            col = (c * chunks + r) * LANE
            op_lo[:, col : col + LANE] = wide_op[
                pl.ds(2 * r + c, type_pad, stride=2 * chunks), :
            ].astype(BF16)
    far = slot_ref.shape[1]
    index[0:boxes, 0:far] = slot_ref[...]
    index[boxes : 2 * boxes, 0:far] = type_ref[...]
    for k in range(3):
        dens3[pl.ds(2 * boxes * k, 2 * boxes), :] = halo[k].astype(F32)
    first = dens3[pl.ds(0, 3 * boxes, stride=2), :]
    second = dens3[pl.ds(1, 3 * boxes, stride=2), :]
    left[pl.ds(0, 3 * boxes, stride=8), :] = first
    left[pl.ds(1, 3 * boxes, stride=8), :] = second
    right[pl.ds(0, 3 * boxes, stride=8), :] = -second
    right[pl.ds(1, 3 * boxes, stride=8), :] = first

    slot_total = d_lo_ref.shape[1]
    per_boxes = boxes // steps
    faces = index.shape[1]
    parents = boxes // 8
    par_rows = d_hi_ref.shape[0] // parents
    hi_lines = op_hi.shape[0] // types
    empty = par_rows // hi_lines - 1
    own = lax.axis_index("samp") * parents
    far_step = -(-far // steps)

    def counts(g):
        source = index[pl.ds(g, 1), :]
        kind = index[pl.ds(boxes + g, 1), :]
        by_source = jnp.where(iota((slot_total, faces), 0) == source, 1.0, 0.0).astype(BF16)
        by_type = jnp.where(iota((type_pad, faces), 0) == kind, 1.0, 0.0).astype(BF16)
        return dot_nt(by_source, by_type).astype(BF16)

    def step_boxes(step, carry):
        start = step * per_boxes
        tally = jnp.concatenate([counts(start + k) for k in range(per_boxes)], 0)
        summed = dot_nn(tally, op_lo[...]).astype(d_lo_ref.dtype)
        d_lo_ref[pl.ds(start, per_boxes)] = summed.reshape(
            per_boxes, slot_total, 2 * chunks * LANE
        )
        tile_copy(step).wait()
        for pair in range(per_step // 2):
            tile = step * per_step + 2 * pair
            both = tiles[pl.ds(tile, 2)]
            weights = jnp.concatenate(
                [both[:, 0].reshape(2 * LANE, LANE), both[:, 1].reshape(2 * LANE, LANE)], 1
            )
            owners, lefts, rights = [], [], []
            for h in range(2):
                entry = code[tile + h]
                row = pl.ds(pl.multiple_of((entry & 63) * 8, 8), 8)
                owners.append(entry >> 6)
                lefts.append(left[row])
                rights.append(right[row])
            lhs = jnp.concatenate([jnp.concatenate(lefts, 0), jnp.concatenate(rights, 0)], 1)
            product = dot_nt(lhs.astype(BF16), weights)
            for h in range(2):
                acc[owners[h]] = (
                    acc[owners[h]] + product[8 * h : 8 * (h + 1), h * LANE : (h + 1) * LANE]
                )
        for e in range(far_step):
            f = step * far_step + e
            inside = f < far
            f = jnp.minimum(f, far - 1)
            for p in range(parents):
                source = jnp.where(inside, par_far_ref[own + p, f], empty)
                kind = par_type_ref[own + p, f]
                at = pl.ds(pl.multiple_of(p * par_rows + source * hi_lines, hi_lines), hi_lines)
                term = op_hi[pl.ds(pl.multiple_of(kind * hi_lines, hi_lines), hi_lines)]
                d_hi_ref[at] = d_hi_ref[at] + term.astype(F32)
        return carry

    lax.fori_loop(0, steps, step_boxes, 0)
    for g in range(boxes):
        row = 2 * g
        near_ref[row : row + 2] = acc[g, 0:2] + 0.5 * dens3[pl.ds(2 * boxes + row, 2), :]


def last_kernel(
    arrived_ref,
    d_lo_ref,
    d_hi_ref,
    shift_hbm,
    interp_hbm,
    receive_ref,
    near_ref,
    out_ref,
    receive,
    shift_ref,
    interp_ref,
    slots,
    upward,
    down,
    incoming,
    blend,
    sems,
    extra,
):
    boxes = receive.shape[0]
    per_step = 4
    steps = boxes // per_step
    others = fetch([(shift_hbm, shift_ref), (interp_hbm, interp_ref)], extra)
    copies = []
    for step in range(steps):
        part = pl.ds(step * per_step, per_step)
        copies.append(pltpu.make_async_copy(receive_ref.at[part], receive.at[part], sems.at[step]))
        copies[-1].start()
    devices, lines, _ = arrived_ref.shape
    own_parents = boxes // 8
    slot_total = d_lo_ref.shape[1]
    chunks = d_lo_ref.shape[2] // (2 * LANE)
    lo_lines = slot_total // devices * 2 * chunks
    hi_lines = (lines - lo_lines) // own_parents
    hi_chunks = hi_lines // 2
    par_rows = d_hi_ref.shape[0] // own_parents
    slots[...] = arrived_ref[:, :lo_lines, :].astype(F32).reshape(devices * lo_lines, LANE)

    def gather(device, sums):
        for q in range(own_parents):
            line = lo_lines + q * hi_lines
            first = arrived_ref[device, line : line + hi_chunks].astype(F32)
            second = arrived_ref[device, line + hi_chunks : line + hi_lines].astype(F32)
            new = []
            for p in range(own_parents):
                row = p * par_rows + (device * own_parents + q) * hi_lines
                o_re = d_hi_ref[pl.ds(row, hi_chunks, stride=2), :]
                o_im = d_hi_ref[pl.ds(row + 1, hi_chunks, stride=2), :]
                new.append(sums[2 * p] + (o_re * first - o_im * second))
                new.append(sums[2 * p + 1] + (o_re * second + o_im * first))
            sums = tuple(new)
        return sums

    zero = jnp.zeros((hi_chunks, LANE), F32)
    sums = lax.fori_loop(0, devices, gather, (zero,) * (2 * own_parents), unroll=4)
    for k in range(2 * own_parents):
        upward[k * hi_chunks : (k + 1) * hi_chunks] = sums[k]
    others[0].wait()
    for r in range(hi_chunks):
        s_re = shift_ref[pl.ds(2 * r, 8, stride=2 * hi_chunks), :]
        s_im = shift_ref[pl.ds(2 * r + 1, 8, stride=2 * hi_chunks), :]
        re_rows, im_rows = [], []
        for p in range(own_parents):
            row = 2 * p * hi_chunks + r
            t_re = upward[row : row + 1]
            t_im = upward[row + hi_chunks : row + hi_chunks + 1]
            re_rows.append(s_re * t_re + s_im * t_im)
            im_rows.append(s_re * t_im - s_im * t_re)
        cols = slice(r * LANE, (r + 1) * LANE)
        down[:, cols] = jnp.concatenate(re_rows + im_rows, 0).astype(BF16)
    for r in range(chunks):
        first = slots[pl.ds(r, slot_total, stride=2 * chunks), :]
        second = slots[pl.ds(chunks + r, slot_total, stride=2 * chunks), :]
        for g in range(boxes):
            o_re = d_lo_ref[g, :, r * LANE : (r + 1) * LANE].astype(F32)
            o_im = d_lo_ref[g, :, (chunks + r) * LANE : (chunks + r + 1) * LANE].astype(F32)
            cols = slice(r * LANE, (r + 1) * LANE)
            incoming[g : g + 1, cols] = jnp.sum(o_re * first - o_im * second, 0, keepdims=True)
            incoming[boxes + g : boxes + g + 1, cols] = jnp.sum(
                o_re * second + o_im * first, 0, keepdims=True
            )
    others[1].wait()
    total = incoming[...] + dot_nt(down[...], interp_ref[...])
    total = total.astype(BF16).astype(F32)
    for r in range(chunks):
        re_part = total[:boxes, r * LANE : (r + 1) * LANE]
        im_part = total[boxes:, r * LANE : (r + 1) * LANE]
        blend[pl.ds(0, boxes, stride=2), r, :] = re_part
        blend[pl.ds(1, boxes, stride=2), r, :] = im_part
        blend[pl.ds(0, boxes, stride=2), chunks + r, :] = -im_part
        blend[pl.ds(1, boxes, stride=2), chunks + r, :] = re_part
    owner = (iota((2 * per_step, LANE), 0) // 2) % per_step
    for step in range(steps):
        rows = slice(step * 2 * per_step, (step + 1) * 2 * per_step)
        lhs = jnp.concatenate([blend[rows, r, :] for r in range(2 * chunks)], 1).astype(BF16)
        copies[step].wait()
        weights = receive[step * per_step : (step + 1) * per_step]
        product = dot_nt(lhs, weights.reshape(per_step * LANE, 2 * chunks * LANE))
        total = near_ref[rows]
        for b in range(per_step):
            total = total + jnp.where(owner == b, product[:, b * LANE : (b + 1) * LANE], 0.0)
        out_ref[rows] = total


def in_hbm(array):
    return pltpu.with_memory_space_constraint(array, pltpu.HBM)


def in_vmem(array):
    return pltpu.with_memory_space_constraint(array, pltpu.VMEM)


def tiled_rows(array):
    count, parts, width = array.shape
    cut = array.reshape(count, parts, width // LANE, LANE)
    return cut.transpose(0, 2, 1, 3).reshape(-1, LANE)


def on_device(
    density,
    radiate,
    receive,
    near_tiles,
    near_src,
    near_tile,
    send_box,
    distant_pattern_slot,
    far_type,
    trans_lo,
    interp_matrix,
    shifts,
    par_far,
    par_type,
    trans_hi,
):
    boxes, _, panels = density.shape
    devices = lax.axis_size("box") * lax.axis_size("samp")
    slots = send_box.shape[2]
    types, _, width_lo = trans_lo.shape
    width_hi = trans_hi.shape[2]
    parents = boxes // 8
    slot_total = devices * slots
    par_total = devices * parents
    type_pad = -(-types // 8) * 8
    lines = slots * 2 * width_lo // LANE + parents * 2 * width_hi // LANE
    held = F32 if slot_total <= 128 else BF16
    rows = density.reshape(boxes * 2, panels)
    lower = shifted(rows, ("box", "samp"), 1)
    upper = shifted(rows, ("box", "samp"), -1)
    shift_rows = tiled_rows(shifts)
    mid = rows
    send = send_box[0].T
    outgoing = pl.pallas_call(
        radiate_kernel,
        out_shape=jax.ShapeDtypeStruct((devices, lines, LANE), BF16),
        in_specs=[HBM_SPEC] * 5,
        out_specs=VMEM_SPEC,
        scratch_shapes=[
            pltpu.VMEM(radiate.shape, BF16),
            pltpu.VMEM(rows.shape, BF16),
            pltpu.SMEM(send.shape, jnp.int32),
            pltpu.VMEM(interp_matrix.shape, BF16),
            pltpu.VMEM(shift_rows.shape, F32),
            pltpu.VMEM((2 * boxes, 2 * width_lo // LANE, LANE), F32),
            pltpu.VMEM((boxes * 8 + 8, LANE), F32),
            pltpu.VMEM((parents * 2 * width_hi // LANE, LANE), F32),
            pltpu.SemaphoreType.DMA((boxes // 4,)),
            pltpu.SemaphoreType.DMA((4,)),
        ],
        compiler_params=pltpu.CompilerParams(vmem_limit_bytes=12 * MIB),
        cost_estimate=pl.CostEstimate(flops=10**9, bytes_accessed=8 * MIB, transcendentals=0),
    )(*(in_hbm(x) for x in (rows, radiate, send, interp_matrix, shift_rows)))
    outgoing, lower, upper = lax.optimization_barrier((outgoing, lower, upper))
    arrived = lax.all_to_all(outgoing, ("box", "samp"), split_axis=0, concat_axis=0, tiled=True)
    tile_count = near_tiles.shape[0]
    far = far_type.shape
    par_shape = par_far.shape
    op_hi_rows = tiled_rows(trans_hi)
    op_lo_rows = tiled_rows(trans_lo)
    hi_lines = 2 * width_hi // LANE
    near, d_lo, d_hi = pl.pallas_call(
        functools.partial(middle_kernel, types, boxes * devices),
        out_shape=(
            pltpu.VMEM((2 * boxes, panels), F32),
            pltpu.VMEM((boxes, slot_total, 2 * width_lo), held),
            pltpu.VMEM((parents * (par_total + 1) * hi_lines, LANE), F32),
        ),
        in_specs=[ANY_SPEC, HBM_SPEC, ANY_SPEC] + [HBM_SPEC] * 9,
        out_specs=(VMEM_SPEC,) * 3,
        scratch_shapes=[
            pltpu.VMEM(near_tiles.shape, BF16),
            pltpu.VMEM((3, 2 * boxes, panels), BF16),
            pltpu.SMEM(near_src.shape, jnp.int32),
            pltpu.SMEM(near_src.shape, jnp.int32),
            pltpu.VMEM(far, jnp.int32),
            pltpu.VMEM(far, jnp.int32),
            pltpu.VMEM(op_lo_rows.shape, BF16),
            pltpu.SMEM(par_shape, jnp.int32),
            pltpu.SMEM(par_shape, jnp.int32),
            pltpu.VMEM(op_hi_rows.shape, BF16),
            pltpu.VMEM((6 * boxes, panels), F32),
            pltpu.VMEM((3 * boxes * 8, LANE), F32),
            pltpu.VMEM((3 * boxes * 8, LANE), F32),
            pltpu.VMEM((boxes, 8, LANE), F32),
            pltpu.SMEM((tile_count + 8,), jnp.int32),
            pltpu.VMEM((2 * boxes, 2 * LANE), jnp.int32),
            pltpu.VMEM((type_pad * 2 * width_lo // LANE, LANE), F32),
            pltpu.VMEM((type_pad, 2 * width_lo), BF16),
            pltpu.SemaphoreType.DMA((4,)),
            pltpu.SemaphoreType.DMA((11,)),
        ],
        compiler_params=pltpu.CompilerParams(vmem_limit_bytes=28 * MIB),
        cost_estimate=pl.CostEstimate(flops=10**10, bytes_accessed=20 * MIB, transcendentals=0),
    )(
        lower,
        mid,
        upper,
        near_src,
        near_tile,
        near_tiles,
        distant_pattern_slot,
        far_type,
        op_lo_rows,
        par_far,
        par_type,
        op_hi_rows,
    )
    lo_lines = slots * 2 * width_lo // LANE
    field = pl.pallas_call(
        last_kernel,
        out_shape=jax.ShapeDtypeStruct((2 * boxes, panels), F32),
        in_specs=[VMEM_SPEC] * 3 + [HBM_SPEC] * 3 + [VMEM_SPEC],
        out_specs=VMEM_SPEC,
        scratch_shapes=[
            pltpu.VMEM(receive.shape, BF16),
            pltpu.VMEM(shift_rows.shape, F32),
            pltpu.VMEM(interp_matrix.shape, BF16),
            pltpu.VMEM((devices * lo_lines, LANE), F32),
            pltpu.VMEM((parents * hi_lines, LANE), F32),
            pltpu.VMEM((2 * boxes, width_hi), BF16),
            pltpu.VMEM((2 * boxes, width_lo), F32),
            pltpu.VMEM((2 * boxes, 2 * width_lo // LANE, LANE), F32),
            pltpu.SemaphoreType.DMA((boxes // 4,)),
            pltpu.SemaphoreType.DMA((2,)),
        ],
        compiler_params=pltpu.CompilerParams(vmem_limit_bytes=12 * MIB),
        cost_estimate=pl.CostEstimate(flops=10**9, bytes_accessed=8 * MIB, transcendentals=0),
    )(arrived, in_vmem(d_lo), in_vmem(d_hi), shift_rows, interp_matrix, receive, near)
    return field.reshape(boxes, 2, panels)


def solution(mesh):
    both = ("box", "samp")
    return jax.shard_map(
        on_device,
        mesh=mesh,
        in_specs=(
            P(both, None, None),
            P(both, None, None),
            P(both, None, None),
            P(both, None, None, None),
            P(both, None),
            P(both, None),
            P(both, None, None),
            P(both, None),
            P(both, None),
            P(),
            P(),
            P(),
            P("box", None),
            P("box", None),
            P(),
        ),
        out_specs=P(both, None, None),
        check_vma=False,
    )
```

time: 78.2 us -> 55.1 us (0.70)
  the two profiles are of different devices: /device:TPU:11 before, /device:TPU:0 now
where the time goes in v2:
time: 55.1 us; the launch traced here: 54.7 us
  Pallas kernels  21.9 us (40%)
  starting transfers between devices  14.9 us (27%)
  local copies, waits for them, and re-layouts  14.6 us (26%)
  waiting for transfers between devices  3.08 us (6%)
    unnamed x32, local copies, waits for them, and re-layouts  14.6 us
    pallas_call x1, Pallas kernels, on_device(): pl.pallas_call(functools.partial(middle_kernel, types, boxes * devices),...  11.4 us
    all_to_all x1, starting transfers between devices, on_device(): lax.all_to_all(outgoing, ('box', 'samp'), split_axis=0, concat_axis=0, ti...  10.6 us
    pallas_call x1, Pallas kernels, on_device(): pl.pallas_call(last_kernel, out_shape=jax.ShapeDtypeStruct((2 * boxes, pa...  5.74 us
    pallas_call x1, Pallas kernels, on_device(): pl.pallas_call(radiate_kernel, out_shape=jax.ShapeDtypeStruct((devices, l...  4.76 us
    ppermute x2, starting transfers between devices, shifted(): lax.ppermute(value, axis, [(source, source + steps) for source in range(f...  4.31 us
    all_to_all x1, waiting for transfers between devices, on_device(): lax.all_to_all(outgoing, ('box', 'samp'), split_axis=0, concat_axis=0, ti...  3.08 us
  transfers between devices with their start and end apart: 3, of which 1 were waited for; matrix products, arithmetic and copies ran while one was open for 0% of the time, Pallas kernels for 29%

profile of v2, /device:TPU:0, one launch (start us, length us, event | category | flops | bytes accessed | tf_op | source)
XLA Modules:
  0.0 54.7 jit_solution(16930447032010455796)
XLA Ops:
  0.0 1.3 %collective-permute-start.1 = (bf16[32,128]{1,0:T(8,128)(2,1)}, bf16[32,128]{1,0:T(8,128)(2,1)S(1)}, u32[]{:S(2)}, u32[]{:S(2)}) collective-permute-start(bf16[32,128]{1,0:T(8,128)(2,1)} %bitcast.22), channel_id=1, source_target_pairs={{1,0},{2,1},{3,2},{4,3},{5,4},{6,5},{7,6},{8,7},{9,8},{10,9},{11,1... | collective-permute-start | bytes 24584 | tf_op jit(solution)/shard_map/ppermute | solution.py:35
  1.3 3.0 %collective-permute-start = (bf16[32,128]{1,0:T(8,128)(2,1)}, bf16[32,128]{1,0:T(8,128)(2,1)S(1)}, u32[]{:S(2)}, u32[]{:S(2)}) collective-permute-start(bf16[32,128]{1,0:T(8,128)(2,1)} %bitcast.23), channel_id=1, source_target_pairs={{0,1},{1,2},{2,3},{3,4},{4,5},{5,6},{6,7},{7,8},{8,9},{9,10},{10,1... | collective-permute-start | bytes 24584 | tf_op jit(solution)/shard_map/ppermute | solution.py:35
  4.3 0.0 copy-start.7
  4.3 0.0 copy-start.10
  4.3 0.0 copy-start.11
  4.4 0.0 copy-start.12
  4.4 0.0 copy-start.13
  4.4 0.0 copy-start.14
  4.4 0.0 copy-start.15
  4.4 4.8 %shard_map.145 = bf16[32,96,128]{2,1,0:T(8,128)(2,1)} custom-call(bf16[32,128]{1,0:T(8,128)(2,1)} %bitcast.24, bf16[16,128,1024]{2,1,0:T(8,128)(2,1)} %radiate_ref.1, s32[4,32]{1,0:T(4,128)} %bitcast.28, bf16[512,2048]{1,0:T(8,128)(2,1)} %interp_hbm.3, f32[256,128]{1,0:T(8,128)} %bitcast.20), custom_call_target="tpu_custom_call" | custom-call | flops 1000000000 | bytes 8388608 | tf_op jit(solution)/shard_map/pallas_call | solution.py:461
  9.2 0.0 collective-permute-done.1.upper_hbm
  9.2 0.0 collective-permute-done.lower_hbm
  9.2 10.6 %all-to-all-start = ((bf16[32,96,128]{2,1,0:T(8,128)(2,1)}), bf16[32,96,128]{2,1,0:T(8,128)(2,1)S(1)}, u32[]{:S(2)}, u32[]{:S(2)}) async-start(bf16[32,96,128]{2,1,0:T(8,128)(2,1)} %shard_map.145), calls=%async_computation | async-start | bytes 1572864 | tf_op jit(solution)/shard_map/all_to_all | solution.py:482
  19.9 0.0 copy-start.8
  19.9 1.7 %copy-done.8 = bf16[316,2,2048]{2,1,0:T(2,128)(2,1)S(1)} copy-done((bf16[316,2,2048]{2,1,0:T(2,128)(2,1)S(1)}, bf16[316,2,2048]{2,1,0:T(2,128)(2,1)}, u32[]{:S(2)}) %copy-start.8) | copy-done | bytes 2588696
  21.6 1.1 %copy-done.9 = bf16[316,2,512]{2,1,0:T(2,128)(2,1)S(1)} copy-done((bf16[316,2,512]{2,1,0:T(2,128)(2,1)S(1)}, bf16[316,2,512]{2,1,0:T(2,128)(2,1)}, u32[]{:S(2)}) %copy-start.9) | copy-done | bytes 647192
  22.7 11.4 %shard_map.146 = (f32[32,128]{1,0:T(8,128)S(1)}, f32[16,128,1024]{2,1,0:T(8,128)S(1)}, f32[4160,128]{1,0:T(8,128)S(1)}) custom-call(bf16[32,128]{1,0:T(8,128)(2,1)S(1)} %collective-permute-done.lower_hbm, bf16[32,128]{1,0:T(8,128)(2,1)S(1)} %bitcast.25, bf16[32,128]{1,0:T(8,128)(2,1)S(1)} %collective-permute-done.1.upper_hbm, s32[16,27]{1,0:T(8,128)S(1)} %copy-done.14, ...), custom_call_target="tpu_custom_call" | custom-call | flops 10000000000 | bytes 20971520 | tf_op jit(solution)/shard_map/pallas_call | solution.py:489
  34.1 3.2 %copy-done.1 = f32[16,128,1024]{2,1,0:T(8,128)} copy-done((f32[16,128,1024]{2,1,0:T(8,128)}, f32[16,128,1024]{2,1,0:T(8,128)S(1)}, u32[]{:S(2)}) %copy-start.1) | copy-done | bytes 8388632
  37.3 1.4 %copy-done.4 = f32[4160,128]{1,0:T(8,128)} copy-done((f32[4160,128]{1,0:T(8,128)}, f32[4160,128]{1,0:T(8,128)S(1)}, u32[]{:S(2)}) %copy-start.4) | copy-done | bytes 2129944
  38.7 3.1 %all-to-all-done.arrived_ref = bf16[32,96,128]{2,1,0:T(8,128)(2,1)S(1)} async-done(((bf16[32,96,128]{2,1,0:T(8,128)(2,1)}), bf16[32,96,128]{2,1,0:T(8,128)(2,1)S(1)}, u32[]{:S(2)}, u32[]{:S(2)}) %all-to-all-start) | async-done | bytes 786464 | tf_op jit(solution)/shard_map/all_to_all | solution.py:482
  41.8 3.4 %copy-done.2 = f32[16,128,1024]{2,1,0:T(8,128)S(1)} copy-done((f32[16,128,1024]{2,1,0:T(8,128)S(1)}, f32[16,128,1024]{2,1,0:T(8,128)}, u32[]{:S(2)}) %copy-start.2) | copy-done | bytes 8388632
  45.2 2.2 %copy-done.3 = bf16[16,128,1024]{2,1,0:T(8,128)(2,1)S(1)} copy-done((bf16[16,128,1024]{2,1,0:T(8,128)(2,1)S(1)}, bf16[16,128,1024]{2,1,0:T(8,128)(2,1)}, u32[]{:S(2)}) %copy-start.3) | copy-done | bytes 4194328
  47.4 1.6 %copy-done.5 = f32[4160,128]{1,0:T(8,128)S(1)} copy-done((f32[4160,128]{1,0:T(8,128)S(1)}, f32[4160,128]{1,0:T(8,128)}, u32[]{:S(2)}) %copy-start.5) | copy-done | bytes 2129944
  49.0 5.7 %shard_map.147 = f32[32,128]{1,0:T(8,128)} custom-call(bf16[32,96,128]{2,1,0:T(8,128)(2,1)S(1)} %all-to-all-done.arrived_ref, f32[16,128,1024]{2,1,0:T(8,128)S(1)} %copy-done.2, f32[4160,128]{1,0:T(8,128)S(1)} %copy-done.5, f32[256,128]{1,0:T(8,128)S(1)} %bitcast.21, bf16[512,2048]{1,0:T(8,128)(2,1)S(1)} %copy-done, bf16[16,128,1024]{2,1,0:T(8,128)(2,1)S(1)} %copy-done.3, ...), custom_call_target="tpu_custom_call" | custom-call | flops 1000000000 | bytes 8388608 | tf_op jit(solution)/shard_map/pallas_call | solution.py:537
  (17 shorter events, 0.0 us)
Async XLA Ops:
  0.0 9.2 %collective-permute-start.1 = (bf16[32,128]{1,0:T(8,128)(2,1)}, bf16[32,128]{1,0:T(8,128)(2,1)S(1)}, u32[]{:S(2)}, u32[]{:S(2)}) collective-permute-start(bf16[32,128]{1,0:T(8,128)(2,1)} %bitcast.22), channel_id=1, source_target_pairs={{1,0},{2,1},{3,2},{4,3},{5,4},{6,5},{7,6},{8,7},{9,8},{10,9},{11,1... | collective-permute-start | bytes 24584 | tf_op jit(solution)/shard_map/ppermute | solution.py:35
  1.3 7.9 %collective-permute-start = (bf16[32,128]{1,0:T(8,128)(2,1)}, bf16[32,128]{1,0:T(8,128)(2,1)S(1)}, u32[]{:S(2)}, u32[]{:S(2)}) collective-permute-start(bf16[32,128]{1,0:T(8,128)(2,1)} %bitcast.23), channel_id=1, source_target_pairs={{0,1},{1,2},{2,3},{3,4},{4,5},{5,6},{6,7},{7,8},{8,9},{9,10},{10,1... | collective-permute-start | bytes 24584 | tf_op jit(solution)/shard_map/ppermute | solution.py:35
  4.3 15.5 %copy-start.7 = (bf16[16,2,128]{2,1,0:T(2,128)(2,1)S(1)}, bf16[16,2,128]{2,1,0:T(2,128)(2,1)}, u32[]{:S(2)}) copy-start(bf16[16,2,128]{2,1,0:T(2,128)(2,1)} %param.15) | copy-start | bytes 24580
  4.3 15.5 %copy-start.10 = (s32[16,189]{1,0:T(8,128)S(1)}, s32[16,189]{1,0:T(8,128)}, u32[]{:S(2)}) copy-start(s32[16,189]{1,0:T(8,128)} %slot_hbm.1) | copy-start | bytes 36292
  4.3 15.5 %copy-start.11 = (s32[16,189]{1,0:T(8,128)S(1)}, s32[16,189]{1,0:T(8,128)}, u32[]{:S(2)}) copy-start(s32[16,189]{1,0:T(8,128)} %type_hbm.1) | copy-start | bytes 36292
  4.4 15.5 %copy-start.12 = (s32[16,189]{1,0:T(8,128)S(1)}, s32[16,189]{1,0:T(8,128)}, u32[]{:S(2)}) copy-start(s32[16,189]{1,0:T(8,128)} %par_far_hbm.1) | copy-start | bytes 36292
  4.4 15.5 %copy-start.13 = (s32[16,189]{1,0:T(8,128)S(1)}, s32[16,189]{1,0:T(8,128)}, u32[]{:S(2)}) copy-start(s32[16,189]{1,0:T(8,128)} %par_type_hbm.1) | copy-start | bytes 36292
  4.4 15.5 %copy-start.14 = (s32[16,27]{1,0:T(8,128)S(1)}, s32[16,27]{1,0:T(8,128)}, u32[]{:S(2)}) copy-start(s32[16,27]{1,0:T(8,128)} %near_src_hbm.1) | copy-start | bytes 5188
  4.4 15.5 %copy-start.15 = (s32[16,27]{1,0:T(8,128)S(1)}, s32[16,27]{1,0:T(8,128)}, u32[]{:S(2)}) copy-start(s32[16,27]{1,0:T(8,128)} %near_tile_hbm.1) | copy-start | bytes 5188
  9.2 32.6 %all-to-all-start = ((bf16[32,96,128]{2,1,0:T(8,128)(2,1)}), bf16[32,96,128]{2,1,0:T(8,128)(2,1)S(1)}, u32[]{:S(2)}, u32[]{:S(2)}) async-start(bf16[32,96,128]{2,1,0:T(8,128)(2,1)} %shard_map.145), calls=%async_computation | async-start | bytes 1572864 | tf_op jit(solution)/shard_map/all_to_all | solution.py:482
  19.9 1.7 %copy-start.8 = (bf16[316,2,2048]{2,1,0:T(2,128)(2,1)S(1)}, bf16[316,2,2048]{2,1,0:T(2,128)(2,1)}, u32[]{:S(2)}) copy-start(bf16[316,2,2048]{2,1,0:T(2,128)(2,1)} %param.29) | copy-start | bytes 7766020
  21.6 1.1 %copy-start.9 = (bf16[316,2,512]{2,1,0:T(2,128)(2,1)S(1)}, bf16[316,2,512]{2,1,0:T(2,128)(2,1)}, u32[]{:S(2)}) copy-start(bf16[316,2,512]{2,1,0:T(2,128)(2,1)} %param.24) | copy-start | bytes 1941508
  22.7 19.1 %copy-start = (bf16[512,2048]{1,0:T(8,128)(2,1)S(1)}, bf16[512,2048]{1,0:T(8,128)(2,1)}, u32[]{:S(2)}) copy-start(bf16[512,2048]{1,0:T(8,128)(2,1)} %interp_hbm.3) | copy-start | bytes 6291460
  22.7 19.1 %copy-start.6 = (f32[8,2,2048]{2,1,0:T(2,128)S(1)}, f32[8,2,2048]{2,1,0:T(2,128)}, u32[]{:S(2)}) copy-start(f32[8,2,2048]{2,1,0:T(2,128)} %param.26) | copy-start | bytes 393220
  34.1 3.2 %copy-start.1 = (f32[16,128,1024]{2,1,0:T(8,128)}, f32[16,128,1024]{2,1,0:T(8,128)S(1)}, u32[]{:S(2)}) copy-start(f32[16,128,1024]{2,1,0:T(8,128)S(1)} %get-tuple-element.14.d_lo_ref) | copy-start | bytes 25165828
  37.3 1.4 %copy-start.4 = (f32[4160,128]{1,0:T(8,128)}, f32[4160,128]{1,0:T(8,128)S(1)}, u32[]{:S(2)}) copy-start(f32[4160,128]{1,0:T(8,128)S(1)} %get-tuple-element.15.d_hi_ref) | copy-start | bytes 6389764
  41.8 3.4 %copy-start.2 = (f32[16,128,1024]{2,1,0:T(8,128)S(1)}, f32[16,128,1024]{2,1,0:T(8,128)}, u32[]{:S(2)}) copy-start(f32[16,128,1024]{2,1,0:T(8,128)} %copy-done.1) | copy-start | bytes 25165828
  45.2 2.2 %copy-start.3 = (bf16[16,128,1024]{2,1,0:T(8,128)(2,1)S(1)}, bf16[16,128,1024]{2,1,0:T(8,128)(2,1)}, u32[]{:S(2)}) copy-start(bf16[16,128,1024]{2,1,0:T(8,128)(2,1)} %receive_ref.1) | copy-start | bytes 12582916
  47.4 1.6 %copy-start.5 = (f32[4160,128]{1,0:T(8,128)S(1)}, f32[4160,128]{1,0:T(8,128)}, u32[]{:S(2)}) copy-start(f32[4160,128]{1,0:T(8,128)} %copy-done.4) | copy-start | bytes 6389764

commit v3 on v2

--- a/solution.py
+++ b/solution.py
@@ -44,6 +44,7 @@
 
 
 def radiate_kernel(
+    group,
     dens_hbm,
     radiate_ref,
     send_hbm,
@@ -105,6 +106,7 @@
     wide = dot_nn(jnp.concatenate([re_part, im_part], 0), interp_ref[...])
     hi_chunks = wide.shape[1] // LANE
     parents = boxes // 8
+    share = hi_chunks // group
     for r in range(hi_chunks):
         cols = slice(r * LANE, (r + 1) * LANE)
         s_re = shift_ref[pl.ds(2 * r, 8, stride=2 * hi_chunks), :]
@@ -112,13 +114,12 @@
         for p in range(parents):
             w_re = wide[p * 8 : (p + 1) * 8, cols]
             w_im = wide[boxes + p * 8 : boxes + (p + 1) * 8, cols]
-            row = p * 2 * hi_chunks + r
+            row = ((r // share) * parents + p) * 2 * share + r % share
             parent[row : row + 1] = jnp.sum(w_re * s_re - w_im * s_im, 0, keepdims=True)
-            row += hi_chunks
+            row += share
             parent[row : row + 1] = jnp.sum(w_re * s_im + w_im * s_re, 0, keepdims=True)
     slots, devices = send_ref.shape
-    hi_rows = parents * 2 * hi_chunks
-    parent_block = parent[...].astype(BF16)
+    hi_rows = parents * 2 * share
 
     def fill(d, carry):
         for k in range(slots // 2):
@@ -126,10 +127,110 @@
                 table[pl.ds(pl.multiple_of(send_ref[2 * k + h, d] * 8, 8), 8), :] for h in range(2)
             ]
             out_ref[d, 16 * k : 16 * (k + 1)] = jnp.concatenate(pair, 0).astype(BF16)
-        out_ref[d, 8 * slots : 8 * slots + hi_rows] = parent_block
+        member = pl.multiple_of(lax.rem(d, group) * hi_rows, 8)
+        out_ref[d, 8 * slots : 8 * slots + hi_rows] = parent[pl.ds(member, hi_rows)].astype(BF16)
         return carry
 
     lax.fori_loop(0, devices, fill, 0)
+
+
+def tally(index, source_row, type_row, sources, types):
+    source = index[pl.ds(source_row, 1), :]
+    kind = index[pl.ds(type_row, 1), :]
+    faces = index.shape[1]
+    by_source = jnp.where(iota((sources, faces), 0) == source, 1.0, 0.0).astype(BF16)
+    by_type = jnp.where(iota((types, faces), 0) == kind, 1.0, 0.0).astype(BF16)
+    return dot_nt(by_source, by_type).astype(BF16)
+
+
+def parent_operator_kernel(
+    types,
+    group,
+    par_far_hbm,
+    par_type_hbm,
+    op_hbm,
+    d_ref,
+    par_far_ref,
+    par_type_ref,
+    op_ref,
+    index,
+    wide,
+    op,
+    extra,
+):
+    others = fetch(
+        [(par_far_hbm, par_far_ref), (par_type_hbm, par_type_ref), (op_hbm, op_ref)], extra
+    )
+    rows, far = par_far_ref.shape
+    lines = op_ref.shape[0] // types
+    share = lines // (2 * group)
+    type_pad = op.shape[0]
+    samp = lax.axis_index("samp")
+    member = lax.rem(samp, group)
+    first_parent = (samp - member) * (d_ref.shape[0] // group)
+    place = member * (2 * share)
+    base = place // 16 * 16
+    index[...] = jnp.full(index.shape, -1, jnp.int32)
+    wide[types * 16 : type_pad * 16] = jnp.zeros(((type_pad - types) * 16, LANE), F32)
+    others[0].wait()
+    others[1].wait()
+    index[0:rows, 0:far] = par_far_ref[...]
+    index[rows : 2 * rows, 0:far] = par_type_ref[...]
+    others[2].wait()
+
+    def widen(t, carry):
+        source = pl.ds(pl.multiple_of(t * lines + base, 16), 16)
+        wide[pl.ds(pl.multiple_of(t * 16, 16), 16)] = op_ref[source].astype(F32)
+        return carry
+
+    lax.fori_loop(0, types, widen, 0, unroll=4)
+    for c in range(2):
+        for k in range(share):
+            col = (c * share + k) * LANE
+            start = place - base + 2 * k + c
+            op[:, col : col + LANE] = wide[pl.ds(start, type_pad, stride=16), :].astype(BF16)
+    parents, sources, _ = d_ref.shape
+    per_step = 4
+
+    def step_parents(step, carry):
+        start = step * per_step
+        counts = jnp.concatenate(
+            [
+                tally(
+                    index,
+                    first_parent + start + k,
+                    rows + first_parent + start + k,
+                    sources,
+                    type_pad,
+                )
+                for k in range(per_step)
+            ],
+            0,
+        )
+        d_ref[pl.ds(start, per_step)] = dot_nn(counts, op[...]).reshape(
+            per_step, sources, 2 * share * LANE
+        )
+        return carry
+
+    lax.fori_loop(0, parents // per_step, step_parents, 0)
+
+
+def parent_kernel(lo_lines, arrived_ref, d_ref, out_ref, wide):
+    parents, sources, width = d_ref.shape
+    share = width // (2 * LANE)
+    rows = out_ref.shape[1]
+    wide[...] = arrived_ref[:, lo_lines:, :].astype(F32).reshape(wide.shape)
+    for k in range(share):
+        first = wide[pl.ds(k, sources, stride=2 * share), :]
+        second = wide[pl.ds(share + k, sources, stride=2 * share), :]
+        for p in range(parents):
+            o_re = d_ref[p, :, k * LANE : (k + 1) * LANE]
+            o_im = d_ref[p, :, (share + k) * LANE : (share + k + 1) * LANE]
+            row = p * 2 * share + k
+            to, row = row // rows, row % rows
+            out_ref[to, row : row + 1] = jnp.sum(o_re * first - o_im * second, 0, keepdims=True)
+            row += share
+            out_ref[to, row : row + 1] = jnp.sum(o_re * second + o_im * first, 0, keepdims=True)
 
 
 def middle_kernel(
@@ -144,12 +245,9 @@
     slot_hbm,
     type_hbm,
     op_lo_hbm,
-    par_far_hbm,
-    par_type_hbm,
-    op_hi_hbm,
+    arrived_ref,
     near_ref,
-    d_lo_ref,
-    d_hi_ref,
+    incoming_ref,
     tiles,
     halo,
     near_src_ref,
@@ -157,9 +255,6 @@
     slot_ref,
     type_ref,
     op_lo_ref,
-    par_far_ref,
-    par_type_ref,
-    op_hi,
     dens3,
     left,
     right,
@@ -168,6 +263,8 @@
     index,
     wide_op,
     op_lo,
+    summed,
+    slots,
     sems,
     extra,
 ):
@@ -185,9 +282,6 @@
             (lower_hbm, halo.at[0]),
             (dens_hbm, halo.at[1]),
             (upper_hbm, halo.at[2]),
-            (par_far_hbm, par_far_ref),
-            (par_type_hbm, par_type_ref),
-            (op_hi_hbm, op_hi),
         ],
         extra,
     )
@@ -199,7 +293,6 @@
     for step in range(steps):
         tile_copy(step).start()
     position = lax.axis_index("box") * lax.axis_size("samp") + lax.axis_index("samp")
-    d_hi_ref[...] = jnp.zeros(d_hi_ref.shape, F32)
     acc[...] = jnp.zeros(acc.shape, F32)
     index[...] = jnp.full(index.shape, -1, jnp.int32)
     left[...] = jnp.zeros(left.shape, F32)
@@ -243,30 +336,21 @@
     right[pl.ds(0, 3 * boxes, stride=8), :] = -second
     right[pl.ds(1, 3 * boxes, stride=8), :] = first
 
-    slot_total = d_lo_ref.shape[1]
+    lo_lines = slots.shape[0] // arrived_ref.shape[0]
+    slots[...] = arrived_ref[:, :lo_lines, :].astype(F32).reshape(slots.shape)
+    slot_total = slots.shape[0] // (2 * chunks)
     per_boxes = boxes // steps
-    faces = index.shape[1]
-    parents = boxes // 8
-    par_rows = d_hi_ref.shape[0] // parents
-    hi_lines = op_hi.shape[0] // types
-    empty = par_rows // hi_lines - 1
-    own = lax.axis_index("samp") * parents
-    far_step = -(-far // steps)
-
-    def counts(g):
-        source = index[pl.ds(g, 1), :]
-        kind = index[pl.ds(boxes + g, 1), :]
-        by_source = jnp.where(iota((slot_total, faces), 0) == source, 1.0, 0.0).astype(BF16)
-        by_type = jnp.where(iota((type_pad, faces), 0) == kind, 1.0, 0.0).astype(BF16)
-        return dot_nt(by_source, by_type).astype(BF16)
 
     def step_boxes(step, carry):
         start = step * per_boxes
-        tally = jnp.concatenate([counts(start + k) for k in range(per_boxes)], 0)
-        summed = dot_nn(tally, op_lo[...]).astype(d_lo_ref.dtype)
-        d_lo_ref[pl.ds(start, per_boxes)] = summed.reshape(
-            per_boxes, slot_total, 2 * chunks * LANE
+        counts = jnp.concatenate(
+            [
+                tally(index, start + k, boxes + start + k, slot_total, type_pad)
+                for k in range(per_boxes)
+            ],
+            0,
         )
+        summed[...] = dot_nn(counts, op_lo[...])
         tile_copy(step).wait()
         for pair in range(per_step // 2):
             tile = step * per_step + 2 * pair
@@ -287,16 +371,20 @@
                 acc[owners[h]] = (
                     acc[owners[h]] + product[8 * h : 8 * (h + 1), h * LANE : (h + 1) * LANE]
                 )
-        for e in range(far_step):
-            f = step * far_step + e
-            inside = f < far
-            f = jnp.minimum(f, far - 1)
-            for p in range(parents):
-                source = jnp.where(inside, par_far_ref[own + p, f], empty)
-                kind = par_type_ref[own + p, f]
-                at = pl.ds(pl.multiple_of(p * par_rows + source * hi_lines, hi_lines), hi_lines)
-                term = op_hi[pl.ds(pl.multiple_of(kind * hi_lines, hi_lines), hi_lines)]
-                d_hi_ref[at] = d_hi_ref[at] + term.astype(F32)
+        for r in range(chunks):
+            cols = slice(r * LANE, (r + 1) * LANE)
+            first = slots[pl.ds(r, slot_total, stride=2 * chunks), :]
+            second = slots[pl.ds(chunks + r, slot_total, stride=2 * chunks), :]
+            for k in range(per_boxes):
+                part = slice(k * slot_total, (k + 1) * slot_total)
+                o_re = summed[part, cols]
+                o_im = summed[part, (chunks + r) * LANE : (chunks + r + 1) * LANE]
+                incoming_ref[start + k, r : r + 1] = jnp.sum(
+                    o_re * first - o_im * second, 0, keepdims=True
+                )
+                incoming_ref[boxes + start + k, r : r + 1] = jnp.sum(
+                    o_re * second + o_im * first, 0, keepdims=True
+                )
         return carry
 
     lax.fori_loop(0, steps, step_boxes, 0)
@@ -306,9 +394,8 @@
 
 
 def last_kernel(
-    arrived_ref,
-    d_lo_ref,
-    d_hi_ref,
+    parent_ref,
+    incoming_ref,
     shift_hbm,
     interp_hbm,
     receive_ref,
@@ -317,10 +404,7 @@
     receive,
     shift_ref,
     interp_ref,
-    slots,
-    upward,
     down,
-    incoming,
     blend,
     sems,
     extra,
@@ -334,61 +418,26 @@
         part = pl.ds(step * per_step, per_step)
         copies.append(pltpu.make_async_copy(receive_ref.at[part], receive.at[part], sems.at[step]))
         copies[-1].start()
-    devices, lines, _ = arrived_ref.shape
     own_parents = boxes // 8
-    slot_total = d_lo_ref.shape[1]
-    chunks = d_lo_ref.shape[2] // (2 * LANE)
-    lo_lines = slot_total // devices * 2 * chunks
-    hi_lines = (lines - lo_lines) // own_parents
-    hi_chunks = hi_lines // 2
-    par_rows = d_hi_ref.shape[0] // own_parents
-    slots[...] = arrived_ref[:, :lo_lines, :].astype(F32).reshape(devices * lo_lines, LANE)
-
-    def gather(device, sums):
-        for q in range(own_parents):
-            line = lo_lines + q * hi_lines
-            first = arrived_ref[device, line : line + hi_chunks].astype(F32)
-            second = arrived_ref[device, line + hi_chunks : line + hi_lines].astype(F32)
-            new = []
-            for p in range(own_parents):
-                row = p * par_rows + (device * own_parents + q) * hi_lines
-                o_re = d_hi_ref[pl.ds(row, hi_chunks, stride=2), :]
-                o_im = d_hi_ref[pl.ds(row + 1, hi_chunks, stride=2), :]
-                new.append(sums[2 * p] + (o_re * first - o_im * second))
-                new.append(sums[2 * p + 1] + (o_re * second + o_im * first))
-            sums = tuple(new)
-        return sums
-
-    zero = jnp.zeros((hi_chunks, LANE), F32)
-    sums = lax.fori_loop(0, devices, gather, (zero,) * (2 * own_parents), unroll=4)
-    for k in range(2 * own_parents):
-        upward[k * hi_chunks : (k + 1) * hi_chunks] = sums[k]
+    hi_chunks = down.shape[1] // LANE
+    chunks = incoming_ref.shape[1]
+    share = hi_chunks // parent_ref.shape[0]
     others[0].wait()
     for r in range(hi_chunks):
         s_re = shift_ref[pl.ds(2 * r, 8, stride=2 * hi_chunks), :]
         s_im = shift_ref[pl.ds(2 * r + 1, 8, stride=2 * hi_chunks), :]
         re_rows, im_rows = [], []
         for p in range(own_parents):
-            row = 2 * p * hi_chunks + r
-            t_re = upward[row : row + 1]
-            t_im = upward[row + hi_chunks : row + hi_chunks + 1]
+            row = p * 2 * share + r % share
+            t_re = parent_ref[r // share, row : row + 1]
+            t_im = parent_ref[r // share, row + share : row + share + 1]
             re_rows.append(s_re * t_re + s_im * t_im)
             im_rows.append(s_re * t_im - s_im * t_re)
         cols = slice(r * LANE, (r + 1) * LANE)
         down[:, cols] = jnp.concatenate(re_rows + im_rows, 0).astype(BF16)
-    for r in range(chunks):
-        first = slots[pl.ds(r, slot_total, stride=2 * chunks), :]
-        second = slots[pl.ds(chunks + r, slot_total, stride=2 * chunks), :]
-        for g in range(boxes):
-            o_re = d_lo_ref[g, :, r * LANE : (r + 1) * LANE].astype(F32)
-            o_im = d_lo_ref[g, :, (chunks + r) * LANE : (chunks + r + 1) * LANE].astype(F32)
-            cols = slice(r * LANE, (r + 1) * LANE)
-            incoming[g : g + 1, cols] = jnp.sum(o_re * first - o_im * second, 0, keepdims=True)
-            incoming[boxes + g : boxes + g + 1, cols] = jnp.sum(
-                o_re * second + o_im * first, 0, keepdims=True
-            )
     others[1].wait()
-    total = incoming[...] + dot_nt(down[...], interp_ref[...])
+    total = jnp.concatenate([incoming_ref[:, r, :] for r in range(chunks)], 1)
+    total = total + dot_nt(down[...], interp_ref[...])
     total = total.astype(BF16).astype(F32)
     for r in range(chunks):
         re_part = total[:boxes, r * LANE : (r + 1) * LANE]
@@ -450,16 +499,20 @@
     slot_total = devices * slots
     par_total = devices * parents
     type_pad = -(-types // 8) * 8
-    lines = slots * 2 * width_lo // LANE + parents * 2 * width_hi // LANE
-    held = F32 if slot_total <= 128 else BF16
+    samp_count = lax.axis_size("samp")
+    group = min(samp_count, 8)
+    share = width_hi // LANE // group
+    lo_lines = slots * 2 * width_lo // LANE
+    hi_lines = parents * 2 * share
+    lines = lo_lines + hi_lines
+    members = None
+    if group < samp_count:
+        members = [list(range(k, k + group)) for k in range(0, samp_count, group)]
     rows = density.reshape(boxes * 2, panels)
-    lower = shifted(rows, ("box", "samp"), 1)
-    upper = shifted(rows, ("box", "samp"), -1)
     shift_rows = tiled_rows(shifts)
-    mid = rows
     send = send_box[0].T
     outgoing = pl.pallas_call(
-        radiate_kernel,
+        functools.partial(radiate_kernel, group),
         out_shape=jax.ShapeDtypeStruct((devices, lines, LANE), BF16),
         in_specs=[HBM_SPEC] * 5,
         out_specs=VMEM_SPEC,
@@ -478,23 +531,53 @@
         compiler_params=pltpu.CompilerParams(vmem_limit_bytes=12 * MIB),
         cost_estimate=pl.CostEstimate(flops=10**9, bytes_accessed=8 * MIB, transcendentals=0),
     )(*(in_hbm(x) for x in (rows, radiate, send, interp_matrix, shift_rows)))
-    outgoing, lower, upper = lax.optimization_barrier((outgoing, lower, upper))
+    outgoing, near_rows = lax.optimization_barrier((outgoing, rows))
     arrived = lax.all_to_all(outgoing, ("box", "samp"), split_axis=0, concat_axis=0, tiled=True)
+    lower = shifted(near_rows, ("box", "samp"), 1)
+    upper = shifted(near_rows, ("box", "samp"), -1)
     tile_count = near_tiles.shape[0]
     far = far_type.shape
-    par_shape = par_far.shape
     op_hi_rows = tiled_rows(trans_hi)
     op_lo_rows = tiled_rows(trans_lo)
-    hi_lines = 2 * width_hi // LANE
-    near, d_lo, d_hi = pl.pallas_call(
+    d_hi = pl.pallas_call(
+        functools.partial(parent_operator_kernel, types, group),
+        out_shape=pltpu.VMEM((parents * group, par_total, 2 * share * LANE), F32),
+        in_specs=[HBM_SPEC] * 3,
+        out_specs=VMEM_SPEC,
+        scratch_shapes=[
+            pltpu.VMEM(par_far.shape, jnp.int32),
+            pltpu.VMEM(par_far.shape, jnp.int32),
+            pltpu.VMEM(op_hi_rows.shape, BF16),
+            pltpu.VMEM((2 * par_far.shape[0], 2 * LANE), jnp.int32),
+            pltpu.VMEM((type_pad * 16, LANE), F32),
+            pltpu.VMEM((type_pad, 2 * share * LANE), BF16),
+            pltpu.SemaphoreType.DMA((3,)),
+        ],
+        compiler_params=pltpu.CompilerParams(vmem_limit_bytes=12 * MIB),
+        cost_estimate=pl.CostEstimate(flops=10**9, bytes_accessed=8 * MIB, transcendentals=0),
+    )(*(in_hbm(x) for x in (par_far, par_type, op_hi_rows)))
+    above = pl.pallas_call(
+        functools.partial(parent_kernel, lo_lines),
+        out_shape=jax.ShapeDtypeStruct((group, hi_lines, LANE), F32),
+        in_specs=[VMEM_SPEC] * 2,
+        out_specs=VMEM_SPEC,
+        scratch_shapes=[pltpu.VMEM((devices * hi_lines, LANE), F32)],
+        compiler_params=pltpu.CompilerParams(vmem_limit_bytes=4 * MIB),
+        cost_estimate=pl.CostEstimate(flops=10**8, bytes_accessed=MIB, transcendentals=0),
+    )(arrived, in_vmem(d_hi))
+    above, lower, upper = lax.optimization_barrier((above, lower, upper))
+    own_above = lax.all_to_all(
+        above, "samp", split_axis=0, concat_axis=0, axis_index_groups=members, tiled=True
+    )
+    steps = 4
+    near, incoming = pl.pallas_call(
         functools.partial(middle_kernel, types, boxes * devices),
         out_shape=(
-            pltpu.VMEM((2 * boxes, panels), F32),
-            pltpu.VMEM((boxes, slot_total, 2 * width_lo), held),
-            pltpu.VMEM((parents * (par_total + 1) * hi_lines, LANE), F32),
+            jax.ShapeDtypeStruct((2 * boxes, panels), F32),
+            jax.ShapeDtypeStruct((2 * boxes, width_lo // LANE, LANE), F32),
         ),
-        in_specs=[ANY_SPEC, HBM_SPEC, ANY_SPEC] + [HBM_SPEC] * 9,
-        out_specs=(VMEM_SPEC,) * 3,
+        in_specs=[ANY_SPEC, HBM_SPEC, ANY_SPEC] + [HBM_SPEC] * 6 + [VMEM_SPEC],
+        out_specs=(VMEM_SPEC,) * 2,
         scratch_shapes=[
             pltpu.VMEM(near_tiles.shape, BF16),
             pltpu.VMEM((3, 2 * boxes, panels), BF16),
@@ -503,9 +586,6 @@
             pltpu.VMEM(far, jnp.int32),
             pltpu.VMEM(far, jnp.int32),
             pltpu.VMEM(op_lo_rows.shape, BF16),
-            pltpu.SMEM(par_shape, jnp.int32),
-            pltpu.SMEM(par_shape, jnp.int32),
-            pltpu.VMEM(op_hi_rows.shape, BF16),
             pltpu.VMEM((6 * boxes, panels), F32),
             pltpu.VMEM((3 * boxes * 8, LANE), F32),
             pltpu.VMEM((3 * boxes * 8, LANE), F32),
@@ -514,46 +594,47 @@
             pltpu.VMEM((2 * boxes, 2 * LANE), jnp.int32),
             pltpu.VMEM((type_pad * 2 * width_lo // LANE, LANE), F32),
             pltpu.VMEM((type_pad, 2 * width_lo), BF16),
-            pltpu.SemaphoreType.DMA((4,)),
-            pltpu.SemaphoreType.DMA((11,)),
+            pltpu.VMEM((boxes // steps * slot_total, 2 * width_lo), F32),
+            pltpu.VMEM((devices * lo_lines, LANE), F32),
+            pltpu.SemaphoreType.DMA((steps,)),
+            pltpu.SemaphoreType.DMA((8,)),
         ],
-        compiler_params=pltpu.CompilerParams(vmem_limit_bytes=28 * MIB),
+        compiler_params=pltpu.CompilerParams(vmem_limit_bytes=(24 if slot_total <= 128 else 40) * MIB),
         cost_estimate=pl.CostEstimate(flops=10**10, bytes_accessed=20 * MIB, transcendentals=0),
     )(
         lower,
-        mid,
+        in_hbm(rows),
         upper,
-        near_src,
-        near_tile,
-        near_tiles,
-        distant_pattern_slot,
-        far_type,
-        op_lo_rows,
-        par_far,
-        par_type,
-        op_hi_rows,
+        *(
+            in_hbm(x)
+            for x in (
+                near_src,
+                near_tile,
+                near_tiles,
+                distant_pattern_slot,
+                far_type,
+                op_lo_rows,
+            )
+        ),
+        arrived,
     )
-    lo_lines = slots * 2 * width_lo // LANE
     field = pl.pallas_call(
         last_kernel,
         out_shape=jax.ShapeDtypeStruct((2 * boxes, panels), F32),
-        in_specs=[VMEM_SPEC] * 3 + [HBM_SPEC] * 3 + [VMEM_SPEC],
+        in_specs=[VMEM_SPEC] * 2 + [HBM_SPEC] * 3 + [VMEM_SPEC],
         out_specs=VMEM_SPEC,
         scratch_shapes=[
             pltpu.VMEM(receive.shape, BF16),
             pltpu.VMEM(shift_rows.shape, F32),
             pltpu.VMEM(interp_matrix.shape, BF16),
-            pltpu.VMEM((devices * lo_lines, LANE), F32),
-            pltpu.VMEM((parents * hi_lines, LANE), F32),
             pltpu.VMEM((2 * boxes, width_hi), BF16),
-            pltpu.VMEM((2 * boxes, width_lo), F32),
             pltpu.VMEM((2 * boxes, 2 * width_lo // LANE, LANE), F32),
             pltpu.SemaphoreType.DMA((boxes // 4,)),
             pltpu.SemaphoreType.DMA((2,)),
         ],
         compiler_params=pltpu.CompilerParams(vmem_limit_bytes=12 * MIB),
         cost_estimate=pl.CostEstimate(flops=10**9, bytes_accessed=8 * MIB, transcendentals=0),
-    )(arrived, in_vmem(d_lo), in_vmem(d_hi), shift_rows, interp_matrix, receive, near)
+    )(own_above, incoming, shift_rows, interp_matrix, receive, near)
     return field.reshape(boxes, 2, panels)
 
 

time: 55.1 us -> 48.5 us (0.88)
  the two profiles are of different devices: /device:TPU:0 before, /device:TPU:13 now
where the time goes in v3:
time: 48.5 us; the launch traced here: 48.1 us
  Pallas kernels  26.5 us (55%)
  starting transfers between devices  19.3 us (40%)
  local copies, waits for them, and re-layouts  2.19 us (5%)
    pallas_call x1, Pallas kernels, on_device(): pl.pallas_call(functools.partial(middle_kernel, types, boxes * devices),...  12.2 us
    all_to_all x1, starting transfers between devices, on_device(): lax.all_to_all(above, 'samp', split_axis=0, concat_axis=0, axis_index_gro...  7.69 us
    all_to_all x1, starting transfers between devices, on_device(): lax.all_to_all(outgoing, ('box', 'samp'), split_axis=0, concat_axis=0, ti...  6.31 us
    ppermute x2, starting transfers between devices, shifted(): lax.ppermute(value, axis, [(source, source + steps) for source in range(f...  5.27 us
    pallas_call x1, Pallas kernels, on_device(): pl.pallas_call(functools.partial(parent_operator_kernel, types, group), o...  5 us
    pallas_call x1, Pallas kernels, on_device(): pl.pallas_call(functools.partial(radiate_kernel, group), out_shape=jax.Sh...  4.65 us
    pallas_call x1, Pallas kernels, on_device(): pl.pallas_call(last_kernel, out_shape=jax.ShapeDtypeStruct((2 * boxes, pa...  3.77 us
    unnamed x8, local copies, waits for them, and re-layouts  2.19 us
  transfers between devices with their start and end apart: 4, of which 0 were waited for; matrix products, arithmetic and copies ran while one was open for 0% of the time, Pallas kernels for 38%

profile of v3, /device:TPU:13, one launch (start us, length us, event | category | flops | bytes accessed | tf_op | source)
XLA Modules:
  0.0 48.1 jit_solution(9568453709992005446)
XLA Ops:
  0.0 0.0 copy-start.3
  0.0 4.7 %shard_map.145 = bf16[32,40,128]{2,1,0:T(8,128)(2,1)} custom-call(bf16[32,128]{1,0:T(8,128)(2,1)} %bitcast.23, bf16[16,128,1024]{2,1,0:T(8,128)(2,1)} %radiate_ref.1, s32[4,32]{1,0:T(4,128)} %bitcast.27, bf16[512,2048]{1,0:T(8,128)(2,1)} %interp_hbm.3, f32[256,128]{1,0:T(8,128)} %bitcast.20), custom_call_target="tpu_custom_call" | custom-call | flops 1000000000 | bytes 8388608 | tf_op jit(solution)/shard_map/pallas_call | solution.py:514
  4.7 6.3 %all-to-all-start = ((bf16[32,40,128]{2,1,0:T(8,128)(2,1)}), bf16[32,40,128]{2,1,0:T(8,128)(2,1)S(1)}, u32[]{:S(2)}, u32[]{:S(2)}) async-start(bf16[32,40,128]{2,1,0:T(8,128)(2,1)} %shard_map.145), calls=%async_computation | async-start | bytes 655360 | tf_op jit(solution)/shard_map/all_to_all | solution.py:535
  11.0 0.0 copy-done.3
  11.0 3.4 %collective-permute-start = (bf16[32,128]{1,0:T(8,128)(2,1)S(1)}, bf16[32,128]{1,0:T(8,128)(2,1)S(1)}, u32[]{:S(2)}, u32[]{:S(2)}) collective-permute-start(bf16[32,128]{1,0:T(8,128)(2,1)S(1)} %bitcast.25), channel_id=1, source_target_pairs={{0,1},{1,2},{2,3},{3,4},{4,5},{5,6},{6,7},{7,8},{8,9},{9,10},{10,1... | collective-permute-start | bytes 24584 | tf_op jit(solution)/shard_map/ppermute | solution.py:35
  14.3 1.9 %collective-permute-start.1 = (bf16[32,128]{1,0:T(8,128)(2,1)S(1)}, bf16[32,128]{1,0:T(8,128)(2,1)S(1)}, u32[]{:S(2)}, u32[]{:S(2)}) collective-permute-start(bf16[32,128]{1,0:T(8,128)(2,1)S(1)} %bitcast.26), channel_id=1, source_target_pairs={{1,0},{2,1},{3,2},{4,3},{5,4},{6,5},{7,6},{8,7},{9,8},{10,9},{11,1... | collective-permute-start | bytes 24584 | tf_op jit(solution)/shard_map/ppermute | solution.py:35
  16.3 5.0 %shard_map.146.d_ref = f32[16,64,512]{2,1,0:T(8,128)S(1)} custom-call(s32[16,189]{1,0:T(8,128)} %par_far_hbm.1, s32[16,189]{1,0:T(8,128)} %par_type_hbm.1, bf16[10112,128]{1,0:T(8,128)(2,1)} %bitcast.22), custom_call_target="tpu_custom_call" | custom-call | flops 1000000000 | bytes 8388608 | tf_op jit(solution)/shard_map/pallas_call | solution.py:542
  21.3 0.0 all-to-all-done.arrived_ref
  21.3 1.0 %shard_map.147 = f32[8,8,128]{2,1,0:T(8,128)} custom-call(bf16[32,40,128]{2,1,0:T(8,128)(2,1)S(1)} %all-to-all-done.arrived_ref, f32[16,64,512]{2,1,0:T(8,128)S(1)} %shard_map.146.d_ref), custom_call_target="tpu_custom_call" | custom-call | flops 100000000 | bytes 1048576 | tf_op jit(solution)/shard_map/pallas_call | solution.py:559
  22.3 0.0 collective-permute-done.lower_hbm
  22.3 0.0 collective-permute-done.1.upper_hbm
  22.3 7.7 %all-to-all-start.1 = ((f32[8,8,128]{2,1,0:T(8,128)}), f32[8,8,128]{2,1,0:T(8,128)S(1)}, u32[]{:S(2)}, u32[]{:S(2)}) async-start(f32[8,8,128]{2,1,0:T(8,128)} %shard_map.147), calls=%async_computation.1 | async-start | bytes 65536 | tf_op jit(solution)/shard_map/all_to_all | solution.py:569
  30.0 0.0 copy-start
  30.0 0.0 copy-start.2
  30.0 12.2 %shard_map.148 = (f32[32,128]{1,0:T(8,128)S(1)}, f32[32,4,128]{2,1,0:T(4,128)S(1)}) custom-call(bf16[32,128]{1,0:T(8,128)(2,1)S(1)} %collective-permute-done.lower_hbm, bf16[32,128]{1,0:T(8,128)(2,1)} %bitcast.24, bf16[32,128]{1,0:T(8,128)(2,1)S(1)} %collective-permute-done.1.upper_hbm, s32[16,27]{1,0:T(8,128)} %near_src_hbm.1, s32[16,27]{1,0:T(8,128)} %near_tile_hbm.1, ...), custom_call_target="tpu_custom_call" | custom-call | flops 10000000000 | bytes 20971520 | tf_op jit(solution)/shard_map/pallas_call | solution.py:573
  42.1 0.0 all-to-all-done.1.parent_ref
  42.1 0.0 copy-done
  42.1 0.0 copy-done.2
  42.2 0.0 copy-start.1
  42.2 2.2 %copy-done.1 = bf16[16,128,1024]{2,1,0:T(8,128)(2,1)S(1)} copy-done((bf16[16,128,1024]{2,1,0:T(8,128)(2,1)S(1)}, bf16[16,128,1024]{2,1,0:T(8,128)(2,1)}, u32[]{:S(2)}) %copy-start.1) | copy-done | bytes 4194328
  44.3 3.8 %shard_map.149 = f32[32,128]{1,0:T(8,128)} custom-call(f32[8,8,128]{2,1,0:T(8,128)S(1)} %all-to-all-done.1.parent_ref, f32[32,4,128]{2,1,0:T(4,128)S(1)} %get-tuple-element.17.incoming_ref, f32[256,128]{1,0:T(8,128)S(1)} %bitcast.21, bf16[512,2048]{1,0:T(8,128)(2,1)S(1)} %copy-done, bf16[16,128,1024]{2,1,0:T(8,128)(2,1)S(1)} %copy-done.1, ...), custom_call_target="tpu_custom_call" | custom-call | flops 1000000000 | bytes 8388608 | tf_op jit(solution)/shard_map/pallas_call | solution.py:621
Async XLA Ops:
  0.0 11.0 %copy-start.3 = (bf16[16,2,128]{2,1,0:T(2,128)(2,1)S(1)}, bf16[16,2,128]{2,1,0:T(2,128)(2,1)}, u32[]{:S(2)}) copy-start(bf16[16,2,128]{2,1,0:T(2,128)(2,1)} %param.15) | copy-start | bytes 24580
  4.7 16.6 %all-to-all-start = ((bf16[32,40,128]{2,1,0:T(8,128)(2,1)}), bf16[32,40,128]{2,1,0:T(8,128)(2,1)S(1)}, u32[]{:S(2)}, u32[]{:S(2)}) async-start(bf16[32,40,128]{2,1,0:T(8,128)(2,1)} %shard_map.145), calls=%async_computation | async-start | bytes 655360 | tf_op jit(solution)/shard_map/all_to_all | solution.py:535
  11.0 11.3 %collective-permute-start = (bf16[32,128]{1,0:T(8,128)(2,1)S(1)}, bf16[32,128]{1,0:T(8,128)(2,1)S(1)}, u32[]{:S(2)}, u32[]{:S(2)}) collective-permute-start(bf16[32,128]{1,0:T(8,128)(2,1)S(1)} %bitcast.25), channel_id=1, source_target_pairs={{0,1},{1,2},{2,3},{3,4},{4,5},{5,6},{6,7},{7,8},{8,9},{9,10},{10,1... | collective-permute-start | bytes 24584 | tf_op jit(solution)/shard_map/ppermute | solution.py:35
  14.3 7.9 %collective-permute-start.1 = (bf16[32,128]{1,0:T(8,128)(2,1)S(1)}, bf16[32,128]{1,0:T(8,128)(2,1)S(1)}, u32[]{:S(2)}, u32[]{:S(2)}) collective-permute-start(bf16[32,128]{1,0:T(8,128)(2,1)S(1)} %bitcast.26), channel_id=1, source_target_pairs={{1,0},{2,1},{3,2},{4,3},{5,4},{6,5},{7,6},{8,7},{9,8},{10,9},{11,1... | collective-permute-start | bytes 24584 | tf_op jit(solution)/shard_map/ppermute | solution.py:35
  22.3 19.9 %all-to-all-start.1 = ((f32[8,8,128]{2,1,0:T(8,128)}), f32[8,8,128]{2,1,0:T(8,128)S(1)}, u32[]{:S(2)}, u32[]{:S(2)}) async-start(f32[8,8,128]{2,1,0:T(8,128)} %shard_map.147), calls=%async_computation.1 | async-start | bytes 65536 | tf_op jit(solution)/shard_map/all_to_all | solution.py:569
  30.0 12.2 %copy-start = (bf16[512,2048]{1,0:T(8,128)(2,1)S(1)}, bf16[512,2048]{1,0:T(8,128)(2,1)}, u32[]{:S(2)}) copy-start(bf16[512,2048]{1,0:T(8,128)(2,1)} %interp_hbm.3) | copy-start | bytes 6291460
  30.0 12.2 %copy-start.2 = (f32[8,2,2048]{2,1,0:T(2,128)S(1)}, f32[8,2,2048]{2,1,0:T(2,128)}, u32[]{:S(2)}) copy-start(f32[8,2,2048]{2,1,0:T(2,128)} %param.26) | copy-start | bytes 393220
  42.2 2.2 %copy-start.1 = (bf16[16,128,1024]{2,1,0:T(8,128)(2,1)S(1)}, bf16[16,128,1024]{2,1,0:T(8,128)(2,1)}, u32[]{:S(2)}) copy-start(bf16[16,128,1024]{2,1,0:T(8,128)(2,1)} %receive_ref.1) | copy-start | bytes 12582916

commit v4 on v3

--- a/solution.py
+++ b/solution.py
@@ -29,10 +29,12 @@
     return lax.dot_general(lhs, rhs, (((1,), (1,)), ((), ())), preferred_element_type=F32)
 
 
-def shifted(value, axis, steps):
-    count = lax.axis_size(axis)
-    first, last = (max(0, -steps), min(count, count - steps))
-    return lax.ppermute(value, axis, [(source, source + steps) for source in range(first, last)])
+def exchanged(value, axes, first):
+    count = lax.axis_size(axes)
+    pairs = []
+    for low in range(first, count - 1, 2):
+        pairs += [(low, low + 1), (low + 1, low)]
+    return lax.ppermute(value, axes, pairs)
 
 
 def fetch(pairs, sems, first=0):
@@ -143,44 +145,118 @@
     return dot_nt(by_source, by_type).astype(BF16)
 
 
-def parent_operator_kernel(
+def index_kernel(
     types,
     group,
+    box_total,
+    near_src_hbm,
+    near_tile_hbm,
+    slot_hbm,
+    type_hbm,
     par_far_hbm,
     par_type_hbm,
-    op_hbm,
+    op_lo_hbm,
+    op_hi_hbm,
+    code_ref,
+    counts_ref,
+    op_lo,
     d_ref,
+    near_src_ref,
+    near_tile_ref,
+    slot_ref,
+    type_ref,
     par_far_ref,
     par_type_ref,
-    op_ref,
+    op_lo_ref,
+    op_hi_ref,
     index,
-    wide,
-    op,
+    wide_lo,
+    wide_hi,
+    op_hi,
+    counts_hi,
     extra,
 ):
     others = fetch(
-        [(par_far_hbm, par_far_ref), (par_type_hbm, par_type_ref), (op_hbm, op_ref)], extra
+        [
+            (near_src_hbm, near_src_ref),
+            (near_tile_hbm, near_tile_ref),
+            (slot_hbm, slot_ref),
+            (type_hbm, type_ref),
+            (par_far_hbm, par_far_ref),
+            (par_type_hbm, par_type_ref),
+            (op_lo_hbm, op_lo_ref),
+            (op_hi_hbm, op_hi_ref),
+        ],
+        extra,
     )
+    boxes, near = near_src_ref.shape
     rows, far = par_far_ref.shape
-    lines = op_ref.shape[0] // types
+    parents, sources, _ = d_ref.shape
+    slot_total = counts_ref.shape[0] // boxes
+    type_pad = op_hi.shape[0]
+    chunks = op_lo.shape[1] // (2 * LANE)
+    lines = op_hi_ref.shape[0] // types
     share = lines // (2 * group)
-    type_pad = op.shape[0]
+    tile_count = code_ref.shape[0] - 8
     samp = lax.axis_index("samp")
+    position = lax.axis_index("box") * lax.axis_size("samp") + samp
     member = lax.rem(samp, group)
-    first_parent = (samp - member) * (d_ref.shape[0] // group)
+    first_parent = 2 * boxes + (samp - member) * (parents // group)
     place = member * (2 * share)
     base = place // 16 * 16
     index[...] = jnp.full(index.shape, -1, jnp.int32)
-    wide[types * 16 : type_pad * 16] = jnp.zeros(((type_pad - types) * 16, LANE), F32)
-    others[0].wait()
-    others[1].wait()
-    index[0:rows, 0:far] = par_far_ref[...]
-    index[rows : 2 * rows, 0:far] = par_type_ref[...]
-    others[2].wait()
+    tail = (type_pad - types) * 2 * chunks
+    wide_lo[types * 2 * chunks : type_pad * 2 * chunks] = jnp.zeros((tail, LANE), F32)
+    wide_hi[types * 16 : type_pad * 16] = jnp.zeros(((type_pad - types) * 16, LANE), F32)
+    for copy in others[:6]:
+        copy.wait()
+
+    def locate(g, carry):
+        for n in range(near):
+            source = near_src_ref[g, n]
+            live = source < box_total
+            tile = jnp.where(live, near_tile_ref[g, n] - position * tile_count, tile_count)
+            code_ref[tile] = g * 64 + source - (position - 1) * boxes
+        return carry
+
+    lax.fori_loop(0, boxes, locate, 0)
+    index[0:boxes, 0:far] = slot_ref[...]
+    index[boxes : 2 * boxes, 0:far] = type_ref[...]
+    index[2 * boxes : 2 * boxes + rows, 0:far] = par_far_ref[...]
+    index[2 * boxes + rows : 2 * boxes + 2 * rows, 0:far] = par_type_ref[...]
+    batch = 4
+
+    def step_boxes(step, carry):
+        for k in range(batch):
+            g = step * batch + k
+            at = pl.ds(pl.multiple_of(g * slot_total, slot_total), slot_total)
+            counts_ref[at] = tally(index, g, boxes + g, slot_total, type_pad)
+        return carry
+
+    lax.fori_loop(0, boxes // batch, step_boxes, 0)
+
+    def step_parents(step, carry):
+        for k in range(batch):
+            p = step * batch + k
+            at = pl.ds(pl.multiple_of(p * sources, sources), sources)
+            row = first_parent + p
+            counts_hi[at] = tally(index, row, rows + row, sources, type_pad)
+        return carry
+
+    lax.fori_loop(0, parents // batch, step_parents, 0)
+    others[6].wait()
+    wide_lo[0 : types * 2 * chunks] = op_lo_ref[...].astype(F32)
+    for c in range(2):
+        for r in range(chunks):
+            col = (c * chunks + r) * LANE
+            op_lo[:, col : col + LANE] = wide_lo[
+                pl.ds(2 * r + c, type_pad, stride=2 * chunks), :
+            ].astype(BF16)
+    others[7].wait()
 
     def widen(t, carry):
         source = pl.ds(pl.multiple_of(t * lines + base, 16), 16)
-        wide[pl.ds(pl.multiple_of(t * 16, 16), 16)] = op_ref[source].astype(F32)
+        wide_hi[pl.ds(pl.multiple_of(t * 16, 16), 16)] = op_hi_ref[source].astype(F32)
         return carry
 
     lax.fori_loop(0, types, widen, 0, unroll=4)
@@ -188,31 +264,16 @@
         for k in range(share):
             col = (c * share + k) * LANE
             start = place - base + 2 * k + c
-            op[:, col : col + LANE] = wide[pl.ds(start, type_pad, stride=16), :].astype(BF16)
-    parents, sources, _ = d_ref.shape
-    per_step = 4
-
-    def step_parents(step, carry):
-        start = step * per_step
-        counts = jnp.concatenate(
-            [
-                tally(
-                    index,
-                    first_parent + start + k,
-                    rows + first_parent + start + k,
-                    sources,
-                    type_pad,
-                )
-                for k in range(per_step)
-            ],
-            0,
-        )
-        d_ref[pl.ds(start, per_step)] = dot_nn(counts, op[...]).reshape(
-            per_step, sources, 2 * share * LANE
+            op_hi[:, col : col + LANE] = wide_hi[pl.ds(start, type_pad, stride=16), :].astype(BF16)
+
+    def sum_parents(step, carry):
+        at = pl.ds(pl.multiple_of(step * batch * sources, batch * sources), batch * sources)
+        d_ref[pl.ds(step * batch, batch)] = dot_nn(counts_hi[at], op_hi[...]).reshape(
+            batch, sources, 2 * share * LANE
         )
         return carry
 
-    lax.fori_loop(0, parents // per_step, step_parents, 0)
+    lax.fori_loop(0, parents // batch, sum_parents, 0)
 
 
 def parent_kernel(lo_lines, arrived_ref, d_ref, out_ref, wide):
@@ -234,54 +295,39 @@
 
 
 def middle_kernel(
-    types,
-    box_total,
-    lower_hbm,
+    even_ref,
     dens_hbm,
-    upper_hbm,
-    near_src_hbm,
-    near_tile_hbm,
+    odd_ref,
     tiles_hbm,
-    slot_hbm,
-    type_hbm,
-    op_lo_hbm,
+    code_hbm,
+    counts_ref,
+    op_lo,
     arrived_ref,
     near_ref,
     incoming_ref,
     tiles,
     halo,
-    near_src_ref,
-    near_tile_ref,
-    slot_ref,
-    type_ref,
-    op_lo_ref,
     dens3,
     left,
     right,
     acc,
     code,
-    index,
-    wide_op,
-    op_lo,
     summed,
     slots,
     sems,
     extra,
 ):
-    boxes, near = near_src_ref.shape
+    boxes = near_ref.shape[0] // 2
     tile_count = tiles.shape[0]
     steps = sems.shape[0]
     per_step = tile_count // steps
+    odd = lax.rem(lax.axis_index("samp"), 2)
     others = fetch(
         [
-            (near_src_hbm, near_src_ref),
-            (near_tile_hbm, near_tile_ref),
-            (op_lo_hbm, op_lo_ref),
-            (slot_hbm, slot_ref),
-            (type_hbm, type_ref),
-            (lower_hbm, halo.at[0]),
+            (code_hbm, code),
+            (even_ref, halo.at[2 - 2 * odd]),
             (dens_hbm, halo.at[1]),
-            (upper_hbm, halo.at[2]),
+            (odd_ref, halo.at[2 * odd]),
         ],
         extra,
     )
@@ -292,41 +338,13 @@
 
     for step in range(steps):
         tile_copy(step).start()
-    position = lax.axis_index("box") * lax.axis_size("samp") + lax.axis_index("samp")
     acc[...] = jnp.zeros(acc.shape, F32)
-    index[...] = jnp.full(index.shape, -1, jnp.int32)
     left[...] = jnp.zeros(left.shape, F32)
     right[...] = jnp.zeros(right.shape, F32)
-    type_pad = op_lo.shape[0]
-    chunks = op_lo.shape[1] // (2 * LANE)
-    wide_op[types * 2 * chunks : type_pad * 2 * chunks] = jnp.zeros(
-        ((type_pad - types) * 2 * chunks, LANE), F32
-    )
-    others[0].wait()
-    others[1].wait()
-
-    def locate(g, carry):
-        for n in range(near):
-            source = near_src_ref[g, n]
-            live = source < box_total
-            tile = jnp.where(live, near_tile_ref[g, n] - position * tile_count, tile_count)
-            code[tile] = g * 64 + source - (position - 1) * boxes
-        return carry
-
-    lax.fori_loop(0, boxes, locate, 0)
-
-    for copy in others[2:]:
+    lo_lines = slots.shape[0] // arrived_ref.shape[0]
+    slots[...] = arrived_ref[:, :lo_lines, :].astype(F32).reshape(slots.shape)
+    for copy in others:
         copy.wait()
-    wide_op[0 : types * 2 * chunks] = op_lo_ref[...].astype(F32)
-    for c in range(2):
-        for r in range(chunks):
-            col = (c * chunks + r) * LANE
-            op_lo[:, col : col + LANE] = wide_op[
-                pl.ds(2 * r + c, type_pad, stride=2 * chunks), :
-            ].astype(BF16)
-    far = slot_ref.shape[1]
-    index[0:boxes, 0:far] = slot_ref[...]
-    index[boxes : 2 * boxes, 0:far] = type_ref[...]
     for k in range(3):
         dens3[pl.ds(2 * boxes * k, 2 * boxes), :] = halo[k].astype(F32)
     first = dens3[pl.ds(0, 3 * boxes, stride=2), :]
@@ -336,21 +354,15 @@
     right[pl.ds(0, 3 * boxes, stride=8), :] = -second
     right[pl.ds(1, 3 * boxes, stride=8), :] = first
 
-    lo_lines = slots.shape[0] // arrived_ref.shape[0]
-    slots[...] = arrived_ref[:, :lo_lines, :].astype(F32).reshape(slots.shape)
+    chunks = op_lo.shape[1] // (2 * LANE)
     slot_total = slots.shape[0] // (2 * chunks)
     per_boxes = boxes // steps
 
     def step_boxes(step, carry):
         start = step * per_boxes
-        counts = jnp.concatenate(
-            [
-                tally(index, start + k, boxes + start + k, slot_total, type_pad)
-                for k in range(per_boxes)
-            ],
-            0,
-        )
-        summed[...] = dot_nn(counts, op_lo[...])
+        height = per_boxes * slot_total
+        at = pl.ds(pl.multiple_of(start * slot_total, height), height)
+        summed[...] = dot_nn(counts_ref[at], op_lo[...])
         tile_copy(step).wait()
         for pair in range(per_step // 2):
             tile = step * per_step + 2 * pair
@@ -533,29 +545,56 @@
     )(*(in_hbm(x) for x in (rows, radiate, send, interp_matrix, shift_rows)))
     outgoing, near_rows = lax.optimization_barrier((outgoing, rows))
     arrived = lax.all_to_all(outgoing, ("box", "samp"), split_axis=0, concat_axis=0, tiled=True)
-    lower = shifted(near_rows, ("box", "samp"), 1)
-    upper = shifted(near_rows, ("box", "samp"), -1)
+    both = ("box", "samp")
+    even = exchanged(near_rows, both, 0)
+    odd = exchanged(near_rows, both, 1)
     tile_count = near_tiles.shape[0]
     far = far_type.shape
     op_hi_rows = tiled_rows(trans_hi)
     op_lo_rows = tiled_rows(trans_lo)
-    d_hi = pl.pallas_call(
-        functools.partial(parent_operator_kernel, types, group),
-        out_shape=pltpu.VMEM((parents * group, par_total, 2 * share * LANE), F32),
-        in_specs=[HBM_SPEC] * 3,
-        out_specs=VMEM_SPEC,
+    code, counts, op_lo, d_hi = pl.pallas_call(
+        functools.partial(index_kernel, types, group, boxes * devices),
+        out_shape=(
+            jax.ShapeDtypeStruct((tile_count + 8,), jnp.int32),
+            pltpu.VMEM((boxes * slot_total, type_pad), BF16),
+            pltpu.VMEM((type_pad, 2 * width_lo), BF16),
+            pltpu.VMEM((parents * group, par_total, 2 * share * LANE), F32),
+        ),
+        in_specs=[HBM_SPEC] * 8,
+        out_specs=(SMEM_SPEC,) + (VMEM_SPEC,) * 3,
         scratch_shapes=[
+            pltpu.SMEM(near_src.shape, jnp.int32),
+            pltpu.SMEM(near_src.shape, jnp.int32),
+            pltpu.VMEM(far, jnp.int32),
+            pltpu.VMEM(far, jnp.int32),
             pltpu.VMEM(par_far.shape, jnp.int32),
             pltpu.VMEM(par_far.shape, jnp.int32),
+            pltpu.VMEM(op_lo_rows.shape, BF16),
             pltpu.VMEM(op_hi_rows.shape, BF16),
-            pltpu.VMEM((2 * par_far.shape[0], 2 * LANE), jnp.int32),
+            pltpu.VMEM((2 * boxes + 2 * par_far.shape[0], 2 * LANE), jnp.int32),
+            pltpu.VMEM((type_pad * 2 * width_lo // LANE, LANE), F32),
             pltpu.VMEM((type_pad * 16, LANE), F32),
             pltpu.VMEM((type_pad, 2 * share * LANE), BF16),
-            pltpu.SemaphoreType.DMA((3,)),
+            pltpu.VMEM((parents * group * par_total, type_pad), BF16),
+            pltpu.SemaphoreType.DMA((8,)),
         ],
-        compiler_params=pltpu.CompilerParams(vmem_limit_bytes=12 * MIB),
-        cost_estimate=pl.CostEstimate(flops=10**9, bytes_accessed=8 * MIB, transcendentals=0),
-    )(*(in_hbm(x) for x in (par_far, par_type, op_hi_rows)))
+        compiler_params=pltpu.CompilerParams(vmem_limit_bytes=16 * MIB),
+        cost_estimate=pl.CostEstimate(flops=10**9, bytes_accessed=16 * MIB, transcendentals=0),
+    )(
+        *(
+            in_hbm(x)
+            for x in (
+                near_src,
+                near_tile,
+                distant_pattern_slot,
+                far_type,
+                par_far,
+                par_type,
+                op_lo_rows,
+                op_hi_rows,
+            )
+        )
+    )
     above = pl.pallas_call(
         functools.partial(parent_kernel, lo_lines),
         out_shape=jax.ShapeDtypeStruct((group, hi_lines, LANE), F32),
@@ -565,57 +604,44 @@
         compiler_params=pltpu.CompilerParams(vmem_limit_bytes=4 * MIB),
         cost_estimate=pl.CostEstimate(flops=10**8, bytes_accessed=MIB, transcendentals=0),
     )(arrived, in_vmem(d_hi))
-    above, lower, upper = lax.optimization_barrier((above, lower, upper))
+    above, even, odd = lax.optimization_barrier((above, even, odd))
     own_above = lax.all_to_all(
         above, "samp", split_axis=0, concat_axis=0, axis_index_groups=members, tiled=True
     )
     steps = 4
     near, incoming = pl.pallas_call(
-        functools.partial(middle_kernel, types, boxes * devices),
+        middle_kernel,
         out_shape=(
             jax.ShapeDtypeStruct((2 * boxes, panels), F32),
             jax.ShapeDtypeStruct((2 * boxes, width_lo // LANE, LANE), F32),
         ),
-        in_specs=[ANY_SPEC, HBM_SPEC, ANY_SPEC] + [HBM_SPEC] * 6 + [VMEM_SPEC],
+        in_specs=[ANY_SPEC, HBM_SPEC, ANY_SPEC, HBM_SPEC, ANY_SPEC] + [VMEM_SPEC] * 3,
         out_specs=(VMEM_SPEC,) * 2,
         scratch_shapes=[
             pltpu.VMEM(near_tiles.shape, BF16),
             pltpu.VMEM((3, 2 * boxes, panels), BF16),
-            pltpu.SMEM(near_src.shape, jnp.int32),
-            pltpu.SMEM(near_src.shape, jnp.int32),
-            pltpu.VMEM(far, jnp.int32),
-            pltpu.VMEM(far, jnp.int32),
-            pltpu.VMEM(op_lo_rows.shape, BF16),
             pltpu.VMEM((6 * boxes, panels), F32),
             pltpu.VMEM((3 * boxes * 8, LANE), F32),
             pltpu.VMEM((3 * boxes * 8, LANE), F32),
             pltpu.VMEM((boxes, 8, LANE), F32),
             pltpu.SMEM((tile_count + 8,), jnp.int32),
-            pltpu.VMEM((2 * boxes, 2 * LANE), jnp.int32),
-            pltpu.VMEM((type_pad * 2 * width_lo // LANE, LANE), F32),
-            pltpu.VMEM((type_pad, 2 * width_lo), BF16),
             pltpu.VMEM((boxes // steps * slot_total, 2 * width_lo), F32),
             pltpu.VMEM((devices * lo_lines, LANE), F32),
             pltpu.SemaphoreType.DMA((steps,)),
-            pltpu.SemaphoreType.DMA((8,)),
+            pltpu.SemaphoreType.DMA((4,)),
         ],
-        compiler_params=pltpu.CompilerParams(vmem_limit_bytes=(24 if slot_total <= 128 else 40) * MIB),
+        compiler_params=pltpu.CompilerParams(
+            vmem_limit_bytes=(22 if slot_total <= 128 else 36) * MIB
+        ),
         cost_estimate=pl.CostEstimate(flops=10**10, bytes_accessed=20 * MIB, transcendentals=0),
     )(
-        lower,
+        even,
         in_hbm(rows),
-        upper,
-        *(
-            in_hbm(x)
-            for x in (
-                near_src,
-                near_tile,
-                near_tiles,
-                distant_pattern_slot,
-                far_type,
-                op_lo_rows,
-            )
-        ),
+        odd,
+        in_hbm(near_tiles),
+        code,
+        in_vmem(counts),
+        in_vmem(op_lo),
         arrived,
     )
     field = pl.pallas_call(
@@ -634,7 +660,7 @@
         ],
         compiler_params=pltpu.CompilerParams(vmem_limit_bytes=12 * MIB),
         cost_estimate=pl.CostEstimate(flops=10**9, bytes_accessed=8 * MIB, transcendentals=0),
-    )(own_above, incoming, shift_rows, interp_matrix, receive, near)
+    )(own_above, incoming, shift_rows, interp_matrix, in_hbm(receive), near)
     return field.reshape(boxes, 2, panels)
 
 

time: 48.5 us -> 47 us (0.969)
  starting transfers between devices: 19.3 us -> 16.4 us
  Pallas kernels: 26.5 us -> 27.5 us
    ppermute x2, starting transfers between devices: 5.27 us -> 3.55 us  [exchanged(): return lax.ppermute(value, axes, pairs)]
    all_to_all x1, starting transfers between devices: 7.69 us -> 6.54 us  [on_device(): lax.all_to_all(above, 'samp', split_axis=0, concat_axis=0, axis_index_gro...]
    pallas_call x2, Pallas kernels: 17.2 us -> 18.1 us  [the longest x1 10.1 us: on_device(): pl.pallas_call(middle_kernel, out_shape=(jax.ShapeDtypeStruct((2 * boxes,...]
    unnamed x8 -> x10, local copies, waits for them, and re-layouts: 2.19 us -> 2.58 us
  transfers between devices with their start and end apart: 4 -> 4, of which waited for: 0 -> 0; matrix products, arithmetic and copies ran while one was open for 0% -> 0% of each run, Pallas kernels for 38% -> 41%
where the time goes in v4:
time: 47 us; the launch traced here: 46.6 us
  Pallas kernels  27.5 us (59%)
  starting transfers between devices  16.4 us (35%)
  local copies, waits for them, and re-layouts  2.58 us (5%)
    pallas_call x1, Pallas kernels, on_device(): pl.pallas_call(middle_kernel, out_shape=(jax.ShapeDtypeStruct((2 * boxes,...  10.1 us
    pallas_call x1, Pallas kernels, on_device(): pl.pallas_call(functools.partial(index_kernel, types, group, boxes * devi...  8.01 us
    all_to_all x1, starting transfers between devices, on_device(): lax.all_to_all(above, 'samp', split_axis=0, concat_axis=0, axis_index_gro...  6.54 us
    all_to_all x1, starting transfers between devices, on_device(): lax.all_to_all(outgoing, ('box', 'samp'), split_axis=0, concat_axis=0, ti...  6.31 us
    pallas_call x1, Pallas kernels, on_device(): pl.pallas_call(functools.partial(radiate_kernel, group), out_shape=jax.Sh...  4.65 us
    pallas_call x1, Pallas kernels, on_device(): pl.pallas_call(last_kernel, out_shape=jax.ShapeDtypeStruct((2 * boxes, pa...  3.81 us
    ppermute x2, starting transfers between devices, exchanged(): return lax.ppermute(value, axes, pairs)  3.55 us
    unnamed x10, local copies, waits for them, and re-layouts  2.58 us
  transfers between devices with their start and end apart: 4, of which 0 were waited for; matrix products, arithmetic and copies ran while one was open for 0% of the time, Pallas kernels for 41%

profile of v4, /device:TPU:13, one launch (start us, length us, event | category | flops | bytes accessed | tf_op | source)
XLA Modules:
  0.0 46.6 jit_solution(10102031640118597835)
XLA Ops:
  0.0 0.0 copy-start.4
  0.0 4.7 %shard_map.145 = bf16[32,40,128]{2,1,0:T(8,128)(2,1)} custom-call(bf16[32,128]{1,0:T(8,128)(2,1)} %bitcast.22, bf16[16,128,1024]{2,1,0:T(8,128)(2,1)} %radiate_ref.1, s32[4,32]{1,0:T(4,128)} %bitcast.26, bf16[512,2048]{1,0:T(8,128)(2,1)} %interp_hbm.3, f32[256,128]{1,0:T(8,128)} %bitcast.20), custom_call_target="tpu_custom_call" | custom-call | flops 1000000000 | bytes 8388608 | tf_op jit(solution)/shard_map/pallas_call | solution.py:526
  4.7 6.3 %all-to-all-start = ((bf16[32,40,128]{2,1,0:T(8,128)(2,1)}), bf16[32,40,128]{2,1,0:T(8,128)(2,1)S(1)}, u32[]{:S(2)}, u32[]{:S(2)}) async-start(bf16[32,40,128]{2,1,0:T(8,128)(2,1)} %shard_map.145), calls=%async_computation | async-start | bytes 655360 | tf_op jit(solution)/shard_map/all_to_all | solution.py:547
  11.0 0.0 copy-done.4
  11.0 0.4 collective-permute-start
  11.4 3.1 %collective-permute-start.1 = (bf16[32,128]{1,0:T(8,128)(2,1)S(1)}, bf16[32,128]{1,0:T(8,128)(2,1)S(1)}, u32[]{:S(2)}, u32[]{:S(2)}) collective-permute-start(bf16[32,128]{1,0:T(8,128)(2,1)S(1)} %bitcast.25), channel_id=1, source_target_pairs={{1,2},{2,1},{3,4},{4,3},{5,6},{6,5},{7,8},{8,7},{9,10},{10,9},{11,... | collective-permute-start | bytes 24584 | tf_op jit(solution)/shard_map/ppermute | solution.py:37
  14.6 8.0 %shard_map.146 = (s32[232]{0:T(256)S(1)}, bf16[2048,320]{1,0:T(8,128)(2,1)S(1)}, bf16[320,1024]{1,0:T(8,128)(2,1)S(1)}, f32[16,64,512]{2,1,0:T(8,128)S(1)}) custom-call(s32[16,27]{1,0:T(8,128)} %near_src_hbm.1, s32[16,27]{1,0:T(8,128)} %near_tile_hbm.1, s32[16,189]{1,0:T(8,128)} %slot_hbm.1, s32[16,189]{1,0:T(8,128)} %type_hbm.1, s32[16,189]{1,0:T(8,128)} %par_far_hbm.1, ...), custom_call_target="tpu_custom_call" | custom-call | flops 1000000000 | bytes 16777216 | tf_op jit(solution)/shard_map/pallas_call | solution.py:555
  22.6 0.0 copy-start.2
  22.6 1.2 %copy-done.2 = bf16[2048,320]{1,0:T(8,128)(2,1)} copy-done((bf16[2048,320]{1,0:T(8,128)(2,1)}, bf16[2048,320]{1,0:T(8,128)(2,1)S(1)}, u32[]{:S(2)}) %copy-start.2) | copy-done | bytes 1310744
  23.7 0.0 all-to-all-done.arrived_ref
  23.7 1.0 %shard_map.147 = f32[8,8,128]{2,1,0:T(8,128)} custom-call(bf16[32,40,128]{2,1,0:T(8,128)(2,1)S(1)} %all-to-all-done.arrived_ref, f32[16,64,512]{2,1,0:T(8,128)S(1)} %get-tuple-element.17.d_ref), custom_call_target="tpu_custom_call" | custom-call | flops 100000000 | bytes 1048576 | tf_op jit(solution)/shard_map/pallas_call | solution.py:598
  24.7 0.0 collective-permute-done.even_ref
  24.7 0.0 collective-permute-done.1.odd_ref
  24.7 6.5 %all-to-all-start.1 = ((f32[8,8,128]{2,1,0:T(8,128)}), f32[8,8,128]{2,1,0:T(8,128)S(1)}, u32[]{:S(2)}, u32[]{:S(2)}) async-start(f32[8,8,128]{2,1,0:T(8,128)} %shard_map.147), calls=%async_computation.1 | async-start | bytes 65536 | tf_op jit(solution)/shard_map/all_to_all | solution.py:608
  31.3 0.0 copy-start.3
  31.3 1.4 %copy-done.3 = bf16[2048,320]{1,0:T(8,128)(2,1)S(1)} copy-done((bf16[2048,320]{1,0:T(8,128)(2,1)S(1)}, bf16[2048,320]{1,0:T(8,128)(2,1)}, u32[]{:S(2)}) %copy-start.3) | copy-done | bytes 1310744
  32.7 0.0 copy-start
  32.7 0.0 copy-start.1
  32.7 10.1 %shard_map.148 = (f32[32,128]{1,0:T(8,128)S(1)}, f32[32,4,128]{2,1,0:T(4,128)S(1)}) custom-call(bf16[32,128]{1,0:T(8,128)(2,1)S(1)} %collective-permute-done.even_ref, bf16[32,128]{1,0:T(8,128)(2,1)} %bitcast.23, bf16[32,128]{1,0:T(8,128)(2,1)S(1)} %collective-permute-done.1.odd_ref, bf16[224,2,128,128]{3,2,1,0:T(8,128)(2,1)} %tiles_hbm.1, ...), custom_call_target="tpu_custom_call" | custom-call | flops 10000000000 | bytes 20971520 | tf_op jit(solution)/shard_map/pallas_call | solution.py:612
  42.8 0.0 all-to-all-done.1.parent_ref
  42.8 0.0 copy-done
  42.8 0.0 copy-done.1
  42.8 3.8 %shard_map.149 = f32[32,128]{1,0:T(8,128)} custom-call(f32[8,8,128]{2,1,0:T(8,128)S(1)} %all-to-all-done.1.parent_ref, f32[32,4,128]{2,1,0:T(4,128)S(1)} %get-tuple-element.25.incoming_ref, f32[256,128]{1,0:T(8,128)S(1)} %bitcast.21, bf16[512,2048]{1,0:T(8,128)(2,1)S(1)} %copy-done, bf16[16,128,1024]{2,1,0:T(8,128)(2,1)} %receive_ref.1, ...), custom_call_target="tpu_custom_call" | custom-call | flops 1000000000 | bytes 8388608 | tf_op jit(solution)/shard_map/pallas_call | solution.py:647
Async XLA Ops:
  0.0 11.0 %copy-start.4 = (bf16[16,2,128]{2,1,0:T(2,128)(2,1)S(1)}, bf16[16,2,128]{2,1,0:T(2,128)(2,1)}, u32[]{:S(2)}) copy-start(bf16[16,2,128]{2,1,0:T(2,128)(2,1)} %param.15) | copy-start | bytes 24580
  4.7 19.1 %all-to-all-start = ((bf16[32,40,128]{2,1,0:T(8,128)(2,1)}), bf16[32,40,128]{2,1,0:T(8,128)(2,1)S(1)}, u32[]{:S(2)}, u32[]{:S(2)}) async-start(bf16[32,40,128]{2,1,0:T(8,128)(2,1)} %shard_map.145), calls=%async_computation | async-start | bytes 655360 | tf_op jit(solution)/shard_map/all_to_all | solution.py:547
  11.0 13.7 %collective-permute-start = (bf16[32,128]{1,0:T(8,128)(2,1)S(1)}, bf16[32,128]{1,0:T(8,128)(2,1)S(1)}, u32[]{:S(2)}, u32[]{:S(2)}) collective-permute-start(bf16[32,128]{1,0:T(8,128)(2,1)S(1)} %bitcast.24), channel_id=1, source_target_pairs={{0,1},{1,0},{2,3},{3,2},{4,5},{5,4},{6,7},{7,6},{8,9},{9,8},{10,11... | collective-permute-start | bytes 24584 | tf_op jit(solution)/shard_map/ppermute | solution.py:37
  11.4 13.3 %collective-permute-start.1 = (bf16[32,128]{1,0:T(8,128)(2,1)S(1)}, bf16[32,128]{1,0:T(8,128)(2,1)S(1)}, u32[]{:S(2)}, u32[]{:S(2)}) collective-permute-start(bf16[32,128]{1,0:T(8,128)(2,1)S(1)} %bitcast.25), channel_id=1, source_target_pairs={{1,2},{2,1},{3,4},{4,3},{5,6},{6,5},{7,8},{8,7},{9,10},{10,9},{11,... | collective-permute-start | bytes 24584 | tf_op jit(solution)/shard_map/ppermute | solution.py:37
  22.6 1.2 %copy-start.2 = (bf16[2048,320]{1,0:T(8,128)(2,1)}, bf16[2048,320]{1,0:T(8,128)(2,1)S(1)}, u32[]{:S(2)}) copy-start(bf16[2048,320]{1,0:T(8,128)(2,1)S(1)} %get-tuple-element.23.counts_ref) | copy-start | bytes 3932164
  24.7 18.0 %all-to-all-start.1 = ((f32[8,8,128]{2,1,0:T(8,128)}), f32[8,8,128]{2,1,0:T(8,128)S(1)}, u32[]{:S(2)}, u32[]{:S(2)}) async-start(f32[8,8,128]{2,1,0:T(8,128)} %shard_map.147), calls=%async_computation.1 | async-start | bytes 65536 | tf_op jit(solution)/shard_map/all_to_all | solution.py:608
  31.3 1.4 %copy-start.3 = (bf16[2048,320]{1,0:T(8,128)(2,1)S(1)}, bf16[2048,320]{1,0:T(8,128)(2,1)}, u32[]{:S(2)}) copy-start(bf16[2048,320]{1,0:T(8,128)(2,1)} %copy-done.2) | copy-start | bytes 3932164
  32.7 10.1 %copy-start = (bf16[512,2048]{1,0:T(8,128)(2,1)S(1)}, bf16[512,2048]{1,0:T(8,128)(2,1)}, u32[]{:S(2)}) copy-start(bf16[512,2048]{1,0:T(8,128)(2,1)} %interp_hbm.3) | copy-start | bytes 6291460
  32.7 10.1 %copy-start.1 = (f32[8,2,2048]{2,1,0:T(2,128)S(1)}, f32[8,2,2048]{2,1,0:T(2,128)}, u32[]{:S(2)}) copy-start(f32[8,2,2048]{2,1,0:T(2,128)} %param.26) | copy-start | bytes 393220

commit v5 on v4

--- a/solution.py
+++ b/solution.py
@@ -133,7 +133,7 @@
         out_ref[d, 8 * slots : 8 * slots + hi_rows] = parent[pl.ds(member, hi_rows)].astype(BF16)
         return carry
 
-    lax.fori_loop(0, devices, fill, 0)
+    lax.fori_loop(0, devices, fill, 0, unroll=4)
 
 
 def tally(index, source_row, type_row, sources, types):
@@ -158,8 +158,7 @@
     op_lo_hbm,
     op_hi_hbm,
     code_ref,
-    counts_ref,
-    op_lo,
+    d_lo_hbm,
     d_ref,
     near_src_ref,
     near_tile_ref,
@@ -172,19 +171,22 @@
     index,
     wide_lo,
     wide_hi,
+    op_lo,
     op_hi,
     counts_hi,
+    d_lo,
+    sems,
     extra,
 ):
     others = fetch(
         [
+            (op_lo_hbm, op_lo_ref),
             (near_src_hbm, near_src_ref),
             (near_tile_hbm, near_tile_ref),
             (slot_hbm, slot_ref),
             (type_hbm, type_ref),
             (par_far_hbm, par_far_ref),
             (par_type_hbm, par_type_ref),
-            (op_lo_hbm, op_lo_ref),
             (op_hi_hbm, op_hi_ref),
         ],
         extra,
@@ -192,7 +194,7 @@
     boxes, near = near_src_ref.shape
     rows, far = par_far_ref.shape
     parents, sources, _ = d_ref.shape
-    slot_total = counts_ref.shape[0] // boxes
+    slot_total = d_lo.shape[1]
     type_pad = op_hi.shape[0]
     chunks = op_lo.shape[1] // (2 * LANE)
     lines = op_hi_ref.shape[0] // types
@@ -208,9 +210,42 @@
     tail = (type_pad - types) * 2 * chunks
     wide_lo[types * 2 * chunks : type_pad * 2 * chunks] = jnp.zeros((tail, LANE), F32)
     wide_hi[types * 16 : type_pad * 16] = jnp.zeros(((type_pad - types) * 16, LANE), F32)
-    for copy in others[:6]:
+    for copy in others[:7]:
         copy.wait()
 
+    index[0:boxes, 0:far] = slot_ref[...]
+    index[boxes : 2 * boxes, 0:far] = type_ref[...]
+    index[2 * boxes : 2 * boxes + rows, 0:far] = par_far_ref[...]
+    index[2 * boxes + rows : 2 * boxes + 2 * rows, 0:far] = par_type_ref[...]
+    batch = 4
+
+    wide_lo[0 : types * 2 * chunks] = op_lo_ref[...].astype(F32)
+    for c in range(2):
+        for r in range(chunks):
+            col = (c * chunks + r) * LANE
+            op_lo[:, col : col + LANE] = wide_lo[
+                pl.ds(2 * r + c, type_pad, stride=2 * chunks), :
+            ].astype(BF16)
+
+    def lo_copy(step):
+        part = pl.ds(step * batch, batch)
+        return pltpu.make_async_copy(d_lo.at[part], d_lo_hbm.at[part], sems.at[step])
+
+    def step_boxes(step, carry):
+        counts = jnp.concatenate(
+            [
+                tally(index, step * batch + k, boxes + step * batch + k, slot_total, type_pad)
+                for k in range(batch)
+            ],
+            0,
+        )
+        d_lo[pl.ds(step * batch, batch)] = (
+            dot_nn(counts, op_lo[...]).astype(BF16).reshape(batch, slot_total, 2 * chunks * LANE)
+        )
+        lo_copy(step).start()
+        return carry
+
+    lax.fori_loop(0, boxes // batch, step_boxes, 0)
     def locate(g, carry):
         for n in range(near):
             source = near_src_ref[g, n]
@@ -220,21 +255,6 @@
         return carry
 
     lax.fori_loop(0, boxes, locate, 0)
-    index[0:boxes, 0:far] = slot_ref[...]
-    index[boxes : 2 * boxes, 0:far] = type_ref[...]
-    index[2 * boxes : 2 * boxes + rows, 0:far] = par_far_ref[...]
-    index[2 * boxes + rows : 2 * boxes + 2 * rows, 0:far] = par_type_ref[...]
-    batch = 4
-
-    def step_boxes(step, carry):
-        for k in range(batch):
-            g = step * batch + k
-            at = pl.ds(pl.multiple_of(g * slot_total, slot_total), slot_total)
-            counts_ref[at] = tally(index, g, boxes + g, slot_total, type_pad)
-        return carry
-
-    lax.fori_loop(0, boxes // batch, step_boxes, 0)
-
     def step_parents(step, carry):
         for k in range(batch):
             p = step * batch + k
@@ -244,14 +264,6 @@
         return carry
 
     lax.fori_loop(0, parents // batch, step_parents, 0)
-    others[6].wait()
-    wide_lo[0 : types * 2 * chunks] = op_lo_ref[...].astype(F32)
-    for c in range(2):
-        for r in range(chunks):
-            col = (c * chunks + r) * LANE
-            op_lo[:, col : col + LANE] = wide_lo[
-                pl.ds(2 * r + c, type_pad, stride=2 * chunks), :
-            ].astype(BF16)
     others[7].wait()
 
     def widen(t, carry):
@@ -274,6 +286,8 @@
         return carry
 
     lax.fori_loop(0, parents // batch, sum_parents, 0)
+    for step in range(boxes // batch):
+        lo_copy(step).wait()
 
 
 def parent_kernel(lo_lines, arrived_ref, d_ref, out_ref, wide):
@@ -300,8 +314,7 @@
     odd_ref,
     tiles_hbm,
     code_hbm,
-    counts_ref,
-    op_lo,
+    d_lo_hbm,
     arrived_ref,
     near_ref,
     incoming_ref,
@@ -312,9 +325,10 @@
     right,
     acc,
     code,
-    summed,
+    d_lo,
     slots,
     sems,
+    lo_sems,
     extra,
 ):
     boxes = near_ref.shape[0] // 2
@@ -336,8 +350,15 @@
         part = pl.ds(step * per_step, per_step)
         return pltpu.make_async_copy(tiles_hbm.at[part], tiles.at[part], sems.at[step])
 
+    per_boxes = boxes // steps
+
+    def lo_copy(step):
+        part = pl.ds(step * per_boxes, per_boxes)
+        return pltpu.make_async_copy(d_lo_hbm.at[part], d_lo.at[part], lo_sems.at[step])
+
     for step in range(steps):
         tile_copy(step).start()
+        lo_copy(step).start()
     acc[...] = jnp.zeros(acc.shape, F32)
     left[...] = jnp.zeros(left.shape, F32)
     right[...] = jnp.zeros(right.shape, F32)
@@ -354,15 +375,11 @@
     right[pl.ds(0, 3 * boxes, stride=8), :] = -second
     right[pl.ds(1, 3 * boxes, stride=8), :] = first
 
-    chunks = op_lo.shape[1] // (2 * LANE)
-    slot_total = slots.shape[0] // (2 * chunks)
-    per_boxes = boxes // steps
+    chunks = d_lo.shape[2] // (2 * LANE)
+    slot_total = d_lo.shape[1]
 
     def step_boxes(step, carry):
         start = step * per_boxes
-        height = per_boxes * slot_total
-        at = pl.ds(pl.multiple_of(start * slot_total, height), height)
-        summed[...] = dot_nn(counts_ref[at], op_lo[...])
         tile_copy(step).wait()
         for pair in range(per_step // 2):
             tile = step * per_step + 2 * pair
@@ -383,14 +400,14 @@
                 acc[owners[h]] = (
                     acc[owners[h]] + product[8 * h : 8 * (h + 1), h * LANE : (h + 1) * LANE]
                 )
+        lo_copy(step).wait()
         for r in range(chunks):
             cols = slice(r * LANE, (r + 1) * LANE)
             first = slots[pl.ds(r, slot_total, stride=2 * chunks), :]
             second = slots[pl.ds(chunks + r, slot_total, stride=2 * chunks), :]
             for k in range(per_boxes):
-                part = slice(k * slot_total, (k + 1) * slot_total)
-                o_re = summed[part, cols]
-                o_im = summed[part, (chunks + r) * LANE : (chunks + r + 1) * LANE]
+                o_re = d_lo[start + k, :, cols].astype(F32)
+                o_im = d_lo[start + k, :, (chunks + r) * LANE : (chunks + r + 1) * LANE].astype(F32)
                 incoming_ref[start + k, r : r + 1] = jnp.sum(
                     o_re * first - o_im * second, 0, keepdims=True
                 )
@@ -543,25 +560,20 @@
         compiler_params=pltpu.CompilerParams(vmem_limit_bytes=12 * MIB),
         cost_estimate=pl.CostEstimate(flops=10**9, bytes_accessed=8 * MIB, transcendentals=0),
     )(*(in_hbm(x) for x in (rows, radiate, send, interp_matrix, shift_rows)))
-    outgoing, near_rows = lax.optimization_barrier((outgoing, rows))
     arrived = lax.all_to_all(outgoing, ("box", "samp"), split_axis=0, concat_axis=0, tiled=True)
-    both = ("box", "samp")
-    even = exchanged(near_rows, both, 0)
-    odd = exchanged(near_rows, both, 1)
     tile_count = near_tiles.shape[0]
     far = far_type.shape
     op_hi_rows = tiled_rows(trans_hi)
     op_lo_rows = tiled_rows(trans_lo)
-    code, counts, op_lo, d_hi = pl.pallas_call(
+    code, d_lo, d_hi = pl.pallas_call(
         functools.partial(index_kernel, types, group, boxes * devices),
         out_shape=(
             jax.ShapeDtypeStruct((tile_count + 8,), jnp.int32),
-            pltpu.VMEM((boxes * slot_total, type_pad), BF16),
-            pltpu.VMEM((type_pad, 2 * width_lo), BF16),
+            pltpu.HBM((boxes, slot_total, 2 * width_lo), BF16),
             pltpu.VMEM((parents * group, par_total, 2 * share * LANE), F32),
         ),
         in_specs=[HBM_SPEC] * 8,
-        out_specs=(SMEM_SPEC,) + (VMEM_SPEC,) * 3,
+        out_specs=(SMEM_SPEC, HBM_SPEC, VMEM_SPEC),
         scratch_shapes=[
             pltpu.SMEM(near_src.shape, jnp.int32),
             pltpu.SMEM(near_src.shape, jnp.int32),
@@ -574,11 +586,16 @@
             pltpu.VMEM((2 * boxes + 2 * par_far.shape[0], 2 * LANE), jnp.int32),
             pltpu.VMEM((type_pad * 2 * width_lo // LANE, LANE), F32),
             pltpu.VMEM((type_pad * 16, LANE), F32),
+            pltpu.VMEM((type_pad, 2 * width_lo), BF16),
             pltpu.VMEM((type_pad, 2 * share * LANE), BF16),
             pltpu.VMEM((parents * group * par_total, type_pad), BF16),
+            pltpu.VMEM((boxes, slot_total, 2 * width_lo), BF16),
+            pltpu.SemaphoreType.DMA((boxes // 4,)),
             pltpu.SemaphoreType.DMA((8,)),
         ],
-        compiler_params=pltpu.CompilerParams(vmem_limit_bytes=16 * MIB),
+        compiler_params=pltpu.CompilerParams(
+            vmem_limit_bytes=(20 if slot_total <= 128 else 46) * MIB
+        ),
         cost_estimate=pl.CostEstimate(flops=10**9, bytes_accessed=16 * MIB, transcendentals=0),
     )(
         *(
@@ -604,7 +621,9 @@
         compiler_params=pltpu.CompilerParams(vmem_limit_bytes=4 * MIB),
         cost_estimate=pl.CostEstimate(flops=10**8, bytes_accessed=MIB, transcendentals=0),
     )(arrived, in_vmem(d_hi))
-    above, even, odd = lax.optimization_barrier((above, even, odd))
+    above, near_rows = lax.optimization_barrier((above, rows))
+    even = exchanged(near_rows, ("box", "samp"), 0)
+    odd = exchanged(near_rows, ("box", "samp"), 1)
     own_above = lax.all_to_all(
         above, "samp", split_axis=0, concat_axis=0, axis_index_groups=members, tiled=True
     )
@@ -615,7 +634,7 @@
             jax.ShapeDtypeStruct((2 * boxes, panels), F32),
             jax.ShapeDtypeStruct((2 * boxes, width_lo // LANE, LANE), F32),
         ),
-        in_specs=[ANY_SPEC, HBM_SPEC, ANY_SPEC, HBM_SPEC, ANY_SPEC] + [VMEM_SPEC] * 3,
+        in_specs=[ANY_SPEC, HBM_SPEC, ANY_SPEC, HBM_SPEC, ANY_SPEC, HBM_SPEC, VMEM_SPEC],
         out_specs=(VMEM_SPEC,) * 2,
         scratch_shapes=[
             pltpu.VMEM(near_tiles.shape, BF16),
@@ -625,13 +644,14 @@
             pltpu.VMEM((3 * boxes * 8, LANE), F32),
             pltpu.VMEM((boxes, 8, LANE), F32),
             pltpu.SMEM((tile_count + 8,), jnp.int32),
-            pltpu.VMEM((boxes // steps * slot_total, 2 * width_lo), F32),
+            pltpu.VMEM((boxes, slot_total, 2 * width_lo), BF16),
             pltpu.VMEM((devices * lo_lines, LANE), F32),
+            pltpu.SemaphoreType.DMA((steps,)),
             pltpu.SemaphoreType.DMA((steps,)),
             pltpu.SemaphoreType.DMA((4,)),
         ],
         compiler_params=pltpu.CompilerParams(
-            vmem_limit_bytes=(22 if slot_total <= 128 else 36) * MIB
+            vmem_limit_bytes=(24 if slot_total <= 128 else 42) * MIB
         ),
         cost_estimate=pl.CostEstimate(flops=10**10, bytes_accessed=20 * MIB, transcendentals=0),
     )(
@@ -640,8 +660,7 @@
         odd,
         in_hbm(near_tiles),
         code,
-        in_vmem(counts),
-        in_vmem(op_lo),
+        in_hbm(d_lo),
         arrived,
     )
     field = pl.pallas_call(

time: 47 us -> 45.2 us (0.962)
  the two profiles are of different devices: /device:TPU:13 before, /device:TPU:0 now
where the time goes in v5:
time: 45.2 us; the launch traced here: 44.5 us
  Pallas kernels  28.6 us (63%)
  starting transfers between devices  14.3 us (32%)
  waiting for transfers between devices  1.43 us (3%)
    pallas_call x1, Pallas kernels, on_device(): pl.pallas_call(functools.partial(index_kernel, types, group, boxes * devi...  10.7 us
    pallas_call x1, Pallas kernels, on_device(): pl.pallas_call(middle_kernel, out_shape=(jax.ShapeDtypeStruct((2 * boxes,...  8.66 us
    all_to_all x1, starting transfers between devices, on_device(): lax.all_to_all(outgoing, ('box', 'samp'), split_axis=0, concat_axis=0, ti...  7.3 us
    all_to_all x1, starting transfers between devices, on_device(): lax.all_to_all(above, 'samp', split_axis=0, concat_axis=0, axis_index_gro...  4.53 us
    pallas_call x1, Pallas kernels, on_device(): pl.pallas_call(functools.partial(radiate_kernel, group), out_shape=jax.Sh...  4.5 us
    pallas_call x1, Pallas kernels, on_device(): pl.pallas_call(last_kernel, out_shape=jax.ShapeDtypeStruct((2 * boxes, pa...  3.81 us
    ppermute x2, starting transfers between devices, exchanged(): return lax.ppermute(value, axes, pairs)  2.44 us
    all_to_all x1, waiting for transfers between devices, on_device(): lax.all_to_all(outgoing, ('box', 'samp'), split_axis=0, concat_axis=0, ti...  1.42 us
  transfers between devices with their start and end apart: 4, of which 1 were waited for; matrix products, arithmetic and copies ran while one was open for 0% of the time, Pallas kernels for 44%

profile of v5, /device:TPU:0, one launch (start us, length us, event | category | flops | bytes accessed | tf_op | source)
XLA Modules:
  0.0 44.5 jit_solution(5362833527491336519)
XLA Ops:
  0.0 4.5 %shard_map.145 = bf16[32,40,128]{2,1,0:T(8,128)(2,1)} custom-call(bf16[32,128]{1,0:T(8,128)(2,1)} %bitcast.22, bf16[16,128,1024]{2,1,0:T(8,128)(2,1)} %radiate_ref.1, s32[4,32]{1,0:T(4,128)} %bitcast.26, bf16[512,2048]{1,0:T(8,128)(2,1)} %interp_hbm.3, f32[256,128]{1,0:T(8,128)} %bitcast.20), custom_call_target="tpu_custom_call" | custom-call | flops 1000000000 | bytes 8388608 | tf_op jit(solution)/shard_map/pallas_call | solution.py:543
  4.5 0.0 copy-start.2
  4.5 7.3 %all-to-all-start = ((bf16[32,40,128]{2,1,0:T(8,128)(2,1)}), bf16[32,40,128]{2,1,0:T(8,128)(2,1)S(1)}, u32[]{:S(2)}, u32[]{:S(2)}) async-start(bf16[32,40,128]{2,1,0:T(8,128)(2,1)} %shard_map.145), calls=%async_computation | async-start | bytes 655360 | tf_op jit(solution)/shard_map/all_to_all | solution.py:563
  11.8 10.7 %shard_map.146 = (s32[232]{0:T(256)S(1)}, bf16[16,128,1024]{2,1,0:T(8,128)(2,1)}, f32[16,64,512]{2,1,0:T(8,128)S(1)}) custom-call(s32[16,27]{1,0:T(8,128)} %near_src_hbm.1, s32[16,27]{1,0:T(8,128)} %near_tile_hbm.1, s32[16,189]{1,0:T(8,128)} %slot_hbm.1, s32[16,189]{1,0:T(8,128)} %type_hbm.1, s32[16,189]{1,0:T(8,128)} %par_far_hbm.1, ...), custom_call_target="tpu_custom_call" | custom-call | flops 1000000000 | bytes 16777216 | tf_op jit(solution)/shard_map/pallas_call | solution.py:568
  22.5 1.4 %all-to-all-done.arrived_ref = bf16[32,40,128]{2,1,0:T(8,128)(2,1)S(1)} async-done(((bf16[32,40,128]{2,1,0:T(8,128)(2,1)}), bf16[32,40,128]{2,1,0:T(8,128)(2,1)S(1)}, u32[]{:S(2)}, u32[]{:S(2)}) %all-to-all-start) | async-done | bytes 327712 | tf_op jit(solution)/shard_map/all_to_all | solution.py:563
  24.0 1.0 %shard_map.147 = f32[8,8,128]{2,1,0:T(8,128)} custom-call(bf16[32,40,128]{2,1,0:T(8,128)(2,1)S(1)} %all-to-all-done.arrived_ref, f32[16,64,512]{2,1,0:T(8,128)S(1)} %get-tuple-element.12.d_ref), custom_call_target="tpu_custom_call" | custom-call | flops 100000000 | bytes 1048576 | tf_op jit(solution)/shard_map/pallas_call | solution.py:615
  24.9 0.0 copy-done.2
  24.9 0.7 %collective-permute-start.1 = (bf16[32,128]{1,0:T(8,128)(2,1)S(1)}, bf16[32,128]{1,0:T(8,128)(2,1)S(1)}, u32[]{:S(2)}, u32[]{:S(2)}) collective-permute-start(bf16[32,128]{1,0:T(8,128)(2,1)S(1)} %bitcast.24), channel_id=1, source_target_pairs={{1,2},{2,1},{3,4},{4,3},{5,6},{6,5},{7,8},{8,7},{9,10},{10,9},{11,... | collective-permute-start | bytes 24584 | tf_op jit(solution)/shard_map/ppermute | solution.py:37
  25.6 1.8 %collective-permute-start = (bf16[32,128]{1,0:T(8,128)(2,1)S(1)}, bf16[32,128]{1,0:T(8,128)(2,1)S(1)}, u32[]{:S(2)}, u32[]{:S(2)}) collective-permute-start(bf16[32,128]{1,0:T(8,128)(2,1)S(1)} %bitcast.25), channel_id=1, source_target_pairs={{0,1},{1,0},{2,3},{3,2},{4,5},{5,4},{6,7},{7,6},{8,9},{9,8},{10,11... | collective-permute-start | bytes 24584 | tf_op jit(solution)/shard_map/ppermute | solution.py:37
  27.4 4.5 %all-to-all-start.1 = ((f32[8,8,128]{2,1,0:T(8,128)}), f32[8,8,128]{2,1,0:T(8,128)S(1)}, u32[]{:S(2)}, u32[]{:S(2)}) async-start(f32[8,8,128]{2,1,0:T(8,128)} %shard_map.147), calls=%async_computation.1 | async-start | bytes 65536 | tf_op jit(solution)/shard_map/all_to_all | solution.py:627
  31.9 0.0 collective-permute-done.1.odd_ref
  31.9 0.0 collective-permute-done.even_ref
  31.9 0.0 copy-start
  31.9 0.0 copy-start.1
  32.0 8.7 %shard_map.148 = (f32[32,128]{1,0:T(8,128)S(1)}, f32[32,4,128]{2,1,0:T(4,128)S(1)}) custom-call(bf16[32,128]{1,0:T(8,128)(2,1)S(1)} %collective-permute-done.even_ref, bf16[32,128]{1,0:T(8,128)(2,1)} %bitcast.23, bf16[32,128]{1,0:T(8,128)(2,1)S(1)} %collective-permute-done.1.odd_ref, bf16[224,2,128,128]{3,2,1,0:T(8,128)(2,1)} %tiles_hbm.1, ...), custom_call_target="tpu_custom_call" | custom-call | flops 10000000000 | bytes 20971520 | tf_op jit(solution)/shard_map/pallas_call | solution.py:631
  40.6 0.0 all-to-all-done.1.parent_ref
  40.6 0.0 copy-done
  40.6 0.0 copy-done.1
  40.7 3.8 %shard_map.149 = f32[32,128]{1,0:T(8,128)} custom-call(f32[8,8,128]{2,1,0:T(8,128)S(1)} %all-to-all-done.1.parent_ref, f32[32,4,128]{2,1,0:T(4,128)S(1)} %get-tuple-element.17.incoming_ref, f32[256,128]{1,0:T(8,128)S(1)} %bitcast.21, bf16[512,2048]{1,0:T(8,128)(2,1)S(1)} %copy-done, bf16[16,128,1024]{2,1,0:T(8,128)(2,1)} %receive_ref.1, ...), custom_call_target="tpu_custom_call" | custom-call | flops 1000000000 | bytes 8388608 | tf_op jit(solution)/shard_map/pallas_call | solution.py:666
Async XLA Ops:
  4.5 20.4 %copy-start.2 = (bf16[16,2,128]{2,1,0:T(2,128)(2,1)S(1)}, bf16[16,2,128]{2,1,0:T(2,128)(2,1)}, u32[]{:S(2)}) copy-start(bf16[16,2,128]{2,1,0:T(2,128)(2,1)} %param.15) | copy-start | bytes 24580
  4.5 19.4 %all-to-all-start = ((bf16[32,40,128]{2,1,0:T(8,128)(2,1)}), bf16[32,40,128]{2,1,0:T(8,128)(2,1)S(1)}, u32[]{:S(2)}, u32[]{:S(2)}) async-start(bf16[32,40,128]{2,1,0:T(8,128)(2,1)} %shard_map.145), calls=%async_computation | async-start | bytes 655360 | tf_op jit(solution)/shard_map/all_to_all | solution.py:563
  24.9 7.0 %collective-permute-start.1 = (bf16[32,128]{1,0:T(8,128)(2,1)S(1)}, bf16[32,128]{1,0:T(8,128)(2,1)S(1)}, u32[]{:S(2)}, u32[]{:S(2)}) collective-permute-start(bf16[32,128]{1,0:T(8,128)(2,1)S(1)} %bitcast.24), channel_id=1, source_target_pairs={{1,2},{2,1},{3,4},{4,3},{5,6},{6,5},{7,8},{8,7},{9,10},{10,9},{11,... | collective-permute-start | bytes 24584 | tf_op jit(solution)/shard_map/ppermute | solution.py:37
  25.6 6.3 %collective-permute-start = (bf16[32,128]{1,0:T(8,128)(2,1)S(1)}, bf16[32,128]{1,0:T(8,128)(2,1)S(1)}, u32[]{:S(2)}, u32[]{:S(2)}) collective-permute-start(bf16[32,128]{1,0:T(8,128)(2,1)S(1)} %bitcast.25), channel_id=1, source_target_pairs={{0,1},{1,0},{2,3},{3,2},{4,5},{5,4},{6,7},{7,6},{8,9},{9,8},{10,11... | collective-permute-start | bytes 24584 | tf_op jit(solution)/shard_map/ppermute | solution.py:37
  27.4 13.2 %all-to-all-start.1 = ((f32[8,8,128]{2,1,0:T(8,128)}), f32[8,8,128]{2,1,0:T(8,128)S(1)}, u32[]{:S(2)}, u32[]{:S(2)}) async-start(f32[8,8,128]{2,1,0:T(8,128)} %shard_map.147), calls=%async_computation.1 | async-start | bytes 65536 | tf_op jit(solution)/shard_map/all_to_all | solution.py:627
  31.9 8.7 %copy-start = (bf16[512,2048]{1,0:T(8,128)(2,1)S(1)}, bf16[512,2048]{1,0:T(8,128)(2,1)}, u32[]{:S(2)}) copy-start(bf16[512,2048]{1,0:T(8,128)(2,1)} %interp_hbm.3) | copy-start | bytes 6291460
  31.9 8.7 %copy-start.1 = (f32[8,2,2048]{2,1,0:T(2,128)S(1)}, f32[8,2,2048]{2,1,0:T(2,128)}, u32[]{:S(2)}) copy-start(f32[8,2,2048]{2,1,0:T(2,128)} %param.26) | copy-start | bytes 393220

commit v6 on v5

--- a/solution.py
+++ b/solution.py
@@ -231,39 +231,34 @@
         part = pl.ds(step * batch, batch)
         return pltpu.make_async_copy(d_lo.at[part], d_lo_hbm.at[part], sems.at[step])
 
-    def step_boxes(step, carry):
-        counts = jnp.concatenate(
-            [
-                tally(index, step * batch + k, boxes + step * batch + k, slot_total, type_pad)
-                for k in range(batch)
-            ],
-            0,
-        )
-        d_lo[pl.ds(step * batch, batch)] = (
-            dot_nn(counts, op_lo[...]).astype(BF16).reshape(batch, slot_total, 2 * chunks * LANE)
-        )
-        lo_copy(step).start()
-        return carry
-
-    lax.fori_loop(0, boxes // batch, step_boxes, 0)
-    def locate(g, carry):
+    def locate(g):
         for n in range(near):
             source = near_src_ref[g, n]
             live = source < box_total
             tile = jnp.where(live, near_tile_ref[g, n] - position * tile_count, tile_count)
             code_ref[tile] = g * 64 + source - (position - 1) * boxes
-        return carry
-
-    lax.fori_loop(0, boxes, locate, 0)
-    def step_parents(step, carry):
+
+    def step_lists(step, carry):
+        counts = []
+        for k in range(batch):
+            g = step * batch + k
+            locate(g)
+            counts.append(tally(index, g, boxes + g, slot_total, type_pad))
+        counts = jnp.concatenate(counts, 0)
+        part = 2 * chunks * LANE // batch
         for k in range(batch):
             p = step * batch + k
             at = pl.ds(pl.multiple_of(p * sources, sources), sources)
             row = first_parent + p
             counts_hi[at] = tally(index, row, rows + row, sources, type_pad)
+            cols = slice(k * part, (k + 1) * part)
+            d_lo[pl.ds(step * batch, batch), :, cols] = (
+                dot_nn(counts, op_lo[:, cols]).astype(BF16).reshape(batch, slot_total, part)
+            )
+        lo_copy(step).start()
         return carry
 
-    lax.fori_loop(0, parents // batch, step_parents, 0)
+    lax.fori_loop(0, boxes // batch, step_lists, 0)
     others[7].wait()
 
     def widen(t, carry):
@@ -327,6 +322,7 @@
     code,
     d_lo,
     slots,
+    received,
     sems,
     lo_sems,
     extra,
@@ -377,11 +373,15 @@
 
     chunks = d_lo.shape[2] // (2 * LANE)
     slot_total = d_lo.shape[1]
+    for r in range(2 * chunks):
+        received[:, r * LANE : (r + 1) * LANE] = slots[pl.ds(r, slot_total, stride=2 * chunks), :]
 
     def step_boxes(step, carry):
         start = step * per_boxes
         tile_copy(step).wait()
-        for pair in range(per_step // 2):
+        lo_copy(step).wait()
+
+        def multiply_pair(pair):
             tile = step * per_step + 2 * pair
             both = tiles[pl.ds(tile, 2)]
             weights = jnp.concatenate(
@@ -400,20 +400,28 @@
                 acc[owners[h]] = (
                     acc[owners[h]] + product[8 * h : 8 * (h + 1), h * LANE : (h + 1) * LANE]
                 )
-        lo_copy(step).wait()
-        for r in range(chunks):
-            cols = slice(r * LANE, (r + 1) * LANE)
-            first = slots[pl.ds(r, slot_total, stride=2 * chunks), :]
-            second = slots[pl.ds(chunks + r, slot_total, stride=2 * chunks), :]
-            for k in range(per_boxes):
-                o_re = d_lo[start + k, :, cols].astype(F32)
-                o_im = d_lo[start + k, :, (chunks + r) * LANE : (chunks + r + 1) * LANE].astype(F32)
-                incoming_ref[start + k, r : r + 1] = jnp.sum(
-                    o_re * first - o_im * second, 0, keepdims=True
-                )
-                incoming_ref[boxes + start + k, r : r + 1] = jnp.sum(
-                    o_re * second + o_im * first, 0, keepdims=True
-                )
+
+        def multiply_slots(r, k):
+            first = received[:, r * LANE : (r + 1) * LANE]
+            second = received[:, (chunks + r) * LANE : (chunks + r + 1) * LANE]
+            o_re = d_lo[start + k, :, r * LANE : (r + 1) * LANE].astype(F32)
+            o_im = d_lo[start + k, :, (chunks + r) * LANE : (chunks + r + 1) * LANE].astype(F32)
+            incoming_ref[start + k, r : r + 1] = jnp.sum(
+                o_re * first - o_im * second, 0, keepdims=True
+            )
+            incoming_ref[boxes + start + k, r : r + 1] = jnp.sum(
+                o_re * second + o_im * first, 0, keepdims=True
+            )
+
+        pairs = per_step // 2
+        parts = [(r, k) for r in range(chunks) for k in range(per_boxes)]
+        done = 0
+        for pair in range(pairs):
+            multiply_pair(pair)
+            upto = len(parts) * (pair + 1) // pairs
+            for r, k in parts[done:upto]:
+                multiply_slots(r, k)
+            done = upto
         return carry
 
     lax.fori_loop(0, steps, step_boxes, 0)
@@ -646,6 +654,7 @@
             pltpu.SMEM((tile_count + 8,), jnp.int32),
             pltpu.VMEM((boxes, slot_total, 2 * width_lo), BF16),
             pltpu.VMEM((devices * lo_lines, LANE), F32),
+            pltpu.VMEM((slot_total, 2 * width_lo), F32),
             pltpu.SemaphoreType.DMA((steps,)),
             pltpu.SemaphoreType.DMA((steps,)),
             pltpu.SemaphoreType.DMA((4,)),

time: 45.2 us -> 44.2 us (0.978)
  Pallas kernels: 28.6 us -> 27.1 us
  waiting for transfers between devices: 1.43 us -> 2.9 us
  starting transfers between devices: 14.3 us -> 13.6 us
    pallas_call x1, Pallas kernels: 10.7 us -> 9.24 us  [on_device(): pl.pallas_call(functools.partial(index_kernel, types, group, boxes * devi...]
    all_to_all x1, waiting for transfers between devices: 1.42 us -> 2.89 us  [on_device(): lax.all_to_all(outgoing, ('box', 'samp'), split_axis=0, concat_axis=0, ti...]
  transfers between devices with their start and end apart: 4 -> 4, of which waited for: 1 -> 1; matrix products, arithmetic and copies ran while one was open for 0% -> 0% of each run, Pallas kernels for 44% -> 41%
where the time goes in v6:
time: 44.2 us; the launch traced here: 43.6 us
  Pallas kernels  27.1 us (61%)
  starting transfers between devices  13.6 us (31%)
  waiting for transfers between devices  2.9 us (7%)
    pallas_call x1, Pallas kernels, on_device(): pl.pallas_call(functools.partial(index_kernel, types, group, boxes * devi...  9.24 us
    pallas_call x1, Pallas kernels, on_device(): pl.pallas_call(middle_kernel, out_shape=(jax.ShapeDtypeStruct((2 * boxes,...  8.55 us
    all_to_all x1, starting transfers between devices, on_device(): lax.all_to_all(outgoing, ('box', 'samp'), split_axis=0, concat_axis=0, ti...  7.3 us
    pallas_call x1, Pallas kernels, on_device(): pl.pallas_call(functools.partial(radiate_kernel, group), out_shape=jax.Sh...  4.5 us
    all_to_all x1, starting transfers between devices, on_device(): lax.all_to_all(above, 'samp', split_axis=0, concat_axis=0, axis_index_gro...  4.16 us
    pallas_call x1, Pallas kernels, on_device(): pl.pallas_call(last_kernel, out_shape=jax.ShapeDtypeStruct((2 * boxes, pa...  3.81 us
    all_to_all x1, waiting for transfers between devices, on_device(): lax.all_to_all(outgoing, ('box', 'samp'), split_axis=0, concat_axis=0, ti...  2.89 us
    ppermute x2, starting transfers between devices, exchanged(): return lax.ppermute(value, axes, pairs)  2.09 us
  transfers between devices with their start and end apart: 4, of which 1 were waited for; matrix products, arithmetic and copies ran while one was open for 0% of the time, Pallas kernels for 41%

profile of v6, /device:TPU:0, one launch (start us, length us, event | category | flops | bytes accessed | tf_op | source)
XLA Modules:
  0.0 43.6 jit_solution(15024823310558656467)
XLA Ops:
  0.0 4.5 %shard_map.145 = bf16[32,40,128]{2,1,0:T(8,128)(2,1)} custom-call(bf16[32,128]{1,0:T(8,128)(2,1)} %bitcast.22, bf16[16,128,1024]{2,1,0:T(8,128)(2,1)} %radiate_ref.1, s32[4,32]{1,0:T(4,128)} %bitcast.26, bf16[512,2048]{1,0:T(8,128)(2,1)} %interp_hbm.3, f32[256,128]{1,0:T(8,128)} %bitcast.20), custom_call_target="tpu_custom_call" | custom-call | flops 1000000000 | bytes 8388608 | tf_op jit(solution)/shard_map/pallas_call | solution.py:551
  4.5 0.0 copy-start.2
  4.5 7.3 %all-to-all-start = ((bf16[32,40,128]{2,1,0:T(8,128)(2,1)}), bf16[32,40,128]{2,1,0:T(8,128)(2,1)S(1)}, u32[]{:S(2)}, u32[]{:S(2)}) async-start(bf16[32,40,128]{2,1,0:T(8,128)(2,1)} %shard_map.145), calls=%async_computation | async-start | bytes 655360 | tf_op jit(solution)/shard_map/all_to_all | solution.py:571
  11.8 9.2 %shard_map.146 = (s32[232]{0:T(256)S(1)}, bf16[16,128,1024]{2,1,0:T(8,128)(2,1)}, f32[16,64,512]{2,1,0:T(8,128)S(1)}) custom-call(s32[16,27]{1,0:T(8,128)} %near_src_hbm.1, s32[16,27]{1,0:T(8,128)} %near_tile_hbm.1, s32[16,189]{1,0:T(8,128)} %slot_hbm.1, s32[16,189]{1,0:T(8,128)} %type_hbm.1, s32[16,189]{1,0:T(8,128)} %par_far_hbm.1, ...), custom_call_target="tpu_custom_call" | custom-call | flops 1000000000 | bytes 16777216 | tf_op jit(solution)/shard_map/pallas_call | solution.py:576
  21.1 2.9 %all-to-all-done.arrived_ref = bf16[32,40,128]{2,1,0:T(8,128)(2,1)S(1)} async-done(((bf16[32,40,128]{2,1,0:T(8,128)(2,1)}), bf16[32,40,128]{2,1,0:T(8,128)(2,1)S(1)}, u32[]{:S(2)}, u32[]{:S(2)}) %all-to-all-start) | async-done | bytes 327712 | tf_op jit(solution)/shard_map/all_to_all | solution.py:571
  24.0 1.0 %shard_map.147 = f32[8,8,128]{2,1,0:T(8,128)} custom-call(bf16[32,40,128]{2,1,0:T(8,128)(2,1)S(1)} %all-to-all-done.arrived_ref, f32[16,64,512]{2,1,0:T(8,128)S(1)} %get-tuple-element.12.d_ref), custom_call_target="tpu_custom_call" | custom-call | flops 100000000 | bytes 1048576 | tf_op jit(solution)/shard_map/pallas_call | solution.py:623
  24.9 0.0 copy-done.2
  24.9 0.7 %collective-permute-start.1 = (bf16[32,128]{1,0:T(8,128)(2,1)S(1)}, bf16[32,128]{1,0:T(8,128)(2,1)S(1)}, u32[]{:S(2)}, u32[]{:S(2)}) collective-permute-start(bf16[32,128]{1,0:T(8,128)(2,1)S(1)} %bitcast.24), channel_id=1, source_target_pairs={{1,2},{2,1},{3,4},{4,3},{5,6},{6,5},{7,8},{8,7},{9,10},{10,9},{11,... | collective-permute-start | bytes 24584 | tf_op jit(solution)/shard_map/ppermute | solution.py:37
  25.6 1.4 %collective-permute-start = (bf16[32,128]{1,0:T(8,128)(2,1)S(1)}, bf16[32,128]{1,0:T(8,128)(2,1)S(1)}, u32[]{:S(2)}, u32[]{:S(2)}) collective-permute-start(bf16[32,128]{1,0:T(8,128)(2,1)S(1)} %bitcast.25), channel_id=1, source_target_pairs={{0,1},{1,0},{2,3},{3,2},{4,5},{5,4},{6,7},{7,6},{8,9},{9,8},{10,11... | collective-permute-start | bytes 24584 | tf_op jit(solution)/shard_map/ppermute | solution.py:37
  27.0 4.2 %all-to-all-start.1 = ((f32[8,8,128]{2,1,0:T(8,128)}), f32[8,8,128]{2,1,0:T(8,128)S(1)}, u32[]{:S(2)}, u32[]{:S(2)}) async-start(f32[8,8,128]{2,1,0:T(8,128)} %shard_map.147), calls=%async_computation.1 | async-start | bytes 65536 | tf_op jit(solution)/shard_map/all_to_all | solution.py:635
  31.2 0.0 collective-permute-done.1.odd_ref
  31.2 0.0 collective-permute-done.even_ref
  31.2 0.0 copy-start
  31.2 0.0 copy-start.1
  31.2 8.5 %shard_map.148 = (f32[32,128]{1,0:T(8,128)S(1)}, f32[32,4,128]{2,1,0:T(4,128)S(1)}) custom-call(bf16[32,128]{1,0:T(8,128)(2,1)S(1)} %collective-permute-done.even_ref, bf16[32,128]{1,0:T(8,128)(2,1)} %bitcast.23, bf16[32,128]{1,0:T(8,128)(2,1)S(1)} %collective-permute-done.1.odd_ref, bf16[224,2,128,128]{3,2,1,0:T(8,128)(2,1)} %tiles_hbm.1, ...), custom_call_target="tpu_custom_call" | custom-call | flops 10000000000 | bytes 20971520 | tf_op jit(solution)/shard_map/pallas_call | solution.py:639
  39.8 0.0 all-to-all-done.1.parent_ref
  39.8 0.0 copy-done
  39.8 0.0 copy-done.1
  39.8 3.8 %shard_map.149 = f32[32,128]{1,0:T(8,128)} custom-call(f32[8,8,128]{2,1,0:T(8,128)S(1)} %all-to-all-done.1.parent_ref, f32[32,4,128]{2,1,0:T(4,128)S(1)} %get-tuple-element.17.incoming_ref, f32[256,128]{1,0:T(8,128)S(1)} %bitcast.21, bf16[512,2048]{1,0:T(8,128)(2,1)S(1)} %copy-done, bf16[16,128,1024]{2,1,0:T(8,128)(2,1)} %receive_ref.1, ...), custom_call_target="tpu_custom_call" | custom-call | flops 1000000000 | bytes 8388608 | tf_op jit(solution)/shard_map/pallas_call | solution.py:675
Async XLA Ops:
  4.5 20.4 %copy-start.2 = (bf16[16,2,128]{2,1,0:T(2,128)(2,1)S(1)}, bf16[16,2,128]{2,1,0:T(2,128)(2,1)}, u32[]{:S(2)}) copy-start(bf16[16,2,128]{2,1,0:T(2,128)(2,1)} %param.15) | copy-start | bytes 24580
  4.5 19.4 %all-to-all-start = ((bf16[32,40,128]{2,1,0:T(8,128)(2,1)}), bf16[32,40,128]{2,1,0:T(8,128)(2,1)S(1)}, u32[]{:S(2)}, u32[]{:S(2)}) async-start(bf16[32,40,128]{2,1,0:T(8,128)(2,1)} %shard_map.145), calls=%async_computation | async-start | bytes 655360 | tf_op jit(solution)/shard_map/all_to_all | solution.py:571
  24.9 6.3 %collective-permute-start.1 = (bf16[32,128]{1,0:T(8,128)(2,1)S(1)}, bf16[32,128]{1,0:T(8,128)(2,1)S(1)}, u32[]{:S(2)}, u32[]{:S(2)}) collective-permute-start(bf16[32,128]{1,0:T(8,128)(2,1)S(1)} %bitcast.24), channel_id=1, source_target_pairs={{1,2},{2,1},{3,4},{4,3},{5,6},{6,5},{7,8},{8,7},{9,10},{10,9},{11,... | collective-permute-start | bytes 24584 | tf_op jit(solution)/shard_map/ppermute | solution.py:37
  25.6 5.6 %collective-permute-start = (bf16[32,128]{1,0:T(8,128)(2,1)S(1)}, bf16[32,128]{1,0:T(8,128)(2,1)S(1)}, u32[]{:S(2)}, u32[]{:S(2)}) collective-permute-start(bf16[32,128]{1,0:T(8,128)(2,1)S(1)} %bitcast.25), channel_id=1, source_target_pairs={{0,1},{1,0},{2,3},{3,2},{4,5},{5,4},{6,7},{7,6},{8,9},{9,8},{10,11... | collective-permute-start | bytes 24584 | tf_op jit(solution)/shard_map/ppermute | solution.py:37
  27.0 12.8 %all-to-all-start.1 = ((f32[8,8,128]{2,1,0:T(8,128)}), f32[8,8,128]{2,1,0:T(8,128)S(1)}, u32[]{:S(2)}, u32[]{:S(2)}) async-start(f32[8,8,128]{2,1,0:T(8,128)} %shard_map.147), calls=%async_computation.1 | async-start | bytes 65536 | tf_op jit(solution)/shard_map/all_to_all | solution.py:635
  31.2 8.6 %copy-start = (bf16[512,2048]{1,0:T(8,128)(2,1)S(1)}, bf16[512,2048]{1,0:T(8,128)(2,1)}, u32[]{:S(2)}) copy-start(bf16[512,2048]{1,0:T(8,128)(2,1)} %interp_hbm.3) | copy-start | bytes 6291460
  31.2 8.6 %copy-start.1 = (f32[8,2,2048]{2,1,0:T(2,128)S(1)}, f32[8,2,2048]{2,1,0:T(2,128)}, u32[]{:S(2)}) copy-start(f32[8,2,2048]{2,1,0:T(2,128)} %param.26) | copy-start | bytes 393220

commit v7 on v6

--- a/solution.py
+++ b/solution.py
@@ -148,20 +148,14 @@
 def index_kernel(
     types,
     group,
-    box_total,
-    near_src_hbm,
-    near_tile_hbm,
     slot_hbm,
     type_hbm,
     par_far_hbm,
     par_type_hbm,
     op_lo_hbm,
     op_hi_hbm,
-    code_ref,
     d_lo_hbm,
     d_ref,
-    near_src_ref,
-    near_tile_ref,
     slot_ref,
     type_ref,
     par_far_ref,
@@ -181,8 +175,6 @@
     others = fetch(
         [
             (op_lo_hbm, op_lo_ref),
-            (near_src_hbm, near_src_ref),
-            (near_tile_hbm, near_tile_ref),
             (slot_hbm, slot_ref),
             (type_hbm, type_ref),
             (par_far_hbm, par_far_ref),
@@ -191,7 +183,7 @@
         ],
         extra,
     )
-    boxes, near = near_src_ref.shape
+    boxes = slot_ref.shape[0]
     rows, far = par_far_ref.shape
     parents, sources, _ = d_ref.shape
     slot_total = d_lo.shape[1]
@@ -199,9 +191,7 @@
     chunks = op_lo.shape[1] // (2 * LANE)
     lines = op_hi_ref.shape[0] // types
     share = lines // (2 * group)
-    tile_count = code_ref.shape[0] - 8
     samp = lax.axis_index("samp")
-    position = lax.axis_index("box") * lax.axis_size("samp") + samp
     member = lax.rem(samp, group)
     first_parent = 2 * boxes + (samp - member) * (parents // group)
     place = member * (2 * share)
@@ -210,7 +200,7 @@
     tail = (type_pad - types) * 2 * chunks
     wide_lo[types * 2 * chunks : type_pad * 2 * chunks] = jnp.zeros((tail, LANE), F32)
     wide_hi[types * 16 : type_pad * 16] = jnp.zeros(((type_pad - types) * 16, LANE), F32)
-    for copy in others[:7]:
+    for copy in others[:5]:
         copy.wait()
 
     index[0:boxes, 0:far] = slot_ref[...]
@@ -218,6 +208,7 @@
     index[2 * boxes : 2 * boxes + rows, 0:far] = par_far_ref[...]
     index[2 * boxes + rows : 2 * boxes + 2 * rows, 0:far] = par_type_ref[...]
     batch = 4
+    share_parents = parents * batch // boxes
 
     wide_lo[0 : types * 2 * chunks] = op_lo_ref[...].astype(F32)
     for c in range(2):
@@ -231,35 +222,28 @@
         part = pl.ds(step * batch, batch)
         return pltpu.make_async_copy(d_lo.at[part], d_lo_hbm.at[part], sems.at[step])
 
-    def locate(g):
-        for n in range(near):
-            source = near_src_ref[g, n]
-            live = source < box_total
-            tile = jnp.where(live, near_tile_ref[g, n] - position * tile_count, tile_count)
-            code_ref[tile] = g * 64 + source - (position - 1) * boxes
-
     def step_lists(step, carry):
         counts = []
         for k in range(batch):
             g = step * batch + k
-            locate(g)
             counts.append(tally(index, g, boxes + g, slot_total, type_pad))
         counts = jnp.concatenate(counts, 0)
         part = 2 * chunks * LANE // batch
         for k in range(batch):
-            p = step * batch + k
-            at = pl.ds(pl.multiple_of(p * sources, sources), sources)
-            row = first_parent + p
-            counts_hi[at] = tally(index, row, rows + row, sources, type_pad)
             cols = slice(k * part, (k + 1) * part)
             d_lo[pl.ds(step * batch, batch), :, cols] = (
                 dot_nn(counts, op_lo[:, cols]).astype(BF16).reshape(batch, slot_total, part)
             )
+            if k < share_parents:
+                p = step * share_parents + k
+                at = pl.ds(pl.multiple_of(p * sources, sources), sources)
+                row = first_parent + p
+                counts_hi[at] = tally(index, row, rows + row, sources, type_pad)
         lo_copy(step).start()
         return carry
 
     lax.fori_loop(0, boxes // batch, step_lists, 0)
-    others[7].wait()
+    others[5].wait()
 
     def widen(t, carry):
         source = pl.ds(pl.multiple_of(t * lines + base, 16), 16)
@@ -273,68 +257,66 @@
             start = place - base + 2 * k + c
             op_hi[:, col : col + LANE] = wide_hi[pl.ds(start, type_pad, stride=16), :].astype(BF16)
 
-    def sum_parents(step, carry):
-        at = pl.ds(pl.multiple_of(step * batch * sources, batch * sources), batch * sources)
-        d_ref[pl.ds(step * batch, batch)] = dot_nn(counts_hi[at], op_hi[...]).reshape(
-            batch, sources, 2 * share * LANE
+    for first in range(0, 2 * share * LANE, 2 * LANE):
+        cols = slice(first, first + 2 * LANE)
+        d_ref[:, :, cols] = dot_nn(counts_hi[...], op_hi[:, cols]).reshape(
+            parents, sources, 2 * LANE
         )
-        return carry
-
-    lax.fori_loop(0, parents // batch, sum_parents, 0)
     for step in range(boxes // batch):
         lo_copy(step).wait()
 
 
-def parent_kernel(lo_lines, arrived_ref, d_ref, out_ref, wide):
+def parent_kernel(lo_lines, arrived_ref, d_ref, mine_ref, theirs_ref, wide):
     parents, sources, width = d_ref.shape
     share = width // (2 * LANE)
-    rows = out_ref.shape[1]
+    own = parents // 2
+    member = lax.rem(lax.axis_index("samp"), 2)
     wide[...] = arrived_ref[:, lo_lines:, :].astype(F32).reshape(wide.shape)
     for k in range(share):
         first = wide[pl.ds(k, sources, stride=2 * share), :]
         second = wide[pl.ds(share + k, sources, stride=2 * share), :]
-        for p in range(parents):
-            o_re = d_ref[p, :, k * LANE : (k + 1) * LANE]
-            o_im = d_ref[p, :, (share + k) * LANE : (share + k + 1) * LANE]
-            row = p * 2 * share + k
-            to, row = row // rows, row % rows
-            out_ref[to, row : row + 1] = jnp.sum(o_re * first - o_im * second, 0, keepdims=True)
-            row += share
-            out_ref[to, row : row + 1] = jnp.sum(o_re * second + o_im * first, 0, keepdims=True)
-
-
-def middle_kernel(
+        for out_ref, start in ((theirs_ref, (1 - member) * own), (mine_ref, member * own)):
+            for q in range(own):
+                o_re = d_ref[start + q, :, k * LANE : (k + 1) * LANE]
+                o_im = d_ref[start + q, :, (share + k) * LANE : (share + k + 1) * LANE]
+                row = q * 2 * share + k
+                out_ref[row : row + 1] = jnp.sum(o_re * first - o_im * second, 0, keepdims=True)
+                row += share
+                out_ref[row : row + 1] = jnp.sum(o_re * second + o_im * first, 0, keepdims=True)
+
+
+def near_kernel(
+    box_total,
     even_ref,
     dens_hbm,
     odd_ref,
+    near_src_hbm,
+    near_tile_hbm,
     tiles_hbm,
-    code_hbm,
-    d_lo_hbm,
-    arrived_ref,
     near_ref,
-    incoming_ref,
     tiles,
     halo,
+    near_src_ref,
+    near_tile_ref,
     dens3,
     left,
     right,
     acc,
     code,
-    d_lo,
-    slots,
-    received,
     sems,
-    lo_sems,
     extra,
 ):
-    boxes = near_ref.shape[0] // 2
+    boxes, near = near_src_ref.shape
     tile_count = tiles.shape[0]
     steps = sems.shape[0]
     per_step = tile_count // steps
-    odd = lax.rem(lax.axis_index("samp"), 2)
+    samp = lax.axis_index("samp")
+    position = lax.axis_index("box") * lax.axis_size("samp") + samp
+    odd = lax.rem(samp, 2)
     others = fetch(
         [
-            (code_hbm, code),
+            (near_src_hbm, near_src_ref),
+            (near_tile_hbm, near_tile_ref),
             (even_ref, halo.at[2 - 2 * odd]),
             (dens_hbm, halo.at[1]),
             (odd_ref, halo.at[2 * odd]),
@@ -346,20 +328,11 @@
         part = pl.ds(step * per_step, per_step)
         return pltpu.make_async_copy(tiles_hbm.at[part], tiles.at[part], sems.at[step])
 
-    per_boxes = boxes // steps
-
-    def lo_copy(step):
-        part = pl.ds(step * per_boxes, per_boxes)
-        return pltpu.make_async_copy(d_lo_hbm.at[part], d_lo.at[part], lo_sems.at[step])
-
     for step in range(steps):
         tile_copy(step).start()
-        lo_copy(step).start()
     acc[...] = jnp.zeros(acc.shape, F32)
     left[...] = jnp.zeros(left.shape, F32)
     right[...] = jnp.zeros(right.shape, F32)
-    lo_lines = slots.shape[0] // arrived_ref.shape[0]
-    slots[...] = arrived_ref[:, :lo_lines, :].astype(F32).reshape(slots.shape)
     for copy in others:
         copy.wait()
     for k in range(3):
@@ -371,67 +344,86 @@
     right[pl.ds(0, 3 * boxes, stride=8), :] = -second
     right[pl.ds(1, 3 * boxes, stride=8), :] = first
 
-    chunks = d_lo.shape[2] // (2 * LANE)
-    slot_total = d_lo.shape[1]
-    for r in range(2 * chunks):
-        received[:, r * LANE : (r + 1) * LANE] = slots[pl.ds(r, slot_total, stride=2 * chunks), :]
-
-    def step_boxes(step, carry):
-        start = step * per_boxes
+
+    def locate(g, carry):
+        for n in range(near):
+            source = near_src_ref[g, n]
+            live = source < box_total
+            tile = jnp.where(live, near_tile_ref[g, n] - position * tile_count, tile_count)
+            code[tile] = g * 64 + source - (position - 1) * boxes
+        return carry
+
+    lax.fori_loop(0, boxes, locate, 0)
+
+    def multiply_pair(tile):
+        both = tiles[pl.ds(tile, 2)]
+        weights = jnp.concatenate(
+            [both[:, 0].reshape(2 * LANE, LANE), both[:, 1].reshape(2 * LANE, LANE)], 1
+        )
+        owners, lefts, rights = [], [], []
+        for h in range(2):
+            entry = code[tile + h]
+            row = pl.ds(pl.multiple_of((entry & 63) * 8, 8), 8)
+            owners.append(entry >> 6)
+            lefts.append(left[row])
+            rights.append(right[row])
+        lhs = jnp.concatenate([jnp.concatenate(lefts, 0), jnp.concatenate(rights, 0)], 1)
+        product = dot_nt(lhs.astype(BF16), weights)
+        for h in range(2):
+            acc[owners[h]] = (
+                acc[owners[h]] + product[8 * h : 8 * (h + 1), h * LANE : (h + 1) * LANE]
+            )
+
+
+    def step_tiles(step, carry):
         tile_copy(step).wait()
-        lo_copy(step).wait()
-
-        def multiply_pair(pair):
-            tile = step * per_step + 2 * pair
-            both = tiles[pl.ds(tile, 2)]
-            weights = jnp.concatenate(
-                [both[:, 0].reshape(2 * LANE, LANE), both[:, 1].reshape(2 * LANE, LANE)], 1
-            )
-            owners, lefts, rights = [], [], []
-            for h in range(2):
-                entry = code[tile + h]
-                row = pl.ds(pl.multiple_of((entry & 63) * 8, 8), 8)
-                owners.append(entry >> 6)
-                lefts.append(left[row])
-                rights.append(right[row])
-            lhs = jnp.concatenate([jnp.concatenate(lefts, 0), jnp.concatenate(rights, 0)], 1)
-            product = dot_nt(lhs.astype(BF16), weights)
-            for h in range(2):
-                acc[owners[h]] = (
-                    acc[owners[h]] + product[8 * h : 8 * (h + 1), h * LANE : (h + 1) * LANE]
-                )
-
-        def multiply_slots(r, k):
-            first = received[:, r * LANE : (r + 1) * LANE]
-            second = received[:, (chunks + r) * LANE : (chunks + r + 1) * LANE]
-            o_re = d_lo[start + k, :, r * LANE : (r + 1) * LANE].astype(F32)
-            o_im = d_lo[start + k, :, (chunks + r) * LANE : (chunks + r + 1) * LANE].astype(F32)
-            incoming_ref[start + k, r : r + 1] = jnp.sum(
-                o_re * first - o_im * second, 0, keepdims=True
-            )
-            incoming_ref[boxes + start + k, r : r + 1] = jnp.sum(
-                o_re * second + o_im * first, 0, keepdims=True
-            )
-
-        pairs = per_step // 2
-        parts = [(r, k) for r in range(chunks) for k in range(per_boxes)]
-        done = 0
-        for pair in range(pairs):
-            multiply_pair(pair)
-            upto = len(parts) * (pair + 1) // pairs
-            for r, k in parts[done:upto]:
-                multiply_slots(r, k)
-            done = upto
+        for pair in range(per_step // 2):
+            multiply_pair(step * per_step + 2 * pair)
         return carry
 
-    lax.fori_loop(0, steps, step_boxes, 0)
+    lax.fori_loop(0, steps, step_tiles, 0)
     for g in range(boxes):
         row = 2 * g
         near_ref[row : row + 2] = acc[g, 0:2] + 0.5 * dens3[pl.ds(2 * boxes + row, 2), :]
 
 
+def leaf_kernel(d_lo_hbm, arrived_ref, incoming_ref, d_lo, slots, received, sems):
+    boxes, slot_total, width = d_lo.shape
+    chunks = width // (2 * LANE)
+    steps = sems.shape[0]
+    per_boxes = boxes // steps
+    copies = []
+    for step in range(steps):
+        part = pl.ds(step * per_boxes, per_boxes)
+        copies.append(pltpu.make_async_copy(d_lo_hbm.at[part], d_lo.at[part], sems.at[step]))
+        copies[-1].start()
+    lo_lines = slots.shape[0] // arrived_ref.shape[0]
+    slots[...] = arrived_ref[:, :lo_lines, :].astype(F32).reshape(slots.shape)
+    for r in range(2 * chunks):
+        received[:, r * LANE : (r + 1) * LANE] = slots[pl.ds(r, slot_total, stride=2 * chunks), :]
+
+    def multiply_slots(r, g):
+        first = received[:, r * LANE : (r + 1) * LANE]
+        second = received[:, (chunks + r) * LANE : (chunks + r + 1) * LANE]
+        o_re = d_lo[g, :, r * LANE : (r + 1) * LANE].astype(F32)
+        o_im = d_lo[g, :, (chunks + r) * LANE : (chunks + r + 1) * LANE].astype(F32)
+        incoming_ref[g, r : r + 1] = jnp.sum(
+            o_re * first - o_im * second, 0, keepdims=True
+        )
+        incoming_ref[boxes + g, r : r + 1] = jnp.sum(
+            o_re * second + o_im * first, 0, keepdims=True
+        )
+
+    for step in range(steps):
+        copies[step].wait()
+        for r in range(chunks):
+            for k in range(per_boxes):
+                multiply_slots(r, step * per_boxes + k)
+
+
 def last_kernel(
-    parent_ref,
+    mine_ref,
+    other_ref,
     incoming_ref,
     shift_hbm,
     interp_hbm,
@@ -441,6 +433,7 @@
     receive,
     shift_ref,
     interp_ref,
+    parent_ref,
     down,
     blend,
     sems,
@@ -455,6 +448,9 @@
         part = pl.ds(step * per_step, per_step)
         copies.append(pltpu.make_async_copy(receive_ref.at[part], receive.at[part], sems.at[step]))
         copies[-1].start()
+    member = lax.rem(lax.axis_index("samp"), 2)
+    parent_ref[member] = mine_ref[...]
+    parent_ref[1 - member] = other_ref[...]
     own_parents = boxes // 8
     hi_chunks = down.shape[1] // LANE
     chunks = incoming_ref.shape[1]
@@ -536,15 +532,11 @@
     slot_total = devices * slots
     par_total = devices * parents
     type_pad = -(-types // 8) * 8
-    samp_count = lax.axis_size("samp")
-    group = min(samp_count, 8)
+    group = 2
     share = width_hi // LANE // group
     lo_lines = slots * 2 * width_lo // LANE
     hi_lines = parents * 2 * share
     lines = lo_lines + hi_lines
-    members = None
-    if group < samp_count:
-        members = [list(range(k, k + group)) for k in range(0, samp_count, group)]
     rows = density.reshape(boxes * 2, panels)
     shift_rows = tiled_rows(shifts)
     send = send_box[0].T
@@ -568,23 +560,47 @@
         compiler_params=pltpu.CompilerParams(vmem_limit_bytes=12 * MIB),
         cost_estimate=pl.CostEstimate(flops=10**9, bytes_accessed=8 * MIB, transcendentals=0),
     )(*(in_hbm(x) for x in (rows, radiate, send, interp_matrix, shift_rows)))
+    both = ("box", "samp")
+    even = exchanged(rows, both, 0)
+    odd = exchanged(rows, both, 1)
+    outgoing, even, odd = lax.optimization_barrier((outgoing, even, odd))
     arrived = lax.all_to_all(outgoing, ("box", "samp"), split_axis=0, concat_axis=0, tiled=True)
     tile_count = near_tiles.shape[0]
     far = far_type.shape
     op_hi_rows = tiled_rows(trans_hi)
     op_lo_rows = tiled_rows(trans_lo)
-    code, d_lo, d_hi = pl.pallas_call(
-        functools.partial(index_kernel, types, group, boxes * devices),
+    steps = 8
+    near = pl.pallas_call(
+        functools.partial(near_kernel, boxes * devices),
+        out_shape=jax.ShapeDtypeStruct((2 * boxes, panels), F32),
+        in_specs=[ANY_SPEC, HBM_SPEC, ANY_SPEC] + [HBM_SPEC] * 3,
+        out_specs=VMEM_SPEC,
+        scratch_shapes=[
+            pltpu.VMEM(near_tiles.shape, BF16),
+            pltpu.VMEM((3, 2 * boxes, panels), BF16),
+            pltpu.SMEM(near_src.shape, jnp.int32),
+            pltpu.SMEM(near_src.shape, jnp.int32),
+            pltpu.VMEM((6 * boxes, panels), F32),
+            pltpu.VMEM((3 * boxes * 8, LANE), F32),
+            pltpu.VMEM((3 * boxes * 8, LANE), F32),
+            pltpu.VMEM((boxes, 8, LANE), F32),
+            pltpu.SMEM((tile_count + 8,), jnp.int32),
+            pltpu.SemaphoreType.DMA((steps,)),
+            pltpu.SemaphoreType.DMA((5,)),
+        ],
+        compiler_params=pltpu.CompilerParams(vmem_limit_bytes=20 * MIB),
+        cost_estimate=pl.CostEstimate(flops=10**10, bytes_accessed=16 * MIB, transcendentals=0),
+    )(even, in_hbm(rows), odd, in_hbm(near_src), in_hbm(near_tile), in_hbm(near_tiles))
+    near, far_type = lax.optimization_barrier((near, far_type))
+    d_lo, d_hi = pl.pallas_call(
+        functools.partial(index_kernel, types, group),
         out_shape=(
-            jax.ShapeDtypeStruct((tile_count + 8,), jnp.int32),
             pltpu.HBM((boxes, slot_total, 2 * width_lo), BF16),
             pltpu.VMEM((parents * group, par_total, 2 * share * LANE), F32),
         ),
-        in_specs=[HBM_SPEC] * 8,
-        out_specs=(SMEM_SPEC, HBM_SPEC, VMEM_SPEC),
+        in_specs=[HBM_SPEC] * 6,
+        out_specs=(HBM_SPEC, VMEM_SPEC),
         scratch_shapes=[
-            pltpu.SMEM(near_src.shape, jnp.int32),
-            pltpu.SMEM(near_src.shape, jnp.int32),
             pltpu.VMEM(far, jnp.int32),
             pltpu.VMEM(far, jnp.int32),
             pltpu.VMEM(par_far.shape, jnp.int32),
@@ -599,7 +615,7 @@
             pltpu.VMEM((parents * group * par_total, type_pad), BF16),
             pltpu.VMEM((boxes, slot_total, 2 * width_lo), BF16),
             pltpu.SemaphoreType.DMA((boxes // 4,)),
-            pltpu.SemaphoreType.DMA((8,)),
+            pltpu.SemaphoreType.DMA((6,)),
         ],
         compiler_params=pltpu.CompilerParams(
             vmem_limit_bytes=(20 if slot_total <= 128 else 46) * MIB
@@ -609,8 +625,6 @@
         *(
             in_hbm(x)
             for x in (
-                near_src,
-                near_tile,
                 distant_pattern_slot,
                 far_type,
                 par_far,
@@ -620,67 +634,43 @@
             )
         )
     )
-    above = pl.pallas_call(
+    mine, theirs = pl.pallas_call(
         functools.partial(parent_kernel, lo_lines),
-        out_shape=jax.ShapeDtypeStruct((group, hi_lines, LANE), F32),
+        out_shape=(jax.ShapeDtypeStruct((hi_lines, LANE), F32),) * 2,
         in_specs=[VMEM_SPEC] * 2,
-        out_specs=VMEM_SPEC,
+        out_specs=(VMEM_SPEC,) * 2,
         scratch_shapes=[pltpu.VMEM((devices * hi_lines, LANE), F32)],
-        compiler_params=pltpu.CompilerParams(vmem_limit_bytes=4 * MIB),
+        compiler_params=pltpu.CompilerParams(vmem_limit_bytes=8 * MIB),
         cost_estimate=pl.CostEstimate(flops=10**8, bytes_accessed=MIB, transcendentals=0),
     )(arrived, in_vmem(d_hi))
-    above, near_rows = lax.optimization_barrier((above, rows))
-    even = exchanged(near_rows, ("box", "samp"), 0)
-    odd = exchanged(near_rows, ("box", "samp"), 1)
-    own_above = lax.all_to_all(
-        above, "samp", split_axis=0, concat_axis=0, axis_index_groups=members, tiled=True
-    )
-    steps = 4
-    near, incoming = pl.pallas_call(
-        middle_kernel,
-        out_shape=(
-            jax.ShapeDtypeStruct((2 * boxes, panels), F32),
-            jax.ShapeDtypeStruct((2 * boxes, width_lo // LANE, LANE), F32),
-        ),
-        in_specs=[ANY_SPEC, HBM_SPEC, ANY_SPEC, HBM_SPEC, ANY_SPEC, HBM_SPEC, VMEM_SPEC],
-        out_specs=(VMEM_SPEC,) * 2,
+    theirs, d_lo = lax.optimization_barrier((theirs, d_lo))
+    other = exchanged(theirs, both, 0)
+    incoming = pl.pallas_call(
+        leaf_kernel,
+        out_shape=jax.ShapeDtypeStruct((2 * boxes, width_lo // LANE, LANE), F32),
+        in_specs=[HBM_SPEC, VMEM_SPEC],
+        out_specs=VMEM_SPEC,
         scratch_shapes=[
-            pltpu.VMEM(near_tiles.shape, BF16),
-            pltpu.VMEM((3, 2 * boxes, panels), BF16),
-            pltpu.VMEM((6 * boxes, panels), F32),
-            pltpu.VMEM((3 * boxes * 8, LANE), F32),
-            pltpu.VMEM((3 * boxes * 8, LANE), F32),
-            pltpu.VMEM((boxes, 8, LANE), F32),
-            pltpu.SMEM((tile_count + 8,), jnp.int32),
             pltpu.VMEM((boxes, slot_total, 2 * width_lo), BF16),
             pltpu.VMEM((devices * lo_lines, LANE), F32),
             pltpu.VMEM((slot_total, 2 * width_lo), F32),
-            pltpu.SemaphoreType.DMA((steps,)),
-            pltpu.SemaphoreType.DMA((steps,)),
-            pltpu.SemaphoreType.DMA((4,)),
+            pltpu.SemaphoreType.DMA((boxes // 2,)),
         ],
         compiler_params=pltpu.CompilerParams(
-            vmem_limit_bytes=(24 if slot_total <= 128 else 42) * MIB
+            vmem_limit_bytes=(10 if slot_total <= 128 else 32) * MIB
         ),
-        cost_estimate=pl.CostEstimate(flops=10**10, bytes_accessed=20 * MIB, transcendentals=0),
-    )(
-        even,
-        in_hbm(rows),
-        odd,
-        in_hbm(near_tiles),
-        code,
-        in_hbm(d_lo),
-        arrived,
-    )
+        cost_estimate=pl.CostEstimate(flops=10**9, bytes_accessed=5 * MIB, transcendentals=0),
+    )(in_hbm(d_lo), arrived)
     field = pl.pallas_call(
         last_kernel,
         out_shape=jax.ShapeDtypeStruct((2 * boxes, panels), F32),
-        in_specs=[VMEM_SPEC] * 2 + [HBM_SPEC] * 3 + [VMEM_SPEC],
+        in_specs=[VMEM_SPEC] * 3 + [HBM_SPEC] * 3 + [VMEM_SPEC],
         out_specs=VMEM_SPEC,
         scratch_shapes=[
             pltpu.VMEM(receive.shape, BF16),
             pltpu.VMEM(shift_rows.shape, F32),
             pltpu.VMEM(interp_matrix.shape, BF16),
+            pltpu.VMEM((group, hi_lines, LANE), F32),
             pltpu.VMEM((2 * boxes, width_hi), BF16),
             pltpu.VMEM((2 * boxes, 2 * width_lo // LANE, LANE), F32),
             pltpu.SemaphoreType.DMA((boxes // 4,)),
@@ -688,7 +678,7 @@
         ],
         compiler_params=pltpu.CompilerParams(vmem_limit_bytes=12 * MIB),
         cost_estimate=pl.CostEstimate(flops=10**9, bytes_accessed=8 * MIB, transcendentals=0),
-    )(own_above, incoming, shift_rows, interp_matrix, in_hbm(receive), near)
+    )(mine, other, incoming, shift_rows, interp_matrix, in_hbm(receive), near)
     return field.reshape(boxes, 2, panels)
 
 

time: 44.2 us -> 40.3 us (0.912)
  starting transfers between devices: 13.6 us -> 10.1 us
  local copies, waits for them, and re-layouts: 0.02 us -> 3.03 us
  waiting for transfers between devices: 2.9 us -> 0.21 us
  Pallas kernels: 27.1 us -> 26.5 us
    all_to_all x1 -> x0, starting transfers between devices: 4.16 us -> none  [on_device(): lax.all_to_all(above, 'samp', split_axis=0, concat_axis=0, axis_index_gro...]
    ppermute x2 -> x3, starting transfers between devices: 2.09 us -> 5.26 us  [exchanged(): return lax.ppermute(value, axes, pairs)]
    unnamed x6 -> x8, local copies, waits for them, and re-layouts: 0.02 us -> 3.03 us
    all_to_all x1, waiting for transfers between devices: 2.89 us -> 0.2 us  [on_device(): lax.all_to_all(outgoing, ('box', 'samp'), split_axis=0, concat_axis=0, ti...]
    all_to_all x1, starting transfers between devices: 7.3 us -> 4.84 us  [on_device(): lax.all_to_all(outgoing, ('box', 'samp'), split_axis=0, concat_axis=0, ti...]
    pallas_call x3 -> x4, Pallas kernels: 18.7 us -> 18.1 us  [the longest x1 7.63 us: on_device(): pl.pallas_call(functools.partial(index_kernel, types, group), out_shape=(...]
  transfers between devices with their start and end apart: 4 -> 4, of which waited for: 1 -> 1; matrix products, arithmetic and copies ran while one was open for 0% -> 0% of each run, Pallas kernels for 41% -> 56%
where the time goes in v7:
time: 40.3 us; the launch traced here: 39.9 us
  Pallas kernels  26.5 us (66%)
  starting transfers between devices  10.1 us (25%)
  local copies, waits for them, and re-layouts  3.03 us (8%)
    pallas_call x1, Pallas kernels, on_device(): pl.pallas_call(functools.partial(index_kernel, types, group), out_shape=(...  7.63 us
    pallas_call x1, Pallas kernels, on_device(): pl.pallas_call(functools.partial(near_kernel, boxes * devices), out_shape...  7.16 us
    ppermute x3, starting transfers between devices, exchanged(): return lax.ppermute(value, axes, pairs)  5.26 us
    all_to_all x1, starting transfers between devices, on_device(): lax.all_to_all(outgoing, ('box', 'samp'), split_axis=0, concat_axis=0, ti...  4.84 us
    pallas_call x1, Pallas kernels, on_device(): pl.pallas_call(functools.partial(radiate_kernel, group), out_shape=jax.Sh...  4.59 us
    pallas_call x1, Pallas kernels, on_device(): pl.pallas_call(last_kernel, out_shape=jax.ShapeDtypeStruct((2 * boxes, pa...  3.81 us
    unnamed x8, local copies, waits for them, and re-layouts  3.03 us
    pallas_call x1, Pallas kernels, on_device(): pl.pallas_call(leaf_kernel, out_shape=jax.ShapeDtypeStruct((2 * boxes, wi...  2.77 us
  transfers between devices with their start and end apart: 4, of which 1 were waited for; matrix products, arithmetic and copies ran while one was open for 0% of the time, Pallas kernels for 56%

profile of v7, /device:TPU:0, one launch (start us, length us, event | category | flops | bytes accessed | tf_op | source)
XLA Modules:
  0.0 39.9 jit_solution(9330278993111412911)
XLA Ops:
  0.0 0.6 %collective-permute-start.1 = (bf16[32,128]{1,0:T(8,128)(2,1)}, bf16[32,128]{1,0:T(8,128)(2,1)S(1)}, u32[]{:S(2)}, u32[]{:S(2)}) collective-permute-start(bf16[32,128]{1,0:T(8,128)(2,1)} %bitcast.22), channel_id=1, source_target_pairs={{1,2},{2,1},{3,4},{4,3},{5,6},{6,5},{7,8},{8,7},{9,10},{10,9},{11,... | collective-permute-start | bytes 24584 | tf_op jit(solution)/shard_map/ppermute | solution.py:37
  0.7 4.5 %collective-permute-start = (bf16[32,128]{1,0:T(8,128)(2,1)}, bf16[32,128]{1,0:T(8,128)(2,1)S(1)}, u32[]{:S(2)}, u32[]{:S(2)}) collective-permute-start(bf16[32,128]{1,0:T(8,128)(2,1)} %bitcast.23), channel_id=1, source_target_pairs={{0,1},{1,0},{2,3},{3,2},{4,5},{5,4},{6,7},{7,6},{8,9},{9,8},{10,11... | collective-permute-start | bytes 24584 | tf_op jit(solution)/shard_map/ppermute | solution.py:37
  5.1 4.6 %shard_map.145 = bf16[32,64,128]{2,1,0:T(8,128)(2,1)} custom-call(bf16[32,128]{1,0:T(8,128)(2,1)} %bitcast.24, bf16[16,128,1024]{2,1,0:T(8,128)(2,1)} %radiate_ref.1, s32[4,32]{1,0:T(4,128)} %bitcast.26, bf16[512,2048]{1,0:T(8,128)(2,1)} %interp_hbm.3, f32[256,128]{1,0:T(8,128)} %bitcast.20), custom_call_target="tpu_custom_call" | custom-call | flops 1000000000 | bytes 8388608 | tf_op jit(solution)/shard_map/pallas_call | solution.py:543
  9.7 0.0 collective-permute-done.1.odd_ref
  9.7 0.0 collective-permute-done.even_ref
  9.7 4.8 %all-to-all-start = ((bf16[32,64,128]{2,1,0:T(8,128)(2,1)}), bf16[32,64,128]{2,1,0:T(8,128)(2,1)S(1)}, u32[]{:S(2)}, u32[]{:S(2)}) async-start(bf16[32,64,128]{2,1,0:T(8,128)(2,1)} %shard_map.145), calls=%async_computation | async-start | bytes 1048576 | tf_op jit(solution)/shard_map/all_to_all | solution.py:567
  14.6 7.2 %shard_map.146.near_ref = f32[32,128]{1,0:T(8,128)S(1)} custom-call(bf16[32,128]{1,0:T(8,128)(2,1)S(1)} %collective-permute-done.even_ref, bf16[32,128]{1,0:T(8,128)(2,1)} %bitcast.25, bf16[32,128]{1,0:T(8,128)(2,1)S(1)} %collective-permute-done.1.odd_ref, s32[16,27]{1,0:T(8,128)} %near_src_hbm.1, s32[16,27]{1,0:T(8,128)} %near_tile_hbm.1, ...), custom_call_target="tpu_custom_call" | custom-call | flops 10000000000 | bytes 16777216 | tf_op jit(solution)/shard_map/pallas_call | solution.py:573
  21.7 0.0 copy-start.3
  21.8 7.6 %shard_map.147 = (bf16[16,128,1024]{2,1,0:T(8,128)(2,1)}, f32[4,64,2048]{2,1,0:T(8,128)S(1)}) custom-call(s32[16,189]{1,0:T(8,128)} %slot_hbm.1, s32[16,189]{1,0:T(8,128)} %type_hbm, s32[16,189]{1,0:T(8,128)} %par_far_hbm.1, s32[16,189]{1,0:T(8,128)} %par_type_hbm.1, bf16[2528,128]{1,0:T(8,128)(2,1)} %bitcast.28, bf16[10112,128]{1,0:T(8,128)(2,1)} %bitcast.27), custom_call_target="tpu_custom_call" | custom-call | flops 1000000000 | bytes 16777216 | tf_op jit(solution)/shard_map/pallas_call | solution.py:595
  29.4 0.0 copy-start.1
  29.4 1.3 %copy-done.1 = f32[4,64,2048]{2,1,0:T(8,128)} copy-done((f32[4,64,2048]{2,1,0:T(8,128)}, f32[4,64,2048]{2,1,0:T(8,128)S(1)}, u32[]{:S(2)}) %copy-start.1) | copy-done | bytes 2097176
  30.7 0.0 copy-start
  30.7 0.2 all-to-all-done.arrived_ref
  30.9 0.0 copy-start.2
  30.9 1.7 %copy-done.2 = f32[4,64,2048]{2,1,0:T(8,128)S(1)} copy-done((f32[4,64,2048]{2,1,0:T(8,128)S(1)}, f32[4,64,2048]{2,1,0:T(8,128)}, u32[]{:S(2)}) %copy-start.2) | copy-done | bytes 2097176
  32.6 0.5 %shard_map.148 = (f32[32,128]{1,0:T(8,128)S(1)}, f32[32,128]{1,0:T(8,128)S(1)}) custom-call(bf16[32,64,128]{2,1,0:T(8,128)(2,1)S(1)} %all-to-all-done.arrived_ref, f32[4,64,2048]{2,1,0:T(8,128)S(1)} %copy-done.2), custom_call_target="tpu_custom_call" | custom-call | flops 100000000 | bytes 1048576 | tf_op jit(solution)/shard_map/pallas_call | solution.py:637
  33.1 0.2 collective-permute-start.2
  33.3 2.8 %shard_map.149.incoming_ref = f32[32,4,128]{2,1,0:T(4,128)S(1)} custom-call(bf16[16,128,1024]{2,1,0:T(8,128)(2,1)} %get-tuple-element.25.d_lo_hbm, bf16[32,64,128]{2,1,0:T(8,128)(2,1)S(1)} %all-to-all-done.arrived_ref), custom_call_target="tpu_custom_call" | custom-call | flops 1000000000 | bytes 5242880 | tf_op jit(solution)/shard_map/pallas_call | solution.py:648
  36.1 0.0 collective-permute-done.2.other_ref
  36.1 0.0 copy-done.3
  36.1 0.0 copy-done
  36.1 3.8 %shard_map.150 = f32[32,128]{1,0:T(8,128)} custom-call(f32[32,128]{1,0:T(8,128)S(1)} %get-tuple-element.21.mine_ref, f32[32,128]{1,0:T(8,128)S(1)} %collective-permute-done.2.other_ref, f32[32,4,128]{2,1,0:T(4,128)S(1)} %shard_map.149.incoming_ref, f32[256,128]{1,0:T(8,128)S(1)} %bitcast.21, bf16[512,2048]{1,0:T(8,128)(2,1)S(1)} %copy-done, ...), custom_call_target="tpu_custom_call" | custom-call | flops 1000000000 | bytes 8388608 | tf_op jit(solution)/shard_map/pallas_call | solution.py:664
Async XLA Ops:
  0.0 9.7 %collective-permute-start.1 = (bf16[32,128]{1,0:T(8,128)(2,1)}, bf16[32,128]{1,0:T(8,128)(2,1)S(1)}, u32[]{:S(2)}, u32[]{:S(2)}) collective-permute-start(bf16[32,128]{1,0:T(8,128)(2,1)} %bitcast.22), channel_id=1, source_target_pairs={{1,2},{2,1},{3,4},{4,3},{5,6},{6,5},{7,8},{8,7},{9,10},{10,9},{11,... | collective-permute-start | bytes 24584 | tf_op jit(solution)/shard_map/ppermute | solution.py:37
  0.7 9.1 %collective-permute-start = (bf16[32,128]{1,0:T(8,128)(2,1)}, bf16[32,128]{1,0:T(8,128)(2,1)S(1)}, u32[]{:S(2)}, u32[]{:S(2)}) collective-permute-start(bf16[32,128]{1,0:T(8,128)(2,1)} %bitcast.23), channel_id=1, source_target_pairs={{0,1},{1,0},{2,3},{3,2},{4,5},{5,4},{6,7},{7,6},{8,9},{9,8},{10,11... | collective-permute-start | bytes 24584 | tf_op jit(solution)/shard_map/ppermute | solution.py:37
  9.7 21.2 %all-to-all-start = ((bf16[32,64,128]{2,1,0:T(8,128)(2,1)}), bf16[32,64,128]{2,1,0:T(8,128)(2,1)S(1)}, u32[]{:S(2)}, u32[]{:S(2)}) async-start(bf16[32,64,128]{2,1,0:T(8,128)(2,1)} %shard_map.145), calls=%async_computation | async-start | bytes 1048576 | tf_op jit(solution)/shard_map/all_to_all | solution.py:567
  21.7 14.3 %copy-start.3 = (f32[8,2,2048]{2,1,0:T(2,128)S(1)}, f32[8,2,2048]{2,1,0:T(2,128)}, u32[]{:S(2)}) copy-start(f32[8,2,2048]{2,1,0:T(2,128)} %param.26) | copy-start | bytes 393220
  29.4 1.3 %copy-start.1 = (f32[4,64,2048]{2,1,0:T(8,128)}, f32[4,64,2048]{2,1,0:T(8,128)S(1)}, u32[]{:S(2)}) copy-start(f32[4,64,2048]{2,1,0:T(8,128)S(1)} %get-tuple-element.20.d_ref) | copy-start | bytes 6291460
  30.7 5.4 %copy-start = (bf16[512,2048]{1,0:T(8,128)(2,1)S(1)}, bf16[512,2048]{1,0:T(8,128)(2,1)}, u32[]{:S(2)}) copy-start(bf16[512,2048]{1,0:T(8,128)(2,1)} %interp_hbm.3) | copy-start | bytes 6291460
  30.9 1.7 %copy-start.2 = (f32[4,64,2048]{2,1,0:T(8,128)S(1)}, f32[4,64,2048]{2,1,0:T(8,128)}, u32[]{:S(2)}) copy-start(f32[4,64,2048]{2,1,0:T(8,128)} %copy-done.1) | copy-start | bytes 6291460
  33.1 2.9 %collective-permute-start.2 = (f32[32,128]{1,0:T(8,128)S(1)}, f32[32,128]{1,0:T(8,128)S(1)}, u32[]{:S(2)}, u32[]{:S(2)}) collective-permute-start(f32[32,128]{1,0:T(8,128)S(1)} %get-tuple-element.24), channel_id=1, source_target_pairs={{0,1},{1,0},{2,3},{3,2},{4,5},{5,4},{6,7},{7,6},{8,9},{9,8},{10,11... | collective-permute-start | bytes 49160 | tf_op jit(solution)/shard_map/ppermute | solution.py:37

commit v8 on v7

--- a/solution.py
+++ b/solution.py
@@ -155,7 +155,7 @@
     op_lo_hbm,
     op_hi_hbm,
     d_lo_hbm,
-    d_ref,
+    d_hi_hbm,
     slot_ref,
     type_ref,
     par_far_ref,
@@ -169,7 +169,9 @@
     op_hi,
     counts_hi,
     d_lo,
+    d_hi,
     sems,
+    hi_sems,
     extra,
 ):
     others = fetch(
@@ -185,7 +187,7 @@
     )
     boxes = slot_ref.shape[0]
     rows, far = par_far_ref.shape
-    parents, sources, _ = d_ref.shape
+    parents, sources, _ = d_hi.shape
     slot_total = d_lo.shape[1]
     type_pad = op_hi.shape[0]
     chunks = op_lo.shape[1] // (2 * LANE)
@@ -257,28 +259,38 @@
             start = place - base + 2 * k + c
             op_hi[:, col : col + LANE] = wide_hi[pl.ds(start, type_pad, stride=16), :].astype(BF16)
 
-    for first in range(0, 2 * share * LANE, 2 * LANE):
-        cols = slice(first, first + 2 * LANE)
-        d_ref[:, :, cols] = dot_nn(counts_hi[...], op_hi[:, cols]).reshape(
-            parents, sources, 2 * LANE
+    hi_copies = []
+    for step in range(share):
+        cols = slice(step * 2 * LANE, (step + 1) * 2 * LANE)
+        d_hi[:, :, cols] = (
+            dot_nn(counts_hi[...], op_hi[:, cols]).astype(BF16).reshape(parents, sources, 2 * LANE)
         )
+        hi_copies.append(
+            pltpu.make_async_copy(d_hi.at[:, :, cols], d_hi_hbm.at[:, :, cols], hi_sems.at[step])
+        )
+        hi_copies[-1].start()
+    for copy in hi_copies:
+        copy.wait()
     for step in range(boxes // batch):
         lo_copy(step).wait()
 
 
-def parent_kernel(lo_lines, arrived_ref, d_ref, mine_ref, theirs_ref, wide):
-    parents, sources, width = d_ref.shape
+def parent_kernel(lo_lines, arrived_ref, d_hi_hbm, mine_ref, theirs_ref, d_hi, wide, sems):
+    parents, sources, width = d_hi.shape
     share = width // (2 * LANE)
     own = parents // 2
     member = lax.rem(lax.axis_index("samp"), 2)
+    copies = fetch([(d_hi_hbm.at[p], d_hi.at[p]) for p in range(parents)], sems)
     wide[...] = arrived_ref[:, lo_lines:, :].astype(F32).reshape(wide.shape)
+    for copy in copies:
+        copy.wait()
     for k in range(share):
         first = wide[pl.ds(k, sources, stride=2 * share), :]
         second = wide[pl.ds(share + k, sources, stride=2 * share), :]
         for out_ref, start in ((theirs_ref, (1 - member) * own), (mine_ref, member * own)):
             for q in range(own):
-                o_re = d_ref[start + q, :, k * LANE : (k + 1) * LANE]
-                o_im = d_ref[start + q, :, (share + k) * LANE : (share + k + 1) * LANE]
+                o_re = d_hi[start + q, :, k * LANE : (k + 1) * LANE].astype(F32)
+                o_im = d_hi[start + q, :, (share + k) * LANE : (share + k + 1) * LANE].astype(F32)
                 row = q * 2 * share + k
                 out_ref[row : row + 1] = jnp.sum(o_re * first - o_im * second, 0, keepdims=True)
                 row += share
@@ -387,44 +399,11 @@
         near_ref[row : row + 2] = acc[g, 0:2] + 0.5 * dens3[pl.ds(2 * boxes + row, 2), :]
 
 
-def leaf_kernel(d_lo_hbm, arrived_ref, incoming_ref, d_lo, slots, received, sems):
-    boxes, slot_total, width = d_lo.shape
-    chunks = width // (2 * LANE)
-    steps = sems.shape[0]
-    per_boxes = boxes // steps
-    copies = []
-    for step in range(steps):
-        part = pl.ds(step * per_boxes, per_boxes)
-        copies.append(pltpu.make_async_copy(d_lo_hbm.at[part], d_lo.at[part], sems.at[step]))
-        copies[-1].start()
-    lo_lines = slots.shape[0] // arrived_ref.shape[0]
-    slots[...] = arrived_ref[:, :lo_lines, :].astype(F32).reshape(slots.shape)
-    for r in range(2 * chunks):
-        received[:, r * LANE : (r + 1) * LANE] = slots[pl.ds(r, slot_total, stride=2 * chunks), :]
-
-    def multiply_slots(r, g):
-        first = received[:, r * LANE : (r + 1) * LANE]
-        second = received[:, (chunks + r) * LANE : (chunks + r + 1) * LANE]
-        o_re = d_lo[g, :, r * LANE : (r + 1) * LANE].astype(F32)
-        o_im = d_lo[g, :, (chunks + r) * LANE : (chunks + r + 1) * LANE].astype(F32)
-        incoming_ref[g, r : r + 1] = jnp.sum(
-            o_re * first - o_im * second, 0, keepdims=True
-        )
-        incoming_ref[boxes + g, r : r + 1] = jnp.sum(
-            o_re * second + o_im * first, 0, keepdims=True
-        )
-
-    for step in range(steps):
-        copies[step].wait()
-        for r in range(chunks):
-            for k in range(per_boxes):
-                multiply_slots(r, step * per_boxes + k)
-
-
 def last_kernel(
     mine_ref,
     other_ref,
-    incoming_ref,
+    d_lo_hbm,
+    arrived_ref,
     shift_hbm,
     interp_hbm,
     receive_ref,
@@ -436,13 +415,26 @@
     parent_ref,
     down,
     blend,
+    d_lo,
+    slots,
+    received,
+    incoming_ref,
     sems,
+    lo_sems,
     extra,
 ):
-    boxes = receive.shape[0]
+    boxes, slot_total, width = d_lo.shape
+    chunks = width // (2 * LANE)
+    lo_steps = lo_sems.shape[0]
+    per_boxes = boxes // lo_steps
+    lo_copies = []
+    for step in range(lo_steps):
+        part = pl.ds(step * per_boxes, per_boxes)
+        lo_copies.append(pltpu.make_async_copy(d_lo_hbm.at[part], d_lo.at[part], lo_sems.at[step]))
+        lo_copies[-1].start()
+    others = fetch([(shift_hbm, shift_ref), (interp_hbm, interp_ref)], extra)
     per_step = 4
     steps = boxes // per_step
-    others = fetch([(shift_hbm, shift_ref), (interp_hbm, interp_ref)], extra)
     copies = []
     for step in range(steps):
         part = pl.ds(step * per_step, per_step)
@@ -453,7 +445,6 @@
     parent_ref[1 - member] = other_ref[...]
     own_parents = boxes // 8
     hi_chunks = down.shape[1] // LANE
-    chunks = incoming_ref.shape[1]
     share = hi_chunks // parent_ref.shape[0]
     others[0].wait()
     for r in range(hi_chunks):
@@ -468,6 +459,28 @@
             im_rows.append(s_re * t_im - s_im * t_re)
         cols = slice(r * LANE, (r + 1) * LANE)
         down[:, cols] = jnp.concatenate(re_rows + im_rows, 0).astype(BF16)
+    lo_lines = slots.shape[0] // arrived_ref.shape[0]
+    slots[...] = arrived_ref[:, :lo_lines, :].astype(F32).reshape(slots.shape)
+    for r in range(2 * chunks):
+        received[:, r * LANE : (r + 1) * LANE] = slots[pl.ds(r, slot_total, stride=2 * chunks), :]
+
+    def multiply_slots(r, g):
+        first = received[:, r * LANE : (r + 1) * LANE]
+        second = received[:, (chunks + r) * LANE : (chunks + r + 1) * LANE]
+        o_re = d_lo[g, :, r * LANE : (r + 1) * LANE].astype(F32)
+        o_im = d_lo[g, :, (chunks + r) * LANE : (chunks + r + 1) * LANE].astype(F32)
+        incoming_ref[g, r : r + 1] = jnp.sum(
+            o_re * first - o_im * second, 0, keepdims=True
+        )
+        incoming_ref[boxes + g, r : r + 1] = jnp.sum(
+            o_re * second + o_im * first, 0, keepdims=True
+        )
+
+    for step in range(lo_steps):
+        lo_copies[step].wait()
+        for r in range(chunks):
+            for k in range(per_boxes):
+                multiply_slots(r, step * per_boxes + k)
     others[1].wait()
     total = jnp.concatenate([incoming_ref[:, r, :] for r in range(chunks)], 1)
     total = total + dot_nt(down[...], interp_ref[...])
@@ -596,10 +609,10 @@
         functools.partial(index_kernel, types, group),
         out_shape=(
             pltpu.HBM((boxes, slot_total, 2 * width_lo), BF16),
-            pltpu.VMEM((parents * group, par_total, 2 * share * LANE), F32),
+            pltpu.HBM((parents * group, par_total, 2 * share * LANE), BF16),
         ),
         in_specs=[HBM_SPEC] * 6,
-        out_specs=(HBM_SPEC, VMEM_SPEC),
+        out_specs=(HBM_SPEC,) * 2,
         scratch_shapes=[
             pltpu.VMEM(far, jnp.int32),
             pltpu.VMEM(far, jnp.int32),
@@ -614,11 +627,13 @@
             pltpu.VMEM((type_pad, 2 * share * LANE), BF16),
             pltpu.VMEM((parents * group * par_total, type_pad), BF16),
             pltpu.VMEM((boxes, slot_total, 2 * width_lo), BF16),
+            pltpu.VMEM((parents * group, par_total, 2 * share * LANE), BF16),
             pltpu.SemaphoreType.DMA((boxes // 4,)),
+            pltpu.SemaphoreType.DMA((share,)),
             pltpu.SemaphoreType.DMA((6,)),
         ],
         compiler_params=pltpu.CompilerParams(
-            vmem_limit_bytes=(20 if slot_total <= 128 else 46) * MIB
+            vmem_limit_bytes=(28 if slot_total <= 128 else 52) * MIB
         ),
         cost_estimate=pl.CostEstimate(flops=10**9, bytes_accessed=16 * MIB, transcendentals=0),
     )(
@@ -637,34 +652,21 @@
     mine, theirs = pl.pallas_call(
         functools.partial(parent_kernel, lo_lines),
         out_shape=(jax.ShapeDtypeStruct((hi_lines, LANE), F32),) * 2,
-        in_specs=[VMEM_SPEC] * 2,
+        in_specs=[VMEM_SPEC, HBM_SPEC],
         out_specs=(VMEM_SPEC,) * 2,
-        scratch_shapes=[pltpu.VMEM((devices * hi_lines, LANE), F32)],
+        scratch_shapes=[
+            pltpu.VMEM((parents * group, par_total, 2 * share * LANE), BF16),
+            pltpu.VMEM((devices * hi_lines, LANE), F32),
+            pltpu.SemaphoreType.DMA((parents * group,)),
+        ],
         compiler_params=pltpu.CompilerParams(vmem_limit_bytes=8 * MIB),
         cost_estimate=pl.CostEstimate(flops=10**8, bytes_accessed=MIB, transcendentals=0),
-    )(arrived, in_vmem(d_hi))
-    theirs, d_lo = lax.optimization_barrier((theirs, d_lo))
+    )(arrived, in_hbm(d_hi))
     other = exchanged(theirs, both, 0)
-    incoming = pl.pallas_call(
-        leaf_kernel,
-        out_shape=jax.ShapeDtypeStruct((2 * boxes, width_lo // LANE, LANE), F32),
-        in_specs=[HBM_SPEC, VMEM_SPEC],
-        out_specs=VMEM_SPEC,
-        scratch_shapes=[
-            pltpu.VMEM((boxes, slot_total, 2 * width_lo), BF16),
-            pltpu.VMEM((devices * lo_lines, LANE), F32),
-            pltpu.VMEM((slot_total, 2 * width_lo), F32),
-            pltpu.SemaphoreType.DMA((boxes // 2,)),
-        ],
-        compiler_params=pltpu.CompilerParams(
-            vmem_limit_bytes=(10 if slot_total <= 128 else 32) * MIB
-        ),
-        cost_estimate=pl.CostEstimate(flops=10**9, bytes_accessed=5 * MIB, transcendentals=0),
-    )(in_hbm(d_lo), arrived)
     field = pl.pallas_call(
         last_kernel,
         out_shape=jax.ShapeDtypeStruct((2 * boxes, panels), F32),
-        in_specs=[VMEM_SPEC] * 3 + [HBM_SPEC] * 3 + [VMEM_SPEC],
+        in_specs=[VMEM_SPEC] * 2 + [HBM_SPEC, VMEM_SPEC] + [HBM_SPEC] * 3 + [VMEM_SPEC],
         out_specs=VMEM_SPEC,
         scratch_shapes=[
             pltpu.VMEM(receive.shape, BF16),
@@ -673,12 +675,28 @@
             pltpu.VMEM((group, hi_lines, LANE), F32),
             pltpu.VMEM((2 * boxes, width_hi), BF16),
             pltpu.VMEM((2 * boxes, 2 * width_lo // LANE, LANE), F32),
+            pltpu.VMEM((boxes, slot_total, 2 * width_lo), BF16),
+            pltpu.VMEM((devices * lo_lines, LANE), F32),
+            pltpu.VMEM((slot_total, 2 * width_lo), F32),
+            pltpu.VMEM((2 * boxes, width_lo // LANE, LANE), F32),
             pltpu.SemaphoreType.DMA((boxes // 4,)),
+            pltpu.SemaphoreType.DMA((boxes // 2,)),
             pltpu.SemaphoreType.DMA((2,)),
         ],
-        compiler_params=pltpu.CompilerParams(vmem_limit_bytes=12 * MIB),
-        cost_estimate=pl.CostEstimate(flops=10**9, bytes_accessed=8 * MIB, transcendentals=0),
-    )(mine, other, incoming, shift_rows, interp_matrix, in_hbm(receive), near)
+        compiler_params=pltpu.CompilerParams(
+            vmem_limit_bytes=(22 if slot_total <= 128 else 40) * MIB
+        ),
+        cost_estimate=pl.CostEstimate(flops=10**9, bytes_accessed=12 * MIB, transcendentals=0),
+    )(
+        mine,
+        other,
+        in_hbm(d_lo),
+        arrived,
+        in_hbm(shift_rows),
+        in_hbm(interp_matrix),
+        in_hbm(receive),
+        near,
+    )
     return field.reshape(boxes, 2, panels)
 
 

time: 40.3 us -> 41.9 us (1.040)
  Pallas kernels: 26.5 us -> 29.6 us
  local copies, waits for them, and re-layouts: 3.03 us -> 0 us
  waiting for transfers between devices: 0.21 us -> 1.93 us
    pallas_call x1, Pallas kernels: 3.81 us -> 7.66 us  [on_device(): pl.pallas_call(last_kernel, out_shape=jax.ShapeDtypeStruct((2 * boxes, pa...]
    unnamed x8 -> x0, local copies, waits for them, and re-layouts: 3.03 us -> none
    pallas_call x1 -> x0, Pallas kernels: 2.77 us -> none  [on_device(): pl.pallas_call(leaf_kernel, out_shape=jax.ShapeDtypeStruct((2 * boxes, wi...]
    pallas_call x1, Pallas kernels: 0.49 us -> 1.73 us  [on_device(): pl.pallas_call(functools.partial(parent_kernel, lo_lines), out_shape=(jax...]
    ppermute x3, waiting for transfers between devices: 0.01 us -> 1.18 us  [exchanged(): return lax.ppermute(value, axes, pairs)]
    pallas_call x1, Pallas kernels: 7.63 us -> 8.43 us  [on_device(): pl.pallas_call(functools.partial(index_kernel, types, group), out_shape=(...]
    all_to_all x1, waiting for transfers between devices: 0.2 us -> 0.75 us  [on_device(): lax.all_to_all(outgoing, ('box', 'samp'), split_axis=0, concat_axis=0, ti...]
  transfers between devices with their start and end apart: 4 -> 4, of which waited for: 1 -> 2; matrix products, arithmetic and copies ran while one was open for 0% -> 0% of each run, Pallas kernels for 56% -> 48%
where the time goes in v8:
time: 41.9 us; the launch traced here: 41.6 us
  Pallas kernels  29.6 us (71%)
  starting transfers between devices  10 us (24%)
  waiting for transfers between devices  1.93 us (5%)
    pallas_call x1, Pallas kernels, on_device(): pl.pallas_call(functools.partial(index_kernel, types, group), out_shape=(...  8.43 us
    pallas_call x1, Pallas kernels, on_device(): pl.pallas_call(last_kernel, out_shape=jax.ShapeDtypeStruct((2 * boxes, pa...  7.66 us
    pallas_call x1, Pallas kernels, on_device(): pl.pallas_call(functools.partial(near_kernel, boxes * devices), out_shape...  7.16 us
    ppermute x3, starting transfers between devices, exchanged(): return lax.ppermute(value, axes, pairs)  5.18 us
    all_to_all x1, starting transfers between devices, on_device(): lax.all_to_all(outgoing, ('box', 'samp'), split_axis=0, concat_axis=0, ti...  4.84 us
    pallas_call x1, Pallas kernels, on_device(): pl.pallas_call(functools.partial(radiate_kernel, group), out_shape=jax.Sh...  4.58 us
    pallas_call x1, Pallas kernels, on_device(): pl.pallas_call(functools.partial(parent_kernel, lo_lines), out_shape=(jax...  1.73 us
    ppermute x3, waiting for transfers between devices, exchanged(): return lax.ppermute(value, axes, pairs)  1.18 us
  transfers between devices with their start and end apart: 4, of which 2 were waited for; matrix products, arithmetic and copies ran while one was open for 0% of the time, Pallas kernels for 48%

profile of v8, /device:TPU:0, one launch (start us, length us, event | category | flops | bytes accessed | tf_op | source)
XLA Modules:
  0.0 41.6 jit_solution(10398942614342453059)
XLA Ops:
  0.0 0.6 %collective-permute-start.1 = (bf16[32,128]{1,0:T(8,128)(2,1)}, bf16[32,128]{1,0:T(8,128)(2,1)S(1)}, u32[]{:S(2)}, u32[]{:S(2)}) collective-permute-start(bf16[32,128]{1,0:T(8,128)(2,1)} %bitcast.22), channel_id=1, source_target_pairs={{1,2},{2,1},{3,4},{4,3},{5,6},{6,5},{7,8},{8,7},{9,10},{10,9},{11,... | collective-permute-start | bytes 24584 | tf_op jit(solution)/shard_map/ppermute | solution.py:37
  0.7 4.5 %collective-permute-start = (bf16[32,128]{1,0:T(8,128)(2,1)}, bf16[32,128]{1,0:T(8,128)(2,1)S(1)}, u32[]{:S(2)}, u32[]{:S(2)}) collective-permute-start(bf16[32,128]{1,0:T(8,128)(2,1)} %bitcast.23), channel_id=1, source_target_pairs={{0,1},{1,0},{2,3},{3,2},{4,5},{5,4},{6,7},{7,6},{8,9},{9,8},{10,11... | collective-permute-start | bytes 24584 | tf_op jit(solution)/shard_map/ppermute | solution.py:37
  5.1 4.6 %shard_map.145 = bf16[32,64,128]{2,1,0:T(8,128)(2,1)} custom-call(bf16[32,128]{1,0:T(8,128)(2,1)} %bitcast.24, bf16[16,128,1024]{2,1,0:T(8,128)(2,1)} %radiate_ref.1, s32[4,32]{1,0:T(4,128)} %bitcast.26, bf16[512,2048]{1,0:T(8,128)(2,1)} %interp_hbm.3, f32[256,128]{1,0:T(8,128)} %bitcast.20), custom_call_target="tpu_custom_call" | custom-call | flops 1000000000 | bytes 8388608 | tf_op jit(solution)/shard_map/pallas_call | solution.py:556
  9.7 0.0 collective-permute-done.1.odd_ref
  9.7 0.0 collective-permute-done.even_ref
  9.7 4.8 %all-to-all-start = ((bf16[32,64,128]{2,1,0:T(8,128)(2,1)}), bf16[32,64,128]{2,1,0:T(8,128)(2,1)S(1)}, u32[]{:S(2)}, u32[]{:S(2)}) async-start(bf16[32,64,128]{2,1,0:T(8,128)(2,1)} %shard_map.145), calls=%async_computation | async-start | bytes 1048576 | tf_op jit(solution)/shard_map/all_to_all | solution.py:580
  14.6 7.2 %shard_map.146.near_ref = f32[32,128]{1,0:T(8,128)S(1)} custom-call(bf16[32,128]{1,0:T(8,128)(2,1)S(1)} %collective-permute-done.even_ref, bf16[32,128]{1,0:T(8,128)(2,1)} %bitcast.25, bf16[32,128]{1,0:T(8,128)(2,1)S(1)} %collective-permute-done.1.odd_ref, s32[16,27]{1,0:T(8,128)} %near_src_hbm.1, s32[16,27]{1,0:T(8,128)} %near_tile_hbm.1, ...), custom_call_target="tpu_custom_call" | custom-call | flops 10000000000 | bytes 16777216 | tf_op jit(solution)/shard_map/pallas_call | solution.py:586
  21.7 8.4 %shard_map.147 = (bf16[16,128,1024]{2,1,0:T(8,128)(2,1)}, bf16[4,64,2048]{2,1,0:T(8,128)(2,1)}) custom-call(s32[16,189]{1,0:T(8,128)} %slot_hbm.1, s32[16,189]{1,0:T(8,128)} %type_hbm, s32[16,189]{1,0:T(8,128)} %par_far_hbm.1, s32[16,189]{1,0:T(8,128)} %par_type_hbm.1, bf16[2528,128]{1,0:T(8,128)(2,1)} %bitcast.28, bf16[10112,128]{1,0:T(8,128)(2,1)} %bitcast.27), custom_call_target="tpu_custom_call" | custom-call | flops 1000000000 | bytes 16777216 | tf_op jit(solution)/shard_map/pallas_call | solution.py:608
  30.2 0.7 %all-to-all-done.arrived_ref = bf16[32,64,128]{2,1,0:T(8,128)(2,1)S(1)} async-done(((bf16[32,64,128]{2,1,0:T(8,128)(2,1)}), bf16[32,64,128]{2,1,0:T(8,128)(2,1)S(1)}, u32[]{:S(2)}, u32[]{:S(2)}) %all-to-all-start) | async-done | bytes 524320 | tf_op jit(solution)/shard_map/all_to_all | solution.py:580
  30.9 1.7 %shard_map.148 = (f32[32,128]{1,0:T(8,128)S(1)}, f32[32,128]{1,0:T(8,128)S(1)}) custom-call(bf16[32,64,128]{2,1,0:T(8,128)(2,1)S(1)} %all-to-all-done.arrived_ref, bf16[4,64,2048]{2,1,0:T(8,128)(2,1)} %get-tuple-element.18.d_hi_hbm), custom_call_target="tpu_custom_call" | custom-call | flops 100000000 | bytes 1048576 | tf_op jit(solution)/shard_map/pallas_call | solution.py:652
  32.7 0.1 collective-permute-start.2
  32.7 1.2 %collective-permute-done.2.other_ref = f32[32,128]{1,0:T(8,128)S(1)} collective-permute-done((f32[32,128]{1,0:T(8,128)S(1)}, f32[32,128]{1,0:T(8,128)S(1)}, u32[]{:S(2)}, u32[]{:S(2)}) %collective-permute-start.2) | collective-permute-done | bytes 16416 | tf_op jit(solution)/shard_map/ppermute | solution.py:37
  33.9 7.7 %shard_map.149 = f32[32,128]{1,0:T(8,128)} custom-call(f32[32,128]{1,0:T(8,128)S(1)} %get-tuple-element.19.mine_ref, f32[32,128]{1,0:T(8,128)S(1)} %collective-permute-done.2.other_ref, bf16[16,128,1024]{2,1,0:T(8,128)(2,1)} %get-tuple-element.21.d_lo_hbm, bf16[32,64,128]{2,1,0:T(8,128)(2,1)S(1)} %all-to-all-done.arrived_ref, f32[256,128]{1,0:T(8,128)} %bitcast.21, ...), custom_call_target="tpu_custom_call" | custom-call | flops 1000000000 | bytes 12582912 | tf_op jit(solution)/shard_map/pallas_call | solution.py:666
Async XLA Ops:
  0.0 9.7 %collective-permute-start.1 = (bf16[32,128]{1,0:T(8,128)(2,1)}, bf16[32,128]{1,0:T(8,128)(2,1)S(1)}, u32[]{:S(2)}, u32[]{:S(2)}) collective-permute-start(bf16[32,128]{1,0:T(8,128)(2,1)} %bitcast.22), channel_id=1, source_target_pairs={{1,2},{2,1},{3,4},{4,3},{5,6},{6,5},{7,8},{8,7},{9,10},{10,9},{11,... | collective-permute-start | bytes 24584 | tf_op jit(solution)/shard_map/ppermute | solution.py:37
  0.7 9.1 %collective-permute-start = (bf16[32,128]{1,0:T(8,128)(2,1)}, bf16[32,128]{1,0:T(8,128)(2,1)S(1)}, u32[]{:S(2)}, u32[]{:S(2)}) collective-permute-start(bf16[32,128]{1,0:T(8,128)(2,1)} %bitcast.23), channel_id=1, source_target_pairs={{0,1},{1,0},{2,3},{3,2},{4,5},{5,4},{6,7},{7,6},{8,9},{9,8},{10,11... | collective-permute-start | bytes 24584 | tf_op jit(solution)/shard_map/ppermute | solution.py:37
  9.7 21.2 %all-to-all-start = ((bf16[32,64,128]{2,1,0:T(8,128)(2,1)}), bf16[32,64,128]{2,1,0:T(8,128)(2,1)S(1)}, u32[]{:S(2)}, u32[]{:S(2)}) async-start(bf16[32,64,128]{2,1,0:T(8,128)(2,1)} %shard_map.145), calls=%async_computation | async-start | bytes 1048576 | tf_op jit(solution)/shard_map/all_to_all | solution.py:580
  32.7 1.2 %collective-permute-start.2 = (f32[32,128]{1,0:T(8,128)S(1)}, f32[32,128]{1,0:T(8,128)S(1)}, u32[]{:S(2)}, u32[]{:S(2)}) collective-permute-start(f32[32,128]{1,0:T(8,128)S(1)} %get-tuple-element.20), channel_id=1, source_target_pairs={{0,1},{1,0},{2,3},{3,2},{4,5},{5,4},{6,7},{7,6},{8,9},{9,8},{10,11... | collective-permute-start | bytes 49160 | tf_op jit(solution)/shard_map/ppermute | solution.py:37

commit v9 on v7

--- a/solution.py
+++ b/solution.py
@@ -259,8 +259,8 @@
 
     for first in range(0, 2 * share * LANE, 2 * LANE):
         cols = slice(first, first + 2 * LANE)
-        d_ref[:, :, cols] = dot_nn(counts_hi[...], op_hi[:, cols]).reshape(
-            parents, sources, 2 * LANE
+        d_ref[:, :, cols] = (
+            dot_nn(counts_hi[...], op_hi[:, cols]).astype(BF16).reshape(parents, sources, 2 * LANE)
         )
     for step in range(boxes // batch):
         lo_copy(step).wait()
@@ -277,8 +277,8 @@
         second = wide[pl.ds(share + k, sources, stride=2 * share), :]
         for out_ref, start in ((theirs_ref, (1 - member) * own), (mine_ref, member * own)):
             for q in range(own):
-                o_re = d_ref[start + q, :, k * LANE : (k + 1) * LANE]
-                o_im = d_ref[start + q, :, (share + k) * LANE : (share + k + 1) * LANE]
+                o_re = d_ref[start + q, :, k * LANE : (k + 1) * LANE].astype(F32)
+                o_im = d_ref[start + q, :, (share + k) * LANE : (share + k + 1) * LANE].astype(F32)
                 row = q * 2 * share + k
                 out_ref[row : row + 1] = jnp.sum(o_re * first - o_im * second, 0, keepdims=True)
                 row += share
@@ -596,7 +596,7 @@
         functools.partial(index_kernel, types, group),
         out_shape=(
             pltpu.HBM((boxes, slot_total, 2 * width_lo), BF16),
-            pltpu.VMEM((parents * group, par_total, 2 * share * LANE), F32),
+            pltpu.VMEM((parents * group, par_total, 2 * share * LANE), BF16),
         ),
         in_specs=[HBM_SPEC] * 6,
         out_specs=(HBM_SPEC, VMEM_SPEC),
@@ -678,7 +678,15 @@
         ],
         compiler_params=pltpu.CompilerParams(vmem_limit_bytes=12 * MIB),
         cost_estimate=pl.CostEstimate(flops=10**9, bytes_accessed=8 * MIB, transcendentals=0),
-    )(mine, other, incoming, shift_rows, interp_matrix, in_hbm(receive), near)
+    )(
+        mine,
+        other,
+        incoming,
+        in_hbm(shift_rows),
+        in_hbm(interp_matrix),
+        in_hbm(receive),
+        near,
+    )
     return field.reshape(boxes, 2, panels)
 
 

time: 40.3 us -> 40.5 us (level)
  local copies, waits for them, and re-layouts: 3.03 us -> 0 us
  Pallas kernels: 26.5 us -> 28.3 us
  waiting for transfers between devices: 0.21 us -> 1.59 us
    unnamed x8 -> x0, local copies, waits for them, and re-layouts: 3.03 us -> none
    pallas_call x1, Pallas kernels: 3.81 us -> 5.7 us  [on_device(): pl.pallas_call(last_kernel, out_shape=jax.ShapeDtypeStruct((2 * boxes, pa...]
    all_to_all x1, waiting for transfers between devices: 0.2 us -> 1.58 us  [on_device(): lax.all_to_all(outgoing, ('box', 'samp'), split_axis=0, concat_axis=0, ti...]
  transfers between devices with their start and end apart: 4 -> 4, of which waited for: 1 -> 1; matrix products, arithmetic and copies ran while one was open for 0% -> 0% of each run, Pallas kernels for 56% -> 55%
where the time goes in v9:
time: 40.5 us; the launch traced here: 40 us
  Pallas kernels  28.3 us (70%)
  starting transfers between devices  10 us (25%)
  waiting for transfers between devices  1.59 us (4%)
    pallas_call x1, Pallas kernels, on_device(): pl.pallas_call(functools.partial(index_kernel, types, group), out_shape=(...  7.59 us
    pallas_call x1, Pallas kernels, on_device(): pl.pallas_call(functools.partial(near_kernel, boxes * devices), out_shape...  7.16 us
    pallas_call x1, Pallas kernels, on_device(): pl.pallas_call(last_kernel, out_shape=jax.ShapeDtypeStruct((2 * boxes, pa...  5.7 us
    ppermute x3, starting transfers between devices, exchanged(): return lax.ppermute(value, axes, pairs)  5.18 us
    all_to_all x1, starting transfers between devices, on_device(): lax.all_to_all(outgoing, ('box', 'samp'), split_axis=0, concat_axis=0, ti...  4.84 us
    pallas_call x1, Pallas kernels, on_device(): pl.pallas_call(functools.partial(radiate_kernel, group), out_shape=jax.Sh...  4.57 us
    pallas_call x1, Pallas kernels, on_device(): pl.pallas_call(leaf_kernel, out_shape=jax.ShapeDtypeStruct((2 * boxes, wi...  2.78 us
    all_to_all x1, waiting for transfers between devices, on_device(): lax.all_to_all(outgoing, ('box', 'samp'), split_axis=0, concat_axis=0, ti...  1.58 us
  transfers between devices with their start and end apart: 4, of which 1 were waited for; matrix products, arithmetic and copies ran while one was open for 0% of the time, Pallas kernels for 55%

profile of v9, /device:TPU:0, one launch (start us, length us, event | category | flops | bytes accessed | tf_op | source)
XLA Modules:
  0.0 40.0 jit_solution(10985340675467735724)
XLA Ops:
  0.0 0.6 %collective-permute-start.1 = (bf16[32,128]{1,0:T(8,128)(2,1)}, bf16[32,128]{1,0:T(8,128)(2,1)S(1)}, u32[]{:S(2)}, u32[]{:S(2)}) collective-permute-start(bf16[32,128]{1,0:T(8,128)(2,1)} %bitcast.22), channel_id=1, source_target_pairs={{1,2},{2,1},{3,4},{4,3},{5,6},{6,5},{7,8},{8,7},{9,10},{10,9},{11,... | collective-permute-start | bytes 24584 | tf_op jit(solution)/shard_map/ppermute | solution.py:37
  0.7 4.5 %collective-permute-start = (bf16[32,128]{1,0:T(8,128)(2,1)}, bf16[32,128]{1,0:T(8,128)(2,1)S(1)}, u32[]{:S(2)}, u32[]{:S(2)}) collective-permute-start(bf16[32,128]{1,0:T(8,128)(2,1)} %bitcast.23), channel_id=1, source_target_pairs={{0,1},{1,0},{2,3},{3,2},{4,5},{5,4},{6,7},{7,6},{8,9},{9,8},{10,11... | collective-permute-start | bytes 24584 | tf_op jit(solution)/shard_map/ppermute | solution.py:37
  5.1 4.6 %shard_map.145 = bf16[32,64,128]{2,1,0:T(8,128)(2,1)} custom-call(bf16[32,128]{1,0:T(8,128)(2,1)} %bitcast.24, bf16[16,128,1024]{2,1,0:T(8,128)(2,1)} %radiate_ref.1, s32[4,32]{1,0:T(4,128)} %bitcast.26, bf16[512,2048]{1,0:T(8,128)(2,1)} %interp_hbm.3, f32[256,128]{1,0:T(8,128)} %bitcast.20), custom_call_target="tpu_custom_call" | custom-call | flops 1000000000 | bytes 8388608 | tf_op jit(solution)/shard_map/pallas_call | solution.py:543
  9.7 0.0 collective-permute-done.1.odd_ref
  9.7 0.0 collective-permute-done.even_ref
  9.7 4.8 %all-to-all-start = ((bf16[32,64,128]{2,1,0:T(8,128)(2,1)}), bf16[32,64,128]{2,1,0:T(8,128)(2,1)S(1)}, u32[]{:S(2)}, u32[]{:S(2)}) async-start(bf16[32,64,128]{2,1,0:T(8,128)(2,1)} %shard_map.145), calls=%async_computation | async-start | bytes 1048576 | tf_op jit(solution)/shard_map/all_to_all | solution.py:567
  14.6 7.2 %shard_map.146.near_ref = f32[32,128]{1,0:T(8,128)S(1)} custom-call(bf16[32,128]{1,0:T(8,128)(2,1)S(1)} %collective-permute-done.even_ref, bf16[32,128]{1,0:T(8,128)(2,1)} %bitcast.25, bf16[32,128]{1,0:T(8,128)(2,1)S(1)} %collective-permute-done.1.odd_ref, s32[16,27]{1,0:T(8,128)} %near_src_hbm.1, s32[16,27]{1,0:T(8,128)} %near_tile_hbm.1, ...), custom_call_target="tpu_custom_call" | custom-call | flops 10000000000 | bytes 16777216 | tf_op jit(solution)/shard_map/pallas_call | solution.py:573
  21.7 7.6 %shard_map.147 = (bf16[16,128,1024]{2,1,0:T(8,128)(2,1)}, bf16[4,64,2048]{2,1,0:T(8,128)(2,1)S(1)}) custom-call(s32[16,189]{1,0:T(8,128)} %slot_hbm.1, s32[16,189]{1,0:T(8,128)} %type_hbm, s32[16,189]{1,0:T(8,128)} %par_far_hbm.1, s32[16,189]{1,0:T(8,128)} %par_type_hbm.1, bf16[2528,128]{1,0:T(8,128)(2,1)} %bitcast.28, bf16[10112,128]{1,0:T(8,128)(2,1)} %bitcast.27), custom_call_target="tpu_custom_call" | custom-call | flops 1000000000 | bytes 16777216 | tf_op jit(solution)/shard_map/pallas_call | solution.py:595
  29.3 1.6 %all-to-all-done.arrived_ref = bf16[32,64,128]{2,1,0:T(8,128)(2,1)S(1)} async-done(((bf16[32,64,128]{2,1,0:T(8,128)(2,1)}), bf16[32,64,128]{2,1,0:T(8,128)(2,1)S(1)}, u32[]{:S(2)}, u32[]{:S(2)}) %all-to-all-start) | async-done | bytes 524320 | tf_op jit(solution)/shard_map/all_to_all | solution.py:567
  30.9 0.5 %shard_map.148 = (f32[32,128]{1,0:T(8,128)S(1)}, f32[32,128]{1,0:T(8,128)S(1)}) custom-call(bf16[32,64,128]{2,1,0:T(8,128)(2,1)S(1)} %all-to-all-done.arrived_ref, bf16[4,64,2048]{2,1,0:T(8,128)(2,1)S(1)} %get-tuple-element.20.d_ref), custom_call_target="tpu_custom_call" | custom-call | flops 100000000 | bytes 1048576 | tf_op jit(solution)/shard_map/pallas_call | solution.py:637
  31.5 0.1 collective-permute-start.2
  31.5 2.8 %shard_map.149.incoming_ref = f32[32,4,128]{2,1,0:T(4,128)S(1)} custom-call(bf16[16,128,1024]{2,1,0:T(8,128)(2,1)} %get-tuple-element.25.d_lo_hbm, bf16[32,64,128]{2,1,0:T(8,128)(2,1)S(1)} %all-to-all-done.arrived_ref), custom_call_target="tpu_custom_call" | custom-call | flops 1000000000 | bytes 5242880 | tf_op jit(solution)/shard_map/pallas_call | solution.py:648
  34.3 0.0 collective-permute-done.2.other_ref
  34.3 5.7 %shard_map.150 = f32[32,128]{1,0:T(8,128)} custom-call(f32[32,128]{1,0:T(8,128)S(1)} %get-tuple-element.21.mine_ref, f32[32,128]{1,0:T(8,128)S(1)} %collective-permute-done.2.other_ref, f32[32,4,128]{2,1,0:T(4,128)S(1)} %shard_map.149.incoming_ref, f32[256,128]{1,0:T(8,128)} %bitcast.21, bf16[512,2048]{1,0:T(8,128)(2,1)} %interp_hbm.3, ...), custom_call_target="tpu_custom_call" | custom-call | flops 1000000000 | bytes 8388608 | tf_op jit(solution)/shard_map/pallas_call | solution.py:664
Async XLA Ops:
  0.0 9.7 %collective-permute-start.1 = (bf16[32,128]{1,0:T(8,128)(2,1)}, bf16[32,128]{1,0:T(8,128)(2,1)S(1)}, u32[]{:S(2)}, u32[]{:S(2)}) collective-permute-start(bf16[32,128]{1,0:T(8,128)(2,1)} %bitcast.22), channel_id=1, source_target_pairs={{1,2},{2,1},{3,4},{4,3},{5,6},{6,5},{7,8},{8,7},{9,10},{10,9},{11,... | collective-permute-start | bytes 24584 | tf_op jit(solution)/shard_map/ppermute | solution.py:37
  0.7 9.0 %collective-permute-start = (bf16[32,128]{1,0:T(8,128)(2,1)}, bf16[32,128]{1,0:T(8,128)(2,1)S(1)}, u32[]{:S(2)}, u32[]{:S(2)}) collective-permute-start(bf16[32,128]{1,0:T(8,128)(2,1)} %bitcast.23), channel_id=1, source_target_pairs={{0,1},{1,0},{2,3},{3,2},{4,5},{5,4},{6,7},{7,6},{8,9},{9,8},{10,11... | collective-permute-start | bytes 24584 | tf_op jit(solution)/shard_map/ppermute | solution.py:37
  9.7 21.2 %all-to-all-start = ((bf16[32,64,128]{2,1,0:T(8,128)(2,1)}), bf16[32,64,128]{2,1,0:T(8,128)(2,1)S(1)}, u32[]{:S(2)}, u32[]{:S(2)}) async-start(bf16[32,64,128]{2,1,0:T(8,128)(2,1)} %shard_map.145), calls=%async_computation | async-start | bytes 1048576 | tf_op jit(solution)/shard_map/all_to_all | solution.py:567
  31.5 2.9 %collective-permute-start.2 = (f32[32,128]{1,0:T(8,128)S(1)}, f32[32,128]{1,0:T(8,128)S(1)}, u32[]{:S(2)}, u32[]{:S(2)}) collective-permute-start(f32[32,128]{1,0:T(8,128)S(1)} %get-tuple-element.24), channel_id=1, source_target_pairs={{0,1},{1,0},{2,3},{3,2},{4,5},{5,4},{6,7},{7,6},{8,9},{9,8},{10,11... | collective-permute-start | bytes 49160 | tf_op jit(solution)/shard_map/ppermute | solution.py:37

commit v10 on v9

--- a/solution.py
+++ b/solution.py
@@ -75,14 +75,18 @@
     for step in range(steps):
         part = pl.ds(step * per_step, per_step)
         copies.append(pltpu.make_async_copy(radiate_ref.at[part], rad.at[part], sems.at[step]))
-        copies[-1].start()
-    others += fetch([(interp_hbm, interp_ref)], extra, 3)
+    for copy in copies[:2]:
+        copy.start()
     others[0].wait()
     dens = dens_ref[...].astype(F32)
     owner = (iota(dens.shape, 0) // 2) % per_step
     blocks = jnp.concatenate([jnp.where(owner == b, dens, 0.0) for b in range(per_step)], 1)
     for step in range(steps):
         copies[step].wait()
+        if step + 2 < steps:
+            copies[step + 2].start()
+        if step == steps - 2:
+            others += fetch([(interp_hbm, interp_ref)], extra, 3)
         rows = slice(step * 2 * per_step, (step + 1) * 2 * per_step)
         weights = rad[step * per_step : (step + 1) * per_step].reshape(per_step * LANE, 2 * width)
         summed[rows] = dot_nn(blocks[rows].astype(BF16), weights).reshape(
@@ -328,7 +332,8 @@
         part = pl.ds(step * per_step, per_step)
         return pltpu.make_async_copy(tiles_hbm.at[part], tiles.at[part], sems.at[step])
 
-    for step in range(steps):
+    ahead = min(3, steps)
+    for step in range(ahead):
         tile_copy(step).start()
     acc[...] = jnp.zeros(acc.shape, F32)
     left[...] = jnp.zeros(left.shape, F32)
@@ -377,6 +382,11 @@
 
     def step_tiles(step, carry):
         tile_copy(step).wait()
+
+        @pl.when(step + ahead < steps)
+        def _():
+            tile_copy(step + ahead).start()
+
         for pair in range(per_step // 2):
             multiply_pair(step * per_step + 2 * pair)
         return carry
@@ -396,7 +406,8 @@
     for step in range(steps):
         part = pl.ds(step * per_boxes, per_boxes)
         copies.append(pltpu.make_async_copy(d_lo_hbm.at[part], d_lo.at[part], sems.at[step]))
-        copies[-1].start()
+    for copy in copies[:3]:
+        copy.start()
     lo_lines = slots.shape[0] // arrived_ref.shape[0]
     slots[...] = arrived_ref[:, :lo_lines, :].astype(F32).reshape(slots.shape)
     for r in range(2 * chunks):
@@ -416,6 +427,8 @@
 
     for step in range(steps):
         copies[step].wait()
+        if step + 3 < steps:
+            copies[step + 3].start()
         for r in range(chunks):
             for k in range(per_boxes):
                 multiply_slots(r, step * per_boxes + k)
@@ -447,7 +460,6 @@
     for step in range(steps):
         part = pl.ds(step * per_step, per_step)
         copies.append(pltpu.make_async_copy(receive_ref.at[part], receive.at[part], sems.at[step]))
-        copies[-1].start()
     member = lax.rem(lax.axis_index("samp"), 2)
     parent_ref[member] = mine_ref[...]
     parent_ref[1 - member] = other_ref[...]
@@ -469,6 +481,8 @@
         cols = slice(r * LANE, (r + 1) * LANE)
         down[:, cols] = jnp.concatenate(re_rows + im_rows, 0).astype(BF16)
     others[1].wait()
+    for copy in copies:
+        copy.start()
     total = jnp.concatenate([incoming_ref[:, r, :] for r in range(chunks)], 1)
     total = total + dot_nt(down[...], interp_ref[...])
     total = total.astype(BF16).astype(F32)

time: 40.5 us -> 42.2 us (1.042)
  Pallas kernels: 28.3 us -> 30.1 us
    pallas_call x1, Pallas kernels: 4.57 us -> 5.86 us  [on_device(): pl.pallas_call(functools.partial(radiate_kernel, group), out_shape=jax.Sh...]
    pallas_call x1, Pallas kernels: 2.78 us -> 3.76 us  [on_device(): pl.pallas_call(leaf_kernel, out_shape=jax.ShapeDtypeStruct((2 * boxes, wi...]
    pallas_call x1, Pallas kernels: 5.7 us -> 5.17 us  [on_device(): pl.pallas_call(last_kernel, out_shape=jax.ShapeDtypeStruct((2 * boxes, pa...]
  transfers between devices with their start and end apart: 4 -> 4, of which waited for: 1 -> 1; matrix products, arithmetic and copies ran while one was open for 0% -> 0% of each run, Pallas kernels for 55% -> 58%
where the time goes in v10:
time: 42.2 us; the launch traced here: 41.8 us
  Pallas kernels  30.1 us (71%)
  starting transfers between devices  10 us (24%)
  waiting for transfers between devices  1.59 us (4%)
    pallas_call x1, Pallas kernels, on_device(): pl.pallas_call(functools.partial(index_kernel, types, group), out_shape=(...  7.59 us
    pallas_call x1, Pallas kernels, on_device(): pl.pallas_call(functools.partial(near_kernel, boxes * devices), out_shape...  7.16 us
    pallas_call x1, Pallas kernels, on_device(): pl.pallas_call(functools.partial(radiate_kernel, group), out_shape=jax.Sh...  5.86 us
    ppermute x3, starting transfers between devices, exchanged(): return lax.ppermute(value, axes, pairs)  5.18 us
    pallas_call x1, Pallas kernels, on_device(): pl.pallas_call(last_kernel, out_shape=jax.ShapeDtypeStruct((2 * boxes, pa...  5.17 us
    all_to_all x1, starting transfers between devices, on_device(): lax.all_to_all(outgoing, ('box', 'samp'), split_axis=0, concat_axis=0, ti...  4.84 us
    pallas_call x1, Pallas kernels, on_device(): pl.pallas_call(leaf_kernel, out_shape=jax.ShapeDtypeStruct((2 * boxes, wi...  3.76 us
    all_to_all x1, waiting for transfers between devices, on_device(): lax.all_to_all(outgoing, ('box', 'samp'), split_axis=0, concat_axis=0, ti...  1.58 us
  transfers between devices with their start and end apart: 4, of which 1 were waited for; matrix products, arithmetic and copies ran while one was open for 0% of the time, Pallas kernels for 58%

profile of v10, /device:TPU:0, one launch (start us, length us, event | category | flops | bytes accessed | tf_op | source)
XLA Modules:
  0.0 41.8 jit_solution(12527644926737606056)
XLA Ops:
  0.0 0.6 %collective-permute-start.1 = (bf16[32,128]{1,0:T(8,128)(2,1)}, bf16[32,128]{1,0:T(8,128)(2,1)S(1)}, u32[]{:S(2)}, u32[]{:S(2)}) collective-permute-start(bf16[32,128]{1,0:T(8,128)(2,1)} %bitcast.22), channel_id=1, source_target_pairs={{1,2},{2,1},{3,4},{4,3},{5,6},{6,5},{7,8},{8,7},{9,10},{10,9},{11,... | collective-permute-start | bytes 24584 | tf_op jit(solution)/shard_map/ppermute | solution.py:37
  0.7 4.5 %collective-permute-start = (bf16[32,128]{1,0:T(8,128)(2,1)}, bf16[32,128]{1,0:T(8,128)(2,1)S(1)}, u32[]{:S(2)}, u32[]{:S(2)}) collective-permute-start(bf16[32,128]{1,0:T(8,128)(2,1)} %bitcast.23), channel_id=1, source_target_pairs={{0,1},{1,0},{2,3},{3,2},{4,5},{5,4},{6,7},{7,6},{8,9},{9,8},{10,11... | collective-permute-start | bytes 24584 | tf_op jit(solution)/shard_map/ppermute | solution.py:37
  5.1 5.9 %shard_map.145 = bf16[32,64,128]{2,1,0:T(8,128)(2,1)} custom-call(bf16[32,128]{1,0:T(8,128)(2,1)} %bitcast.24, bf16[16,128,1024]{2,1,0:T(8,128)(2,1)} %radiate_ref.1, s32[4,32]{1,0:T(4,128)} %bitcast.26, bf16[512,2048]{1,0:T(8,128)(2,1)} %interp_hbm.3, f32[256,128]{1,0:T(8,128)} %bitcast.20), custom_call_target="tpu_custom_call" | custom-call | flops 1000000000 | bytes 8388608 | tf_op jit(solution)/shard_map/pallas_call | solution.py:557
  11.0 0.0 collective-permute-done.1.odd_ref
  11.0 0.0 collective-permute-done.even_ref
  11.0 4.8 %all-to-all-start = ((bf16[32,64,128]{2,1,0:T(8,128)(2,1)}), bf16[32,64,128]{2,1,0:T(8,128)(2,1)S(1)}, u32[]{:S(2)}, u32[]{:S(2)}) async-start(bf16[32,64,128]{2,1,0:T(8,128)(2,1)} %shard_map.145), calls=%async_computation | async-start | bytes 1048576 | tf_op jit(solution)/shard_map/all_to_all | solution.py:581
  15.9 7.2 %shard_map.146.near_ref = f32[32,128]{1,0:T(8,128)S(1)} custom-call(bf16[32,128]{1,0:T(8,128)(2,1)S(1)} %collective-permute-done.even_ref, bf16[32,128]{1,0:T(8,128)(2,1)} %bitcast.25, bf16[32,128]{1,0:T(8,128)(2,1)S(1)} %collective-permute-done.1.odd_ref, s32[16,27]{1,0:T(8,128)} %near_src_hbm.1, s32[16,27]{1,0:T(8,128)} %near_tile_hbm.1, ...), custom_call_target="tpu_custom_call" | custom-call | flops 10000000000 | bytes 16777216 | tf_op jit(solution)/shard_map/pallas_call | solution.py:587
  23.0 7.6 %shard_map.147 = (bf16[16,128,1024]{2,1,0:T(8,128)(2,1)}, bf16[4,64,2048]{2,1,0:T(8,128)(2,1)S(1)}) custom-call(s32[16,189]{1,0:T(8,128)} %slot_hbm.1, s32[16,189]{1,0:T(8,128)} %type_hbm, s32[16,189]{1,0:T(8,128)} %par_far_hbm.1, s32[16,189]{1,0:T(8,128)} %par_type_hbm.1, bf16[2528,128]{1,0:T(8,128)(2,1)} %bitcast.28, bf16[10112,128]{1,0:T(8,128)(2,1)} %bitcast.27), custom_call_target="tpu_custom_call" | custom-call | flops 1000000000 | bytes 16777216 | tf_op jit(solution)/shard_map/pallas_call | solution.py:609
  30.6 1.6 %all-to-all-done.arrived_ref = bf16[32,64,128]{2,1,0:T(8,128)(2,1)S(1)} async-done(((bf16[32,64,128]{2,1,0:T(8,128)(2,1)}), bf16[32,64,128]{2,1,0:T(8,128)(2,1)S(1)}, u32[]{:S(2)}, u32[]{:S(2)}) %all-to-all-start) | async-done | bytes 524320 | tf_op jit(solution)/shard_map/all_to_all | solution.py:581
  32.2 0.5 %shard_map.148 = (f32[32,128]{1,0:T(8,128)S(1)}, f32[32,128]{1,0:T(8,128)S(1)}) custom-call(bf16[32,64,128]{2,1,0:T(8,128)(2,1)S(1)} %all-to-all-done.arrived_ref, bf16[4,64,2048]{2,1,0:T(8,128)(2,1)S(1)} %get-tuple-element.20.d_ref), custom_call_target="tpu_custom_call" | custom-call | flops 100000000 | bytes 1048576 | tf_op jit(solution)/shard_map/pallas_call | solution.py:651
  32.7 0.1 collective-permute-start.2
  32.8 3.8 %shard_map.149.incoming_ref = f32[32,4,128]{2,1,0:T(4,128)S(1)} custom-call(bf16[16,128,1024]{2,1,0:T(8,128)(2,1)} %get-tuple-element.25.d_lo_hbm, bf16[32,64,128]{2,1,0:T(8,128)(2,1)S(1)} %all-to-all-done.arrived_ref), custom_call_target="tpu_custom_call" | custom-call | flops 1000000000 | bytes 5242880 | tf_op jit(solution)/shard_map/pallas_call | solution.py:662
  36.6 0.0 collective-permute-done.2.other_ref
  36.6 5.2 %shard_map.150 = f32[32,128]{1,0:T(8,128)} custom-call(f32[32,128]{1,0:T(8,128)S(1)} %get-tuple-element.21.mine_ref, f32[32,128]{1,0:T(8,128)S(1)} %collective-permute-done.2.other_ref, f32[32,4,128]{2,1,0:T(4,128)S(1)} %shard_map.149.incoming_ref, f32[256,128]{1,0:T(8,128)} %bitcast.21, bf16[512,2048]{1,0:T(8,128)(2,1)} %interp_hbm.3, ...), custom_call_target="tpu_custom_call" | custom-call | flops 1000000000 | bytes 8388608 | tf_op jit(solution)/shard_map/pallas_call | solution.py:678
Async XLA Ops:
  0.0 11.0 %collective-permute-start.1 = (bf16[32,128]{1,0:T(8,128)(2,1)}, bf16[32,128]{1,0:T(8,128)(2,1)S(1)}, u32[]{:S(2)}, u32[]{:S(2)}) collective-permute-start(bf16[32,128]{1,0:T(8,128)(2,1)} %bitcast.22), channel_id=1, source_target_pairs={{1,2},{2,1},{3,4},{4,3},{5,6},{6,5},{7,8},{8,7},{9,10},{10,9},{11,... | collective-permute-start | bytes 24584 | tf_op jit(solution)/shard_map/ppermute | solution.py:37
  0.7 10.3 %collective-permute-start = (bf16[32,128]{1,0:T(8,128)(2,1)}, bf16[32,128]{1,0:T(8,128)(2,1)S(1)}, u32[]{:S(2)}, u32[]{:S(2)}) collective-permute-start(bf16[32,128]{1,0:T(8,128)(2,1)} %bitcast.23), channel_id=1, source_target_pairs={{0,1},{1,0},{2,3},{3,2},{4,5},{5,4},{6,7},{7,6},{8,9},{9,8},{10,11... | collective-permute-start | bytes 24584 | tf_op jit(solution)/shard_map/ppermute | solution.py:37
  11.0 21.2 %all-to-all-start = ((bf16[32,64,128]{2,1,0:T(8,128)(2,1)}), bf16[32,64,128]{2,1,0:T(8,128)(2,1)S(1)}, u32[]{:S(2)}, u32[]{:S(2)}) async-start(bf16[32,64,128]{2,1,0:T(8,128)(2,1)} %shard_map.145), calls=%async_computation | async-start | bytes 1048576 | tf_op jit(solution)/shard_map/all_to_all | solution.py:581
  32.7 3.9 %collective-permute-start.2 = (f32[32,128]{1,0:T(8,128)S(1)}, f32[32,128]{1,0:T(8,128)S(1)}, u32[]{:S(2)}, u32[]{:S(2)}) collective-permute-start(f32[32,128]{1,0:T(8,128)S(1)} %get-tuple-element.24), channel_id=1, source_target_pairs={{0,1},{1,0},{2,3},{3,2},{4,5},{5,4},{6,7},{7,6},{8,9},{9,8},{10,11... | collective-permute-start | bytes 49160 | tf_op jit(solution)/shard_map/ppermute | solution.py:37

commit v11 on v9

--- a/solution.py
+++ b/solution.py
@@ -43,6 +43,12 @@
         copies.append(pltpu.make_async_copy(source, target, sems.at[first + k]))
         copies[-1].start()
     return copies
+
+
+def pieces(source, target, count):
+    rows = source.shape[0] // count
+    parts = [pl.ds(k * rows, rows) for k in range(count)]
+    return [(source.at[part], target.at[part]) for part in parts]
 
 
 def radiate_kernel(
@@ -71,18 +77,15 @@
     others = fetch(
         [(dens_hbm, dens_ref), (send_hbm, send_ref), (shift_hbm, shift_ref)], extra
     )
-    copies = []
-    for step in range(steps):
-        part = pl.ds(step * per_step, per_step)
-        copies.append(pltpu.make_async_copy(radiate_ref.at[part], rad.at[part], sems.at[step]))
-        copies[-1].start()
-    others += fetch([(interp_hbm, interp_ref)], extra, 3)
+    copies = fetch(pieces(radiate_ref, rad, boxes), sems)
+    others += fetch(pieces(interp_hbm, interp_ref, 4), extra, 3)
     others[0].wait()
     dens = dens_ref[...].astype(F32)
     owner = (iota(dens.shape, 0) // 2) % per_step
     blocks = jnp.concatenate([jnp.where(owner == b, dens, 0.0) for b in range(per_step)], 1)
     for step in range(steps):
-        copies[step].wait()
+        for copy in copies[step * per_step : (step + 1) * per_step]:
+            copy.wait()
         rows = slice(step * 2 * per_step, (step + 1) * 2 * per_step)
         weights = rad[step * per_step : (step + 1) * per_step].reshape(per_step * LANE, 2 * width)
         summed[rows] = dot_nn(blocks[rows].astype(BF16), weights).reshape(
@@ -179,7 +182,7 @@
             (type_hbm, type_ref),
             (par_far_hbm, par_far_ref),
             (par_type_hbm, par_type_ref),
-            (op_hi_hbm, op_hi_ref),
+            *pieces(op_hi_hbm, op_hi_ref, 4),
         ],
         extra,
     )
@@ -243,7 +246,8 @@
         return carry
 
     lax.fori_loop(0, boxes // batch, step_lists, 0)
-    others[5].wait()
+    for copy in others[5:]:
+        copy.wait()
 
     def widen(t, carry):
         source = pl.ds(pl.multiple_of(t * lines + base, 16), 16)
@@ -308,7 +312,8 @@
 ):
     boxes, near = near_src_ref.shape
     tile_count = tiles.shape[0]
-    steps = sems.shape[0]
+    split = 4
+    steps = sems.shape[0] // split
     per_step = tile_count // steps
     samp = lax.axis_index("samp")
     position = lax.axis_index("box") * lax.axis_size("samp") + samp
@@ -324,12 +329,12 @@
         extra,
     )
 
-    def tile_copy(step):
-        part = pl.ds(step * per_step, per_step)
-        return pltpu.make_async_copy(tiles_hbm.at[part], tiles.at[part], sems.at[step])
-
-    for step in range(steps):
-        tile_copy(step).start()
+    def tile_copy(piece):
+        part = pl.ds(piece * (per_step // split), per_step // split)
+        return pltpu.make_async_copy(tiles_hbm.at[part], tiles.at[part], sems.at[piece])
+
+    for piece in range(steps * split):
+        tile_copy(piece).start()
     acc[...] = jnp.zeros(acc.shape, F32)
     left[...] = jnp.zeros(left.shape, F32)
     right[...] = jnp.zeros(right.shape, F32)
@@ -376,7 +381,8 @@
 
 
     def step_tiles(step, carry):
-        tile_copy(step).wait()
+        for piece in range(split):
+            tile_copy(step * split + piece).wait()
         for pair in range(per_step // 2):
             multiply_pair(step * per_step + 2 * pair)
         return carry
@@ -442,12 +448,8 @@
     boxes = receive.shape[0]
     per_step = 4
     steps = boxes // per_step
-    others = fetch([(shift_hbm, shift_ref), (interp_hbm, interp_ref)], extra)
-    copies = []
-    for step in range(steps):
-        part = pl.ds(step * per_step, per_step)
-        copies.append(pltpu.make_async_copy(receive_ref.at[part], receive.at[part], sems.at[step]))
-        copies[-1].start()
+    others = fetch([(shift_hbm, shift_ref), *pieces(interp_hbm, interp_ref, 4)], extra)
+    copies = fetch(pieces(receive_ref, receive, boxes), sems)
     member = lax.rem(lax.axis_index("samp"), 2)
     parent_ref[member] = mine_ref[...]
     parent_ref[1 - member] = other_ref[...]
@@ -468,7 +470,8 @@
             im_rows.append(s_re * t_im - s_im * t_re)
         cols = slice(r * LANE, (r + 1) * LANE)
         down[:, cols] = jnp.concatenate(re_rows + im_rows, 0).astype(BF16)
-    others[1].wait()
+    for copy in others[1:]:
+        copy.wait()
     total = jnp.concatenate([incoming_ref[:, r, :] for r in range(chunks)], 1)
     total = total + dot_nt(down[...], interp_ref[...])
     total = total.astype(BF16).astype(F32)
@@ -483,7 +486,8 @@
     for step in range(steps):
         rows = slice(step * 2 * per_step, (step + 1) * 2 * per_step)
         lhs = jnp.concatenate([blend[rows, r, :] for r in range(2 * chunks)], 1).astype(BF16)
-        copies[step].wait()
+        for copy in copies[step * per_step : (step + 1) * per_step]:
+            copy.wait()
         weights = receive[step * per_step : (step + 1) * per_step]
         product = dot_nt(lhs, weights.reshape(per_step * LANE, 2 * chunks * LANE))
         total = near_ref[rows]
@@ -554,8 +558,8 @@
             pltpu.VMEM((2 * boxes, 2 * width_lo // LANE, LANE), F32),
             pltpu.VMEM((boxes * 8 + 8, LANE), F32),
             pltpu.VMEM((parents * 2 * width_hi // LANE, LANE), F32),
-            pltpu.SemaphoreType.DMA((boxes // 4,)),
-            pltpu.SemaphoreType.DMA((4,)),
+            pltpu.SemaphoreType.DMA((boxes,)),
+            pltpu.SemaphoreType.DMA((7,)),
         ],
         compiler_params=pltpu.CompilerParams(vmem_limit_bytes=12 * MIB),
         cost_estimate=pl.CostEstimate(flops=10**9, bytes_accessed=8 * MIB, transcendentals=0),
@@ -585,7 +589,7 @@
             pltpu.VMEM((3 * boxes * 8, LANE), F32),
             pltpu.VMEM((boxes, 8, LANE), F32),
             pltpu.SMEM((tile_count + 8,), jnp.int32),
-            pltpu.SemaphoreType.DMA((steps,)),
+            pltpu.SemaphoreType.DMA((steps * 4,)),
             pltpu.SemaphoreType.DMA((5,)),
         ],
         compiler_params=pltpu.CompilerParams(vmem_limit_bytes=20 * MIB),
@@ -615,7 +619,7 @@
             pltpu.VMEM((parents * group * par_total, type_pad), BF16),
             pltpu.VMEM((boxes, slot_total, 2 * width_lo), BF16),
             pltpu.SemaphoreType.DMA((boxes // 4,)),
-            pltpu.SemaphoreType.DMA((6,)),
+            pltpu.SemaphoreType.DMA((9,)),
         ],
         compiler_params=pltpu.CompilerParams(
             vmem_limit_bytes=(20 if slot_total <= 128 else 46) * MIB
@@ -654,7 +658,7 @@
             pltpu.VMEM((boxes, slot_total, 2 * width_lo), BF16),
             pltpu.VMEM((devices * lo_lines, LANE), F32),
             pltpu.VMEM((slot_total, 2 * width_lo), F32),
-            pltpu.SemaphoreType.DMA((boxes // 2,)),
+            pltpu.SemaphoreType.DMA((boxes,)),
         ],
         compiler_params=pltpu.CompilerParams(
             vmem_limit_bytes=(10 if slot_total <= 128 else 32) * MIB
@@ -673,8 +677,8 @@
             pltpu.VMEM((group, hi_lines, LANE), F32),
             pltpu.VMEM((2 * boxes, width_hi), BF16),
             pltpu.VMEM((2 * boxes, 2 * width_lo // LANE, LANE), F32),
-            pltpu.SemaphoreType.DMA((boxes // 4,)),
-            pltpu.SemaphoreType.DMA((2,)),
+            pltpu.SemaphoreType.DMA((boxes,)),
+            pltpu.SemaphoreType.DMA((5,)),
         ],
         compiler_params=pltpu.CompilerParams(vmem_limit_bytes=12 * MIB),
         cost_estimate=pl.CostEstimate(flops=10**9, bytes_accessed=8 * MIB, transcendentals=0),

time: 40.5 us -> 41.1 us (1.015)
  Pallas kernels: 28.3 us -> 29.3 us
  transfers between devices with their start and end apart: 4 -> 4, of which waited for: 1 -> 1; matrix products, arithmetic and copies ran while one was open for 0% -> 0% of each run, Pallas kernels for 55% -> 56%
where the time goes in v11:
time: 41.1 us; the launch traced here: 40.7 us
  Pallas kernels  29.3 us (71%)
  starting transfers between devices  10 us (24%)
  waiting for transfers between devices  1.31 us (3%)
    pallas_call x1, Pallas kernels, on_device(): pl.pallas_call(functools.partial(index_kernel, types, group), out_shape=(...  7.63 us
    pallas_call x1, Pallas kernels, on_device(): pl.pallas_call(functools.partial(near_kernel, boxes * devices), out_shape...  7.41 us
    pallas_call x1, Pallas kernels, on_device(): pl.pallas_call(last_kernel, out_shape=jax.ShapeDtypeStruct((2 * boxes, pa...  6 us
    ppermute x3, starting transfers between devices, exchanged(): return lax.ppermute(value, axes, pairs)  5.18 us
    all_to_all x1, starting transfers between devices, on_device(): lax.all_to_all(outgoing, ('box', 'samp'), split_axis=0, concat_axis=0, ti...  4.84 us
    pallas_call x1, Pallas kernels, on_device(): pl.pallas_call(functools.partial(radiate_kernel, group), out_shape=jax.Sh...  4.77 us
    pallas_call x1, Pallas kernels, on_device(): pl.pallas_call(leaf_kernel, out_shape=jax.ShapeDtypeStruct((2 * boxes, wi...  2.97 us
    all_to_all x1, waiting for transfers between devices, on_device(): lax.all_to_all(outgoing, ('box', 'samp'), split_axis=0, concat_axis=0, ti...  1.3 us
  transfers between devices with their start and end apart: 4, of which 1 were waited for; matrix products, arithmetic and copies ran while one was open for 0% of the time, Pallas kernels for 56%

profile of v11, /device:TPU:0, one launch (start us, length us, event | category | flops | bytes accessed | tf_op | source)
XLA Modules:
  0.0 40.7 jit_solution(8750385032145866478)
XLA Ops:
  0.0 0.6 %collective-permute-start.1 = (bf16[32,128]{1,0:T(8,128)(2,1)}, bf16[32,128]{1,0:T(8,128)(2,1)S(1)}, u32[]{:S(2)}, u32[]{:S(2)}) collective-permute-start(bf16[32,128]{1,0:T(8,128)(2,1)} %bitcast.22), channel_id=1, source_target_pairs={{1,2},{2,1},{3,4},{4,3},{5,6},{6,5},{7,8},{8,7},{9,10},{10,9},{11,... | collective-permute-start | bytes 24584 | tf_op jit(solution)/shard_map/ppermute | solution.py:37
  0.7 4.5 %collective-permute-start = (bf16[32,128]{1,0:T(8,128)(2,1)}, bf16[32,128]{1,0:T(8,128)(2,1)S(1)}, u32[]{:S(2)}, u32[]{:S(2)}) collective-permute-start(bf16[32,128]{1,0:T(8,128)(2,1)} %bitcast.23), channel_id=1, source_target_pairs={{0,1},{1,0},{2,3},{3,2},{4,5},{5,4},{6,7},{7,6},{8,9},{9,8},{10,11... | collective-permute-start | bytes 24584 | tf_op jit(solution)/shard_map/ppermute | solution.py:37
  5.1 4.8 %shard_map.145 = bf16[32,64,128]{2,1,0:T(8,128)(2,1)} custom-call(bf16[32,128]{1,0:T(8,128)(2,1)} %bitcast.24, bf16[16,128,1024]{2,1,0:T(8,128)(2,1)} %radiate_ref.1, s32[4,32]{1,0:T(4,128)} %bitcast.26, bf16[512,2048]{1,0:T(8,128)(2,1)} %interp_hbm.3, f32[256,128]{1,0:T(8,128)} %bitcast.20), custom_call_target="tpu_custom_call" | custom-call | flops 1000000000 | bytes 8388608 | tf_op jit(solution)/shard_map/pallas_call | solution.py:547
  9.9 0.0 collective-permute-done.1.odd_ref
  9.9 0.0 collective-permute-done.even_ref
  9.9 4.8 %all-to-all-start = ((bf16[32,64,128]{2,1,0:T(8,128)(2,1)}), bf16[32,64,128]{2,1,0:T(8,128)(2,1)S(1)}, u32[]{:S(2)}, u32[]{:S(2)}) async-start(bf16[32,64,128]{2,1,0:T(8,128)(2,1)} %shard_map.145), calls=%async_computation | async-start | bytes 1048576 | tf_op jit(solution)/shard_map/all_to_all | solution.py:571
  14.8 7.4 %shard_map.146.near_ref = f32[32,128]{1,0:T(8,128)S(1)} custom-call(bf16[32,128]{1,0:T(8,128)(2,1)S(1)} %collective-permute-done.even_ref, bf16[32,128]{1,0:T(8,128)(2,1)} %bitcast.25, bf16[32,128]{1,0:T(8,128)(2,1)S(1)} %collective-permute-done.1.odd_ref, s32[16,27]{1,0:T(8,128)} %near_src_hbm.1, s32[16,27]{1,0:T(8,128)} %near_tile_hbm.1, ...), custom_call_target="tpu_custom_call" | custom-call | flops 10000000000 | bytes 16777216 | tf_op jit(solution)/shard_map/pallas_call | solution.py:577
  22.2 7.6 %shard_map.147 = (bf16[16,128,1024]{2,1,0:T(8,128)(2,1)}, bf16[4,64,2048]{2,1,0:T(8,128)(2,1)S(1)}) custom-call(s32[16,189]{1,0:T(8,128)} %slot_hbm.1, s32[16,189]{1,0:T(8,128)} %type_hbm, s32[16,189]{1,0:T(8,128)} %par_far_hbm.1, s32[16,189]{1,0:T(8,128)} %par_type_hbm.1, bf16[2528,128]{1,0:T(8,128)(2,1)} %bitcast.28, bf16[10112,128]{1,0:T(8,128)(2,1)} %bitcast.27), custom_call_target="tpu_custom_call" | custom-call | flops 1000000000 | bytes 16777216 | tf_op jit(solution)/shard_map/pallas_call | solution.py:599
  29.8 1.3 %all-to-all-done.arrived_ref = bf16[32,64,128]{2,1,0:T(8,128)(2,1)S(1)} async-done(((bf16[32,64,128]{2,1,0:T(8,128)(2,1)}), bf16[32,64,128]{2,1,0:T(8,128)(2,1)S(1)}, u32[]{:S(2)}, u32[]{:S(2)}) %all-to-all-start) | async-done | bytes 524320 | tf_op jit(solution)/shard_map/all_to_all | solution.py:571
  31.1 0.5 %shard_map.148 = (f32[32,128]{1,0:T(8,128)S(1)}, f32[32,128]{1,0:T(8,128)S(1)}) custom-call(bf16[32,64,128]{2,1,0:T(8,128)(2,1)S(1)} %all-to-all-done.arrived_ref, bf16[4,64,2048]{2,1,0:T(8,128)(2,1)S(1)} %get-tuple-element.20.d_ref), custom_call_target="tpu_custom_call" | custom-call | flops 100000000 | bytes 1048576 | tf_op jit(solution)/shard_map/pallas_call | solution.py:641
  31.6 0.1 collective-permute-start.2
  31.7 3.0 %shard_map.149.incoming_ref = f32[32,4,128]{2,1,0:T(4,128)S(1)} custom-call(bf16[16,128,1024]{2,1,0:T(8,128)(2,1)} %get-tuple-element.25.d_lo_hbm, bf16[32,64,128]{2,1,0:T(8,128)(2,1)S(1)} %all-to-all-done.arrived_ref), custom_call_target="tpu_custom_call" | custom-call | flops 1000000000 | bytes 5242880 | tf_op jit(solution)/shard_map/pallas_call | solution.py:652
  34.7 0.0 collective-permute-done.2.other_ref
  34.7 6.0 %shard_map.150 = f32[32,128]{1,0:T(8,128)} custom-call(f32[32,128]{1,0:T(8,128)S(1)} %get-tuple-element.21.mine_ref, f32[32,128]{1,0:T(8,128)S(1)} %collective-permute-done.2.other_ref, f32[32,4,128]{2,1,0:T(4,128)S(1)} %shard_map.149.incoming_ref, f32[256,128]{1,0:T(8,128)} %bitcast.21, bf16[512,2048]{1,0:T(8,128)(2,1)} %interp_hbm.3, ...), custom_call_target="tpu_custom_call" | custom-call | flops 1000000000 | bytes 8388608 | tf_op jit(solution)/shard_map/pallas_call | solution.py:668
Async XLA Ops:
  0.0 9.9 %collective-permute-start.1 = (bf16[32,128]{1,0:T(8,128)(2,1)}, bf16[32,128]{1,0:T(8,128)(2,1)S(1)}, u32[]{:S(2)}, u32[]{:S(2)}) collective-permute-start(bf16[32,128]{1,0:T(8,128)(2,1)} %bitcast.22), channel_id=1, source_target_pairs={{1,2},{2,1},{3,4},{4,3},{5,6},{6,5},{7,8},{8,7},{9,10},{10,9},{11,... | collective-permute-start | bytes 24584 | tf_op jit(solution)/shard_map/ppermute | solution.py:37
  0.7 9.2 %collective-permute-start = (bf16[32,128]{1,0:T(8,128)(2,1)}, bf16[32,128]{1,0:T(8,128)(2,1)S(1)}, u32[]{:S(2)}, u32[]{:S(2)}) collective-permute-start(bf16[32,128]{1,0:T(8,128)(2,1)} %bitcast.23), channel_id=1, source_target_pairs={{0,1},{1,0},{2,3},{3,2},{4,5},{5,4},{6,7},{7,6},{8,9},{9,8},{10,11... | collective-permute-start | bytes 24584 | tf_op jit(solution)/shard_map/ppermute | solution.py:37
  9.9 21.2 %all-to-all-start = ((bf16[32,64,128]{2,1,0:T(8,128)(2,1)}), bf16[32,64,128]{2,1,0:T(8,128)(2,1)S(1)}, u32[]{:S(2)}, u32[]{:S(2)}) async-start(bf16[32,64,128]{2,1,0:T(8,128)(2,1)} %shard_map.145), calls=%async_computation | async-start | bytes 1048576 | tf_op jit(solution)/shard_map/all_to_all | solution.py:571
  31.6 3.1 %collective-permute-start.2 = (f32[32,128]{1,0:T(8,128)S(1)}, f32[32,128]{1,0:T(8,128)S(1)}, u32[]{:S(2)}, u32[]{:S(2)}) collective-permute-start(f32[32,128]{1,0:T(8,128)S(1)} %get-tuple-element.24), channel_id=1, source_target_pairs={{0,1},{1,0},{2,3},{3,2},{4,5},{5,4},{6,7},{7,6},{8,9},{9,8},{10,11... | collective-permute-start | bytes 49160 | tf_op jit(solution)/shard_map/ppermute | solution.py:37

commit v12 on v9

--- a/solution.py
+++ b/solution.py
@@ -682,8 +682,8 @@
         mine,
         other,
         incoming,
-        in_hbm(shift_rows),
-        in_hbm(interp_matrix),
+        shift_rows,
+        interp_matrix,
         in_hbm(receive),
         near,
     )

time: 40.5 us -> 39.9 us (0.985)
  local copies, waits for them, and re-layouts: 0 us -> 2.19 us
  Pallas kernels: 28.3 us -> 26.6 us
  waiting for transfers between devices: 1.59 us -> 0.46 us
    unnamed x0 -> x8, local copies, waits for them, and re-layouts: none -> 2.19 us
    pallas_call x1, Pallas kernels: 5.7 us -> 3.81 us  [on_device(): pl.pallas_call(last_kernel, out_shape=jax.ShapeDtypeStruct((2 * boxes, pa...]
    all_to_all x1, waiting for transfers between devices: 1.58 us -> 0.45 us  [on_device(): lax.all_to_all(outgoing, ('box', 'samp'), split_axis=0, concat_axis=0, ti...]
  transfers between devices with their start and end apart: 4 -> 4, of which waited for: 1 -> 1; matrix products, arithmetic and copies ran while one was open for 0% -> 0% of each run, Pallas kernels for 55% -> 57%
where the time goes in v12:
time: 39.9 us; the launch traced here: 39.4 us
  Pallas kernels  26.6 us (67%)
  starting transfers between devices  10 us (25%)
  local copies, waits for them, and re-layouts  2.19 us (5%)
  waiting for transfers between devices  0.46 us (1%)
    pallas_call x1, Pallas kernels, on_device(): pl.pallas_call(functools.partial(index_kernel, types, group), out_shape=(...  7.74 us
    pallas_call x1, Pallas kernels, on_device(): pl.pallas_call(functools.partial(near_kernel, boxes * devices), out_shape...  7.16 us
    ppermute x3, starting transfers between devices, exchanged(): return lax.ppermute(value, axes, pairs)  5.18 us
    all_to_all x1, starting transfers between devices, on_device(): lax.all_to_all(outgoing, ('box', 'samp'), split_axis=0, concat_axis=0, ti...  4.84 us
    pallas_call x1, Pallas kernels, on_device(): pl.pallas_call(functools.partial(radiate_kernel, group), out_shape=jax.Sh...  4.61 us
    pallas_call x1, Pallas kernels, on_device(): pl.pallas_call(last_kernel, out_shape=jax.ShapeDtypeStruct((2 * boxes, pa...  3.81 us
    pallas_call x1, Pallas kernels, on_device(): pl.pallas_call(leaf_kernel, out_shape=jax.ShapeDtypeStruct((2 * boxes, wi...  2.78 us
    unnamed x8, local copies, waits for them, and re-layouts  2.19 us
  transfers between devices with their start and end apart: 4, of which 1 were waited for; matrix products, arithmetic and copies ran while one was open for 0% of the time, Pallas kernels for 57%

profile of v12, /device:TPU:0, one launch (start us, length us, event | category | flops | bytes accessed | tf_op | source)
XLA Modules:
  0.0 39.4 jit_solution(17918483624711333285)
XLA Ops:
  0.0 0.6 %collective-permute-start.1 = (bf16[32,128]{1,0:T(8,128)(2,1)}, bf16[32,128]{1,0:T(8,128)(2,1)S(1)}, u32[]{:S(2)}, u32[]{:S(2)}) collective-permute-start(bf16[32,128]{1,0:T(8,128)(2,1)} %bitcast.22), channel_id=1, source_target_pairs={{1,2},{2,1},{3,4},{4,3},{5,6},{6,5},{7,8},{8,7},{9,10},{10,9},{11,... | collective-permute-start | bytes 24584 | tf_op jit(solution)/shard_map/ppermute | solution.py:37
  0.7 4.5 %collective-permute-start = (bf16[32,128]{1,0:T(8,128)(2,1)}, bf16[32,128]{1,0:T(8,128)(2,1)S(1)}, u32[]{:S(2)}, u32[]{:S(2)}) collective-permute-start(bf16[32,128]{1,0:T(8,128)(2,1)} %bitcast.23), channel_id=1, source_target_pairs={{0,1},{1,0},{2,3},{3,2},{4,5},{5,4},{6,7},{7,6},{8,9},{9,8},{10,11... | collective-permute-start | bytes 24584 | tf_op jit(solution)/shard_map/ppermute | solution.py:37
  5.1 4.6 %shard_map.145 = bf16[32,64,128]{2,1,0:T(8,128)(2,1)} custom-call(bf16[32,128]{1,0:T(8,128)(2,1)} %bitcast.24, bf16[16,128,1024]{2,1,0:T(8,128)(2,1)} %radiate_ref.1, s32[4,32]{1,0:T(4,128)} %bitcast.26, bf16[512,2048]{1,0:T(8,128)(2,1)} %interp_hbm.3, f32[256,128]{1,0:T(8,128)} %bitcast.20), custom_call_target="tpu_custom_call" | custom-call | flops 1000000000 | bytes 8388608 | tf_op jit(solution)/shard_map/pallas_call | solution.py:543
  9.7 0.0 collective-permute-done.1.odd_ref
  9.7 0.0 collective-permute-done.even_ref
  9.7 4.8 %all-to-all-start = ((bf16[32,64,128]{2,1,0:T(8,128)(2,1)}), bf16[32,64,128]{2,1,0:T(8,128)(2,1)S(1)}, u32[]{:S(2)}, u32[]{:S(2)}) async-start(bf16[32,64,128]{2,1,0:T(8,128)(2,1)} %shard_map.145), calls=%async_computation | async-start | bytes 1048576 | tf_op jit(solution)/shard_map/all_to_all | solution.py:567
  14.6 7.2 %shard_map.146.near_ref = f32[32,128]{1,0:T(8,128)S(1)} custom-call(bf16[32,128]{1,0:T(8,128)(2,1)S(1)} %collective-permute-done.even_ref, bf16[32,128]{1,0:T(8,128)(2,1)} %bitcast.25, bf16[32,128]{1,0:T(8,128)(2,1)S(1)} %collective-permute-done.1.odd_ref, s32[16,27]{1,0:T(8,128)} %near_src_hbm.1, s32[16,27]{1,0:T(8,128)} %near_tile_hbm.1, ...), custom_call_target="tpu_custom_call" | custom-call | flops 10000000000 | bytes 16777216 | tf_op jit(solution)/shard_map/pallas_call | solution.py:573
  21.8 0.0 copy-start
  21.8 0.0 copy-start.3
  21.8 7.7 %shard_map.147 = (bf16[16,128,1024]{2,1,0:T(8,128)(2,1)}, bf16[4,64,2048]{2,1,0:T(8,128)(2,1)S(1)}) custom-call(s32[16,189]{1,0:T(8,128)} %slot_hbm.1, s32[16,189]{1,0:T(8,128)} %type_hbm, s32[16,189]{1,0:T(8,128)} %par_far_hbm.1, s32[16,189]{1,0:T(8,128)} %par_type_hbm.1, bf16[2528,128]{1,0:T(8,128)(2,1)} %bitcast.28, bf16[10112,128]{1,0:T(8,128)(2,1)} %bitcast.27), custom_call_target="tpu_custom_call" | custom-call | flops 1000000000 | bytes 16777216 | tf_op jit(solution)/shard_map/pallas_call | solution.py:595
  29.5 0.0 copy-start.1
  29.5 0.9 %copy-done.1 = bf16[4,64,2048]{2,1,0:T(8,128)(2,1)} copy-done((bf16[4,64,2048]{2,1,0:T(8,128)(2,1)}, bf16[4,64,2048]{2,1,0:T(8,128)(2,1)S(1)}, u32[]{:S(2)}) %copy-start.1) | copy-done | bytes 1048600
  30.5 0.5 %all-to-all-done.arrived_ref = bf16[32,64,128]{2,1,0:T(8,128)(2,1)S(1)} async-done(((bf16[32,64,128]{2,1,0:T(8,128)(2,1)}), bf16[32,64,128]{2,1,0:T(8,128)(2,1)S(1)}, u32[]{:S(2)}, u32[]{:S(2)}) %all-to-all-start) | async-done | bytes 524320 | tf_op jit(solution)/shard_map/all_to_all | solution.py:567
  31.0 0.0 copy-start.2
  31.0 1.2 %copy-done.2 = bf16[4,64,2048]{2,1,0:T(8,128)(2,1)S(1)} copy-done((bf16[4,64,2048]{2,1,0:T(8,128)(2,1)S(1)}, bf16[4,64,2048]{2,1,0:T(8,128)(2,1)}, u32[]{:S(2)}) %copy-start.2) | copy-done | bytes 1048600
  32.2 0.5 %shard_map.148 = (f32[32,128]{1,0:T(8,128)S(1)}, f32[32,128]{1,0:T(8,128)S(1)}) custom-call(bf16[32,64,128]{2,1,0:T(8,128)(2,1)S(1)} %all-to-all-done.arrived_ref, bf16[4,64,2048]{2,1,0:T(8,128)(2,1)S(1)} %copy-done.2), custom_call_target="tpu_custom_call" | custom-call | flops 100000000 | bytes 1048576 | tf_op jit(solution)/shard_map/pallas_call | solution.py:637
  32.7 0.1 collective-permute-start.2
  32.8 2.8 %shard_map.149.incoming_ref = f32[32,4,128]{2,1,0:T(4,128)S(1)} custom-call(bf16[16,128,1024]{2,1,0:T(8,128)(2,1)} %get-tuple-element.25.d_lo_hbm, bf16[32,64,128]{2,1,0:T(8,128)(2,1)S(1)} %all-to-all-done.arrived_ref), custom_call_target="tpu_custom_call" | custom-call | flops 1000000000 | bytes 5242880 | tf_op jit(solution)/shard_map/pallas_call | solution.py:648
  35.6 0.0 collective-permute-done.2.other_ref
  35.6 0.0 copy-done
  35.6 0.0 copy-done.3
  35.6 3.8 %shard_map.150 = f32[32,128]{1,0:T(8,128)} custom-call(f32[32,128]{1,0:T(8,128)S(1)} %get-tuple-element.21.mine_ref, f32[32,128]{1,0:T(8,128)S(1)} %collective-permute-done.2.other_ref, f32[32,4,128]{2,1,0:T(4,128)S(1)} %shard_map.149.incoming_ref, f32[256,128]{1,0:T(8,128)S(1)} %bitcast.21, bf16[512,2048]{1,0:T(8,128)(2,1)S(1)} %copy-done, ...), custom_call_target="tpu_custom_call" | custom-call | flops 1000000000 | bytes 8388608 | tf_op jit(solution)/shard_map/pallas_call | solution.py:664
Async XLA Ops:
  0.0 9.7 %collective-permute-start.1 = (bf16[32,128]{1,0:T(8,128)(2,1)}, bf16[32,128]{1,0:T(8,128)(2,1)S(1)}, u32[]{:S(2)}, u32[]{:S(2)}) collective-permute-start(bf16[32,128]{1,0:T(8,128)(2,1)} %bitcast.22), channel_id=1, source_target_pairs={{1,2},{2,1},{3,4},{4,3},{5,6},{6,5},{7,8},{8,7},{9,10},{10,9},{11,... | collective-permute-start | bytes 24584 | tf_op jit(solution)/shard_map/ppermute | solution.py:37
  0.7 9.1 %collective-permute-start = (bf16[32,128]{1,0:T(8,128)(2,1)}, bf16[32,128]{1,0:T(8,128)(2,1)S(1)}, u32[]{:S(2)}, u32[]{:S(2)}) collective-permute-start(bf16[32,128]{1,0:T(8,128)(2,1)} %bitcast.23), channel_id=1, source_target_pairs={{0,1},{1,0},{2,3},{3,2},{4,5},{5,4},{6,7},{7,6},{8,9},{9,8},{10,11... | collective-permute-start | bytes 24584 | tf_op jit(solution)/shard_map/ppermute | solution.py:37
  9.7 21.2 %all-to-all-start = ((bf16[32,64,128]{2,1,0:T(8,128)(2,1)}), bf16[32,64,128]{2,1,0:T(8,128)(2,1)S(1)}, u32[]{:S(2)}, u32[]{:S(2)}) async-start(bf16[32,64,128]{2,1,0:T(8,128)(2,1)} %shard_map.145), calls=%async_computation | async-start | bytes 1048576 | tf_op jit(solution)/shard_map/all_to_all | solution.py:567
  21.8 13.8 %copy-start = (bf16[512,2048]{1,0:T(8,128)(2,1)S(1)}, bf16[512,2048]{1,0:T(8,128)(2,1)}, u32[]{:S(2)}) copy-start(bf16[512,2048]{1,0:T(8,128)(2,1)} %interp_hbm.3) | copy-start | bytes 6291460
  21.8 13.8 %copy-start.3 = (f32[8,2,2048]{2,1,0:T(2,128)S(1)}, f32[8,2,2048]{2,1,0:T(2,128)}, u32[]{:S(2)}) copy-start(f32[8,2,2048]{2,1,0:T(2,128)} %param.26) | copy-start | bytes 393220
  29.5 1.0 %copy-start.1 = (bf16[4,64,2048]{2,1,0:T(8,128)(2,1)}, bf16[4,64,2048]{2,1,0:T(8,128)(2,1)S(1)}, u32[]{:S(2)}) copy-start(bf16[4,64,2048]{2,1,0:T(8,128)(2,1)S(1)} %get-tuple-element.20.d_ref) | copy-start | bytes 3145732
  31.0 1.2 %copy-start.2 = (bf16[4,64,2048]{2,1,0:T(8,128)(2,1)S(1)}, bf16[4,64,2048]{2,1,0:T(8,128)(2,1)}, u32[]{:S(2)}) copy-start(bf16[4,64,2048]{2,1,0:T(8,128)(2,1)} %copy-done.1) | copy-start | bytes 3145732
  32.7 2.9 %collective-permute-start.2 = (f32[32,128]{1,0:T(8,128)S(1)}, f32[32,128]{1,0:T(8,128)S(1)}, u32[]{:S(2)}, u32[]{:S(2)}) collective-permute-start(f32[32,128]{1,0:T(8,128)S(1)} %get-tuple-element.24), channel_id=1, source_target_pairs={{0,1},{1,0},{2,3},{3,2},{4,5},{5,4},{6,7},{7,6},{8,9},{9,8},{10,11... | collective-permute-start | bytes 49160 | tf_op jit(solution)/shard_map/ppermute | solution.py:37

commit v13 on v12

--- a/solution.py
+++ b/solution.py
@@ -643,7 +643,9 @@
         compiler_params=pltpu.CompilerParams(vmem_limit_bytes=8 * MIB),
         cost_estimate=pl.CostEstimate(flops=10**8, bytes_accessed=MIB, transcendentals=0),
     )(arrived, in_vmem(d_hi))
-    theirs, d_lo = lax.optimization_barrier((theirs, d_lo))
+    theirs, d_lo, late_interp, late_shift = lax.optimization_barrier(
+        (theirs, d_lo, interp_matrix, shift_rows)
+    )
     other = exchanged(theirs, both, 0)
     incoming = pl.pallas_call(
         leaf_kernel,
@@ -682,8 +684,8 @@
         mine,
         other,
         incoming,
-        shift_rows,
-        interp_matrix,
+        late_shift,
+        late_interp,
         in_hbm(receive),
         near,
     )

time: 39.9 us -> 39.9 us (level)
  no operation moved by 1% of the time
where the time goes in v13:
time: 39.9 us; the launch traced here: 39.4 us
  Pallas kernels  26.6 us (67%)
  starting transfers between devices  10 us (25%)
  local copies, waits for them, and re-layouts  2.19 us (5%)
  waiting for transfers between devices  0.47 us (1%)
    pallas_call x1, Pallas kernels, on_device(): pl.pallas_call(functools.partial(index_kernel, types, group), out_shape=(...  7.74 us
    pallas_call x1, Pallas kernels, on_device(): pl.pallas_call(functools.partial(near_kernel, boxes * devices), out_shape...  7.15 us
    ppermute x3, starting transfers between devices, exchanged(): return lax.ppermute(value, axes, pairs)  5.18 us
    all_to_all x1, starting transfers between devices, on_device(): lax.all_to_all(outgoing, ('box', 'samp'), split_axis=0, concat_axis=0, ti...  4.84 us
    pallas_call x1, Pallas kernels, on_device(): pl.pallas_call(functools.partial(radiate_kernel, group), out_shape=jax.Sh...  4.61 us
    pallas_call x1, Pallas kernels, on_device(): pl.pallas_call(last_kernel, out_shape=jax.ShapeDtypeStruct((2 * boxes, pa...  3.81 us
    pallas_call x1, Pallas kernels, on_device(): pl.pallas_call(leaf_kernel, out_shape=jax.ShapeDtypeStruct((2 * boxes, wi...  2.78 us
    unnamed x8, local copies, waits for them, and re-layouts  2.19 us
  transfers between devices with their start and end apart: 4, of which 1 were waited for; matrix products, arithmetic and copies ran while one was open for 0% of the time, Pallas kernels for 57%

profile of v13, /device:TPU:0, one launch (start us, length us, event | category | flops | bytes accessed | tf_op | source)
XLA Modules:
  0.0 39.4 jit_solution(17918483624711333285)
XLA Ops:
  0.0 0.6 %collective-permute-start.1 = (bf16[32,128]{1,0:T(8,128)(2,1)}, bf16[32,128]{1,0:T(8,128)(2,1)S(1)}, u32[]{:S(2)}, u32[]{:S(2)}) collective-permute-start(bf16[32,128]{1,0:T(8,128)(2,1)} %bitcast.22), channel_id=1, source_target_pairs={{1,2},{2,1},{3,4},{4,3},{5,6},{6,5},{7,8},{8,7},{9,10},{10,9},{11,... | collective-permute-start | bytes 24584 | tf_op jit(solution)/shard_map/ppermute | solution.py:37
  0.7 4.5 %collective-permute-start = (bf16[32,128]{1,0:T(8,128)(2,1)}, bf16[32,128]{1,0:T(8,128)(2,1)S(1)}, u32[]{:S(2)}, u32[]{:S(2)}) collective-permute-start(bf16[32,128]{1,0:T(8,128)(2,1)} %bitcast.23), channel_id=1, source_target_pairs={{0,1},{1,0},{2,3},{3,2},{4,5},{5,4},{6,7},{7,6},{8,9},{9,8},{10,11... | collective-permute-start | bytes 24584 | tf_op jit(solution)/shard_map/ppermute | solution.py:37
  5.1 4.6 %shard_map.145 = bf16[32,64,128]{2,1,0:T(8,128)(2,1)} custom-call(bf16[32,128]{1,0:T(8,128)(2,1)} %bitcast.24, bf16[16,128,1024]{2,1,0:T(8,128)(2,1)} %radiate_ref.1, s32[4,32]{1,0:T(4,128)} %bitcast.26, bf16[512,2048]{1,0:T(8,128)(2,1)} %interp_hbm.2, f32[256,128]{1,0:T(8,128)} %bitcast.20), custom_call_target="tpu_custom_call" | custom-call | flops 1000000000 | bytes 8388608 | tf_op jit(solution)/shard_map/pallas_call | solution.py:543
  9.7 0.0 collective-permute-done.1.odd_ref
  9.7 0.0 collective-permute-done.even_ref
  9.7 4.8 %all-to-all-start = ((bf16[32,64,128]{2,1,0:T(8,128)(2,1)}), bf16[32,64,128]{2,1,0:T(8,128)(2,1)S(1)}, u32[]{:S(2)}, u32[]{:S(2)}) async-start(bf16[32,64,128]{2,1,0:T(8,128)(2,1)} %shard_map.145), calls=%async_computation | async-start | bytes 1048576 | tf_op jit(solution)/shard_map/all_to_all | solution.py:567
  14.6 7.1 %shard_map.146.near_ref = f32[32,128]{1,0:T(8,128)S(1)} custom-call(bf16[32,128]{1,0:T(8,128)(2,1)S(1)} %collective-permute-done.even_ref, bf16[32,128]{1,0:T(8,128)(2,1)} %bitcast.25, bf16[32,128]{1,0:T(8,128)(2,1)S(1)} %collective-permute-done.1.odd_ref, s32[16,27]{1,0:T(8,128)} %near_src_hbm.1, s32[16,27]{1,0:T(8,128)} %near_tile_hbm.1, ...), custom_call_target="tpu_custom_call" | custom-call | flops 10000000000 | bytes 16777216 | tf_op jit(solution)/shard_map/pallas_call | solution.py:573
  21.8 0.0 copy-start
  21.8 0.0 copy-start.3
  21.8 7.7 %shard_map.147 = (bf16[16,128,1024]{2,1,0:T(8,128)(2,1)}, bf16[4,64,2048]{2,1,0:T(8,128)(2,1)S(1)}) custom-call(s32[16,189]{1,0:T(8,128)} %slot_hbm.1, s32[16,189]{1,0:T(8,128)} %type_hbm, s32[16,189]{1,0:T(8,128)} %par_far_hbm.1, s32[16,189]{1,0:T(8,128)} %par_type_hbm.1, bf16[2528,128]{1,0:T(8,128)(2,1)} %bitcast.28, bf16[10112,128]{1,0:T(8,128)(2,1)} %bitcast.27), custom_call_target="tpu_custom_call" | custom-call | flops 1000000000 | bytes 16777216 | tf_op jit(solution)/shard_map/pallas_call | solution.py:595
  29.5 0.0 copy-start.1
  29.5 0.9 %copy-done.1 = bf16[4,64,2048]{2,1,0:T(8,128)(2,1)} copy-done((bf16[4,64,2048]{2,1,0:T(8,128)(2,1)}, bf16[4,64,2048]{2,1,0:T(8,128)(2,1)S(1)}, u32[]{:S(2)}) %copy-start.1) | copy-done | bytes 1048600
  30.5 0.5 %all-to-all-done.arrived_ref = bf16[32,64,128]{2,1,0:T(8,128)(2,1)S(1)} async-done(((bf16[32,64,128]{2,1,0:T(8,128)(2,1)}), bf16[32,64,128]{2,1,0:T(8,128)(2,1)S(1)}, u32[]{:S(2)}, u32[]{:S(2)}) %all-to-all-start) | async-done | bytes 524320 | tf_op jit(solution)/shard_map/all_to_all | solution.py:567
  31.0 0.0 copy-start.2
  31.0 1.2 %copy-done.2 = bf16[4,64,2048]{2,1,0:T(8,128)(2,1)S(1)} copy-done((bf16[4,64,2048]{2,1,0:T(8,128)(2,1)S(1)}, bf16[4,64,2048]{2,1,0:T(8,128)(2,1)}, u32[]{:S(2)}) %copy-start.2) | copy-done | bytes 1048600
  32.2 0.5 %shard_map.148 = (f32[32,128]{1,0:T(8,128)S(1)}, f32[32,128]{1,0:T(8,128)S(1)}) custom-call(bf16[32,64,128]{2,1,0:T(8,128)(2,1)S(1)} %all-to-all-done.arrived_ref, bf16[4,64,2048]{2,1,0:T(8,128)(2,1)S(1)} %copy-done.2), custom_call_target="tpu_custom_call" | custom-call | flops 100000000 | bytes 1048576 | tf_op jit(solution)/shard_map/pallas_call | solution.py:637
  32.7 0.1 collective-permute-start.2
  32.8 2.8 %shard_map.149.incoming_ref = f32[32,4,128]{2,1,0:T(4,128)S(1)} custom-call(bf16[16,128,1024]{2,1,0:T(8,128)(2,1)} %get-tuple-element.27.d_lo_hbm, bf16[32,64,128]{2,1,0:T(8,128)(2,1)S(1)} %all-to-all-done.arrived_ref), custom_call_target="tpu_custom_call" | custom-call | flops 1000000000 | bytes 5242880 | tf_op jit(solution)/shard_map/pallas_call | solution.py:650
  35.6 0.0 collective-permute-done.2.other_ref
  35.6 0.0 copy-done
  35.6 0.0 copy-done.3
  35.6 3.8 %shard_map.150 = f32[32,128]{1,0:T(8,128)} custom-call(f32[32,128]{1,0:T(8,128)S(1)} %get-tuple-element.23.mine_ref, f32[32,128]{1,0:T(8,128)S(1)} %collective-permute-done.2.other_ref, f32[32,4,128]{2,1,0:T(4,128)S(1)} %shard_map.149.incoming_ref, f32[256,128]{1,0:T(8,128)S(1)} %bitcast.21, bf16[512,2048]{1,0:T(8,128)(2,1)S(1)} %copy-done, ...), custom_call_target="tpu_custom_call" | custom-call | flops 1000000000 | bytes 8388608 | tf_op jit(solution)/shard_map/pallas_call | solution.py:666
Async XLA Ops:
  0.0 9.7 %collective-permute-start.1 = (bf16[32,128]{1,0:T(8,128)(2,1)}, bf16[32,128]{1,0:T(8,128)(2,1)S(1)}, u32[]{:S(2)}, u32[]{:S(2)}) collective-permute-start(bf16[32,128]{1,0:T(8,128)(2,1)} %bitcast.22), channel_id=1, source_target_pairs={{1,2},{2,1},{3,4},{4,3},{5,6},{6,5},{7,8},{8,7},{9,10},{10,9},{11,... | collective-permute-start | bytes 24584 | tf_op jit(solution)/shard_map/ppermute | solution.py:37
  0.7 9.1 %collective-permute-start = (bf16[32,128]{1,0:T(8,128)(2,1)}, bf16[32,128]{1,0:T(8,128)(2,1)S(1)}, u32[]{:S(2)}, u32[]{:S(2)}) collective-permute-start(bf16[32,128]{1,0:T(8,128)(2,1)} %bitcast.23), channel_id=1, source_target_pairs={{0,1},{1,0},{2,3},{3,2},{4,5},{5,4},{6,7},{7,6},{8,9},{9,8},{10,11... | collective-permute-start | bytes 24584 | tf_op jit(solution)/shard_map/ppermute | solution.py:37
  9.7 21.2 %all-to-all-start = ((bf16[32,64,128]{2,1,0:T(8,128)(2,1)}), bf16[32,64,128]{2,1,0:T(8,128)(2,1)S(1)}, u32[]{:S(2)}, u32[]{:S(2)}) async-start(bf16[32,64,128]{2,1,0:T(8,128)(2,1)} %shard_map.145), calls=%async_computation | async-start | bytes 1048576 | tf_op jit(solution)/shard_map/all_to_all | solution.py:567
  21.8 13.8 %copy-start = (bf16[512,2048]{1,0:T(8,128)(2,1)S(1)}, bf16[512,2048]{1,0:T(8,128)(2,1)}, u32[]{:S(2)}) copy-start(bf16[512,2048]{1,0:T(8,128)(2,1)} %interp_hbm.2) | copy-start | bytes 6291460
  21.8 13.8 %copy-start.3 = (f32[8,2,2048]{2,1,0:T(2,128)S(1)}, f32[8,2,2048]{2,1,0:T(2,128)}, u32[]{:S(2)}) copy-start(f32[8,2,2048]{2,1,0:T(2,128)} %param.26) | copy-start | bytes 393220
  29.5 1.0 %copy-start.1 = (bf16[4,64,2048]{2,1,0:T(8,128)(2,1)}, bf16[4,64,2048]{2,1,0:T(8,128)(2,1)S(1)}, u32[]{:S(2)}) copy-start(bf16[4,64,2048]{2,1,0:T(8,128)(2,1)S(1)} %get-tuple-element.22.d_ref) | copy-start | bytes 3145732
  31.0 1.2 %copy-start.2 = (bf16[4,64,2048]{2,1,0:T(8,128)(2,1)S(1)}, bf16[4,64,2048]{2,1,0:T(8,128)(2,1)}, u32[]{:S(2)}) copy-start(bf16[4,64,2048]{2,1,0:T(8,128)(2,1)} %copy-done.1) | copy-start | bytes 3145732
  32.7 2.9 %collective-permute-start.2 = (f32[32,128]{1,0:T(8,128)S(1)}, f32[32,128]{1,0:T(8,128)S(1)}, u32[]{:S(2)}, u32[]{:S(2)}) collective-permute-start(f32[32,128]{1,0:T(8,128)S(1)} %get-tuple-element.26), channel_id=1, source_target_pairs={{0,1},{1,0},{2,3},{3,2},{4,5},{5,4},{6,7},{7,6},{8,9},{9,8},{10,11... | collective-permute-start | bytes 49160 | tf_op jit(solution)/shard_map/ppermute | solution.py:37
